TPU v7x, 32 devices: a whole 2x2x4 slice. The times are simulated.
32 devices in a mesh: dp: 16 (over z, y, x), tensor: 2 (over core).
Axes of the slice: x: 2, y: 2, z: 4, core: 2. Of those that a mesh axis runs over, the one named last changes fastest.
Arguments:
- tokens: bfloat16 [32768, 768], P('dp'), may hold values from -6 to 6
- query_weight: bfloat16 [768, 768], P('dp', 'tensor'), may hold values from -0.21875 to 0.21875
- key_weight: bfloat16 [768, 768], P('dp', 'tensor'), may hold values from -0.21875 to 0.21875
- value_weight: bfloat16 [768, 768], P('dp', 'tensor'), may hold values from -0.21875 to 0.21875
- output_weight: bfloat16 [768, 768], P('dp', 'tensor'), may hold values from -1.75 to 1.75
- up_weight: bfloat16 [768, 3072], P('dp', 'tensor'), may hold values from -0.21875 to 0.21875
- down_weight: bfloat16 [768, 3072], P('dp', 'tensor'), may hold values from -0.109375 to 0.109375
- query_bias: float32 [768], P('tensor'), may hold values from -3 to 3
- value_bias: float32 [768], P('tensor'), may hold values from -3 to 3
- output_bias: float32 [768], replicated, may hold values from -0.6 to 0.6
- first_gain: float32 [768], replicated, may hold values from 0.5 to 1.5
- first_shift: float32 [768], replicated, may hold values from -0.6 to 0.6
- up_bias: float32 [3072], P('tensor'), may hold values from -3 to 3
- down_bias: float32 [768], replicated, may hold values from -0.6 to 0.6
- second_gain: float32 [768], replicated, may hold values from 0.5 to 1.5
- second_shift: float32 [768], replicated, may hold values from -0.6 to 0.6
- group_sizes: int32 [8], replicated, may hold values from 1 to 128, 256 in all
- sentence_order: int32 [512], replicated, may hold values from 0 to 511, each once
Outputs:
- pair_loss: float32 [], replicated
- grad_tokens: float32 [32768, 768], P('dp')
- grad_query_weight: float32 [768, 768], P('dp', 'tensor')
- grad_key_weight: float32 [768, 768], P('dp', 'tensor')
- grad_value_weight: float32 [768, 768], P('dp', 'tensor')
- grad_output_weight: float32 [768, 768], P('dp', 'tensor')
- grad_up_weight: float32 [768, 3072], P('dp', 'tensor')
- grad_down_weight: float32 [768, 3072], P('dp', 'tensor')
- grad_query_bias: float32 [768], P('tensor')
- grad_value_bias: float32 [768], P('tensor')
- grad_output_bias: float32 [768], replicated
- grad_first_gain: float32 [768], replicated
- grad_first_shift: float32 [768], replicated
- grad_up_bias: float32 [3072], P('tensor')
- grad_down_bias: float32 [768], replicated
- grad_second_gain: float32 [768], replicated
- grad_second_shift: float32 [768], replicated
Inputs may be any that keep to these rules, and one draw needn't show every extreme that they name: Group g holds the pairs from group_sizes[0] + ... + group_sizes[g - 1] onward; the sizes add up to 256 and the largest is 128. A permutation of the sentences: pair p has source sentence_order[p] and target sentence_order[256 + p].
All inputs are finite; a program needn't handle non-finite values.
Results may differ from a plain program's by a relative error of at most 0.02.
Values may be sent and summed in bfloat16 or wider, within the bound.
No kernel may reach another device: no remote copies, remote signals or barrier semaphores. Data moves between devices by JAX's collectives and lax.ppermute only.
A program may use at most 192 MiB of HBM per device.

v0:
```python
import jax
import jax.numpy as jnp
from jax import lax
from jax.sharding import PartitionSpec as P

D = 768
HD = 64
SEQ = 64


score_scale = 40.0
margin = 0.3
loss_scale = 65536.0
norm_eps = 1e-06
masked_score = -30000.0


def product(left, right):
    return jnp.dot(left, right, preferred_element_type=jnp.float32)


def contract_last(left, right):
    return lax.dot_general(
        left, right, (((1,), (1,)), ((), ())), preferred_element_type=jnp.float32
    )


def contract_first(left, right):
    return lax.dot_general(
        left, right, (((0,), (0,)), ((), ())), preferred_element_type=jnp.float32
    )


def exact_gelu(values):
    return jax.nn.gelu(values, approximate=False)


def norm_forward(values, gain_vec, shift_vec):
    centre = jnp.mean(values, axis=-1, keepdims=True)
    spread = jnp.mean(jnp.square(values - centre), axis=-1, keepdims=True)
    inv_scale = lax.rsqrt(spread + norm_eps)
    normed = (values - centre) * inv_scale
    return (normed * gain_vec + shift_vec, normed, inv_scale)


def norm_backward(upstream, normed, inv_scale, gain_vec):
    scaled = upstream * gain_vec
    first_mean = jnp.mean(scaled, axis=-1, keepdims=True)
    second_mean = jnp.mean(scaled * normed, axis=-1, keepdims=True)
    grad_in = inv_scale * (scaled - first_mean - normed * second_mean)
    return (grad_in, jnp.sum(upstream * normed, axis=0), jnp.sum(upstream, axis=0))


def pair_objective(gathered, pooled, group_sizes, sentence_order, device):
    total_sent = gathered.shape[0]
    pair_count = total_sent // 2
    own_count = pooled.shape[0]
    unit_all = gathered * lax.rsqrt(jnp.sum(gathered * gathered, axis=-1, keepdims=True) + norm_eps)
    unit_low = unit_all.astype(jnp.bfloat16)
    sources = jnp.take(unit_low, sentence_order[:pair_count], axis=0)
    targets = jnp.take(unit_low, sentence_order[pair_count:], axis=0)
    group_ends = jnp.cumsum(group_sizes)
    pair_ids = jnp.arange(pair_count, dtype=jnp.int32)
    group_of = jnp.sum((pair_ids[:, None] >= group_ends[None, :]).astype(jnp.int32), axis=1)
    block_rows = min(512, pair_count)

    def scan_step(carried, offset):
        col_peak, col_total = carried
        row_ids = offset + jnp.arange(block_rows, dtype=jnp.int32)
        row_units = lax.dynamic_slice_in_dim(sources, offset, block_rows, 0)
        row_groups = lax.dynamic_slice_in_dim(group_of, offset, block_rows, 0)
        is_same = row_ids[:, None] == pair_ids[None, :]
        scores = score_scale * contract_last(row_units, targets)
        scores = scores - score_scale * margin * is_same.astype(jnp.float32)
        scores = jnp.where(row_groups[:, None] == group_of[None, :], scores, masked_score)
        row_peak = jnp.max(scores, axis=1, keepdims=True)
        row_lse = row_peak[:, 0] + jnp.log(jnp.sum(jnp.exp(scores - row_peak), axis=1))
        diagonal = jnp.sum(jnp.where(is_same, scores, 0.0), axis=1)
        new_peak = jnp.maximum(col_peak, jnp.max(scores, axis=0))
        new_total = col_total * jnp.exp(col_peak - new_peak) + jnp.sum(
            jnp.exp(scores - new_peak[None, :]), axis=0
        )
        return ((new_peak, new_total), (row_lse, diagonal))

    offsets = jnp.arange(pair_count // block_rows, dtype=jnp.int32) * block_rows
    start_state = (
        jnp.full((pair_count,), -1e30, jnp.float32),
        jnp.zeros((pair_count,), jnp.float32),
    )
    (col_peak, col_total), (row_lse, diagonal) = lax.scan(scan_step, start_state, offsets)
    col_lse = col_peak + jnp.log(col_total)
    row_lse = row_lse.reshape(pair_count)
    diagonal = diagonal.reshape(pair_count)
    loss_value = jnp.mean(row_lse + col_lse - 2.0 * diagonal)
    own_ids = device * own_count + jnp.arange(own_count, dtype=jnp.int32)
    matches = sentence_order[None, :] == own_ids[:, None]
    position = jnp.sum(
        jnp.where(matches, jnp.arange(total_sent, dtype=jnp.int32)[None, :], 0), axis=1
    )
    is_source = position < pair_count
    own_pair = jnp.where(is_source, position, position - pair_count)
    own_inverse = lax.rsqrt(jnp.sum(pooled * pooled, axis=-1, keepdims=True) + norm_eps)
    own_unit = pooled * own_inverse
    own_low = own_unit.astype(jnp.bfloat16)
    source_rows = is_source[:, None]
    pair_match = own_pair[:, None] == pair_ids[None, :]
    toward_targets = score_scale * contract_last(own_low, targets)
    toward_sources = score_scale * contract_last(own_low, sources)
    own_scores = jnp.where(source_rows, toward_targets, toward_sources)
    own_scores = own_scores - score_scale * margin * pair_match.astype(jnp.float32)
    own_group = jnp.sum(jnp.where(pair_match, group_of[None, :], 0), axis=1)
    own_scores = jnp.where(own_group[:, None] == group_of[None, :], own_scores, masked_score)
    own_lse = jnp.sum(
        jnp.where(pair_match, jnp.where(source_rows, row_lse[None, :], col_lse[None, :]), 0.0),
        axis=1,
    )
    other_lse = jnp.where(source_rows, col_lse[None, :], row_lse[None, :])
    grad_coeff = loss_scale / pair_count
    grad_scores = grad_coeff * (
        jnp.exp(own_scores - own_lse[:, None])
        + jnp.exp(own_scores - other_lse)
        - 2.0 * pair_match.astype(jnp.float32)
    )
    grad_low = grad_scores.astype(jnp.bfloat16)
    grad_unit = score_scale * jnp.where(
        source_rows, product(grad_low, targets), product(grad_low, sources)
    )
    grad_pooled = own_inverse * (
        grad_unit - own_unit * jnp.sum(grad_unit * own_unit, axis=-1, keepdims=True)
    )
    return (loss_value, grad_pooled)


def local(
    tokens,
    query_weight,
    key_weight,
    value_weight,
    output_weight,
    up_weight,
    down_weight,
    query_bias,
    value_bias,
    output_bias,
    first_gain,
    first_shift,
    up_bias,
    down_bias,
    second_gain,
    second_shift,
    group_sizes,
    sentence_order,
):
    full_query, full_key, full_value, full_output, full_up, full_down = (
        lax.all_gather(query_weight, "dp", axis=0, tiled=True),
        lax.all_gather(key_weight, "dp", axis=0, tiled=True),
        lax.all_gather(value_weight, "dp", axis=0, tiled=True),
        lax.all_gather(output_weight, "dp", axis=0, tiled=True),
        lax.all_gather(up_weight, "dp", axis=0, tiled=True),
        lax.all_gather(down_weight, "dp", axis=0, tiled=True),
    )
    row_count = tokens.shape[0]
    sentences = row_count // SEQ
    head_cols = full_query.shape[1]
    head_shape = (sentences, SEQ, head_cols // HD, HD)
    attn_scale = HD ** (-0.5)
    queries = (product(tokens, full_query) + query_bias).astype(jnp.bfloat16)
    key_rows = product(tokens, full_key).astype(jnp.bfloat16)
    values = (product(tokens, full_value) + value_bias).astype(jnp.bfloat16)
    query_heads = queries.reshape(head_shape)
    key_heads = key_rows.reshape(head_shape)
    value_heads = values.reshape(head_shape)
    scores = (
        jnp.einsum("sqhd,skhd->shqk", query_heads, key_heads, preferred_element_type=jnp.float32)
        * attn_scale
    )
    row_peak = jnp.max(scores, axis=-1, keepdims=True)
    log_norm = row_peak + jnp.log(jnp.sum(jnp.exp(scores - row_peak), axis=-1, keepdims=True))
    probs_low = jnp.exp(scores - log_norm).astype(jnp.bfloat16)
    context = jnp.einsum(
        "shqk,skhd->sqhd", probs_low, value_heads, preferred_element_type=jnp.float32
    )
    context = context.astype(jnp.bfloat16).reshape(row_count, head_cols)
    attention_part = contract_last(context, full_output).astype(jnp.bfloat16)
    attended = lax.psum(attention_part, "tensor").astype(jnp.float32)
    residual = tokens.astype(jnp.float32) + attended + output_bias
    hidden_first, normed_first, inv_first = norm_forward(residual, first_gain, first_shift)
    hidden_low = hidden_first.astype(jnp.bfloat16)
    pre_act = product(hidden_low, full_up) + up_bias
    activation, gelu_back = jax.vjp(exact_gelu, pre_act)
    act_low = activation.astype(jnp.bfloat16)
    ffn_part = contract_last(act_low, full_down).astype(jnp.bfloat16)
    ffn_total = lax.psum(ffn_part, "tensor").astype(jnp.float32)
    second = hidden_first + ffn_total + down_bias
    output, normed_two, inv_two = norm_forward(second, second_gain, second_shift)
    pooled = jnp.mean(output.reshape(sentences, SEQ, D), axis=1)
    gathered = lax.all_gather(pooled, "dp", axis=0, tiled=True)
    loss_value, grad_pooled = pair_objective(
        gathered, pooled, group_sizes, sentence_order, lax.axis_index("dp")
    )
    grad_output = jnp.broadcast_to((grad_pooled / SEQ)[:, None, :], (sentences, SEQ, D)).reshape(
        row_count, D
    )
    grad_second, grad_second_gain, grad_second_shift = norm_backward(
        grad_output, normed_two, inv_two, second_gain
    )
    grad_down_bias = jnp.sum(grad_second, axis=0)
    grad_ffn_low = grad_second.astype(jnp.bfloat16)
    grad_down_weight = contract_first(grad_ffn_low, act_low)
    (grad_pre,) = gelu_back(product(grad_ffn_low, full_down))
    grad_pre_low = grad_pre.astype(jnp.bfloat16)
    grad_up_bias = jnp.sum(grad_pre_low.astype(jnp.float32), axis=0)
    grad_up_weight = contract_first(hidden_low, grad_pre_low)
    hidden_part = contract_last(grad_pre_low, full_up).astype(jnp.bfloat16)
    grad_hidden = grad_second + lax.psum(hidden_part, "tensor").astype(jnp.float32)
    grad_residual, grad_first_gain, grad_first_shift = norm_backward(
        grad_hidden, normed_first, inv_first, first_gain
    )
    grad_output_bias = jnp.sum(grad_residual, axis=0)
    grad_attn_low = grad_residual.astype(jnp.bfloat16)
    grad_output_weight = contract_first(grad_attn_low, context)
    grad_context = product(grad_attn_low, full_output).astype(jnp.bfloat16).reshape(head_shape)
    again_scores = (
        jnp.einsum("sqhd,skhd->shqk", query_heads, key_heads, preferred_element_type=jnp.float32)
        * attn_scale
    )
    attn_probs = jnp.exp(again_scores - log_norm)
    again_low = attn_probs.astype(jnp.bfloat16)
    grad_values = jnp.einsum(
        "shqk,sqhd->skhd", again_low, grad_context, preferred_element_type=jnp.float32
    )
    grad_values = grad_values.astype(jnp.bfloat16).reshape(row_count, head_cols)
    grad_probs = jnp.einsum(
        "sqhd,skhd->shqk", grad_context, value_heads, preferred_element_type=jnp.float32
    )
    grad_scores = attn_probs * (
        grad_probs - jnp.sum(grad_probs * attn_probs, axis=-1, keepdims=True)
    )
    grad_scores_low = grad_scores.astype(jnp.bfloat16)
    grad_queries = jnp.einsum(
        "shqk,skhd->sqhd", grad_scores_low, key_heads, preferred_element_type=jnp.float32
    )
    grad_queries = (grad_queries * attn_scale).astype(jnp.bfloat16).reshape(row_count, head_cols)
    grad_keys = jnp.einsum(
        "shqk,sqhd->skhd", grad_scores_low, query_heads, preferred_element_type=jnp.float32
    )
    grad_keys = (grad_keys * attn_scale).astype(jnp.bfloat16).reshape(row_count, head_cols)
    grad_query_bias = jnp.sum(grad_queries.astype(jnp.float32), axis=0)
    grad_value_bias = jnp.sum(grad_values.astype(jnp.float32), axis=0)
    grad_query_weight = contract_first(tokens, grad_queries)
    grad_key_weight = contract_first(tokens, grad_keys)
    grad_value_weight = contract_first(tokens, grad_values)
    input_terms = (
        contract_last(grad_queries, full_query)
        + contract_last(grad_keys, full_key)
        + contract_last(grad_values, full_value)
    ).astype(jnp.bfloat16)
    grad_tokens = grad_residual + lax.psum(input_terms, "tensor").astype(jnp.float32)
    shard_query, shard_key, shard_value, shard_output, shard_up, shard_down = (
        lax.psum_scatter(grad_query_weight, "dp", scatter_dimension=0, tiled=True),
        lax.psum_scatter(grad_key_weight, "dp", scatter_dimension=0, tiled=True),
        lax.psum_scatter(grad_value_weight, "dp", scatter_dimension=0, tiled=True),
        lax.psum_scatter(grad_output_weight, "dp", scatter_dimension=0, tiled=True),
        lax.psum_scatter(grad_up_weight, "dp", scatter_dimension=0, tiled=True),
        lax.psum_scatter(grad_down_weight, "dp", scatter_dimension=0, tiled=True),
    )
    (
        sum_query_bias,
        sum_value_bias,
        sum_output_bias,
        sum_first_gain,
        sum_first_shift,
        sum_up_bias,
        sum_down_bias,
        sum_second_gain,
        sum_second_shift,
    ) = lax.psum(
        (
            grad_query_bias,
            grad_value_bias,
            grad_output_bias,
            grad_first_gain,
            grad_first_shift,
            grad_up_bias,
            grad_down_bias,
            grad_second_gain,
            grad_second_shift,
        ),
        "dp",
    )
    return (
        loss_value,
        grad_tokens,
        shard_query,
        shard_key,
        shard_value,
        shard_output,
        shard_up,
        shard_down,
        sum_query_bias,
        sum_value_bias,
        sum_output_bias,
        sum_first_gain,
        sum_first_shift,
        sum_up_bias,
        sum_down_bias,
        sum_second_gain,
        sum_second_shift,
    )


def solution(mesh):
    placed = (
        P("dp", None),
        P("dp", "tensor"),
        P("dp", "tensor"),
        P("dp", "tensor"),
        P("dp", "tensor"),
        P("dp", "tensor"),
        P("dp", "tensor"),
        P("tensor"),
        P("tensor"),
        P(),
        P(),
        P(),
        P("tensor"),
        P(),
        P(),
        P(),
        P(),
        P(),
    )
    return jax.shard_map(
        local,
        mesh=mesh,
        in_specs=placed,
        out_specs=(
            P(),
            P("dp", None),
            P("dp", "tensor"),
            P("dp", "tensor"),
            P("dp", "tensor"),
            P("dp", "tensor"),
            P("dp", "tensor"),
            P("dp", "tensor"),
            P("tensor"),
            P("tensor"),
            P(),
            P(),
            P(),
            P("tensor"),
            P(),
            P(),
            P(),
        ),
        check_vma=False,
    )
```

profile of v0, /device:TPU:0, one launch (start us, length us, event | category | flops | bytes accessed | tf_op | source)
XLA Modules:
  0.0 1440.1 jit_solution(17819014441857637793)
XLA Ops:
  8.1 48.6 %all_gather.22 = bf16[768,384]{1,0:T(8,128)(2,1)} all-gather(bf16[48,384]{1,0:T(8,128)(2,1)} %param.21), channel_id=1, replica_groups=mesh['dp'=16,'tensor'=2] {'dp'}, dimensions={0}, use_global_device_ids=true | all-gather | bytes 626688 | tf_op jit(solution)/shard_map/all_gather | solution.py:155
  56.7 39.1 %all_gather.23 = bf16[768,384]{1,0:T(8,128)(2,1)S(1)} all-gather(bf16[48,384]{1,0:T(8,128)(2,1)} %param.22), channel_id=1, replica_groups=mesh['dp'=16,'tensor'=2] {'dp'}, dimensions={0}, use_global_device_ids=true | all-gather | bytes 626688 | tf_op jit(solution)/shard_map/all_gather | solution.py:156
  95.7 43.6 %all_gather.21 = bf16[768,384]{1,0:T(8,128)(2,1)} all-gather(bf16[48,384]{1,0:T(8,128)(2,1)} %param.23), channel_id=1, replica_groups=mesh['dp'=16,'tensor'=2] {'dp'}, dimensions={0}, use_global_device_ids=true | all-gather | bytes 626688 | tf_op jit(solution)/shard_map/all_gather | solution.py:157
  139.4 41.7 %all_gather.24 = bf16[768,384]{1,0:T(8,128)(2,1)} all-gather(bf16[48,384]{1,0:T(8,128)(2,1)} %param.24), channel_id=1, replica_groups=mesh['dp'=16,'tensor'=2] {'dp'}, dimensions={0}, use_global_device_ids=true | all-gather | bytes 626688 | tf_op jit(solution)/shard_map/all_gather | solution.py:158
  181.0 5.0 convolution_convert_fusion.4
  186.0 5.9 reshape.261
  191.9 4.0 add_convert_fusion.3
  195.9 5.9 reshape.263
  201.8 4.0 add_convert_fusion.2
  205.8 5.9 reshape.264
  211.7 6.6 copy.110
  218.3 4.4 multiply_reduce_fusion.7
  228.9 3.7 copy.103
  232.6 5.6 reshape.226
  238.2 5.1 convolution_convert_fusion
  244.5 19.4 %all-reduce.6.cloned.1.call-done = bf16[2048,768]{1,0:T(8,128)(2,1)} async-done(((bf16[2048,768]{1,0:T(8,128)(2,1)}), bf16[2048,768]{1,0:T(8,128)(2,1)}) %all-reduce.6.cloned.1.call-update) | async-done | bytes 3145744 | tf_op jit(solution)/shard_map/psum | solution.py:185
  263.9 3.1 fusion.13
  269.0 37.3 %all-gather.4.cloned.1.call-done = bf16[768,1536]{1,0:T(8,128)(2,1)} async-done(((bf16[48,1536]{1,0:T(8,128)(2,1)}), bf16[768,1536]{1,0:T(8,128)(2,1)}) %all-gather.4.cloned.1.call-update) | async-done | bytes 2359312 | tf_op jit(solution)/shard_map/all_gather | solution.py:159
  306.4 36.5 %multiply_convert_fusion = (bf16[2048,1536]{1,0:T(8,128)(2,1)}, f32[2048,1536]{1,0:T(8,128)}, f32[2048,1536]{1,0:T(8,128)}) fusion(f32[1536]{0:T(1024)S(1)} %copy-done.28, bf16[768,1536]{1,0:T(8,128)(2,1)} %all-gather.4.cloned.1.call-done, f32[768]{0:T(1024)S(1)} %copy-done.26, f32[768]{0:T(1024)S(1)} %copy-done.22, f32[2048]{0:T(1024)S(1)} %add_rsqrt_fusion.1, ...), kind=kOutput, calls=%fused_computation.6 | convolution fusion | flops 5053612032 | bytes 40139776 | tf_op jit(solution)/shard_map/dot_general | solution.py:19
  342.9 26.9 %all-gather.6.cloned.1.call-done = bf16[768,1536]{1,0:T(8,128)(2,1)} async-done(((bf16[48,1536]{1,0:T(8,128)(2,1)}), bf16[768,1536]{1,0:T(8,128)(2,1)}) %all-gather.6.cloned.1.call-update) | async-done | bytes 2359312 | tf_op jit(solution)/shard_map/all_gather | solution.py:160
  369.9 9.1 convolution_convert_fusion.2
  379.0 21.6 %all-reduce.8.cloned.1.call-done = bf16[2048,768]{1,0:T(8,128)(2,1)} async-done(((bf16[2048,768]{1,0:T(8,128)(2,1)}), bf16[2048,768]{1,0:T(8,128)(2,1)}) %all-reduce.8.cloned.1.call-update) | async-done | bytes 3145744 | tf_op jit(solution)/shard_map/psum | solution.py:193
  400.6 4.9 fusion.49
  410.0 58.4 %all-gather.8.cloned.1.call-done = f32[512,768]{1,0:T(8,128)} async-done(((f32[32,768]{1,0:T(8,128)}), f32[512,768]{1,0:T(8,128)}) %all-gather.8.cloned.1.call-update) | async-done | bytes 1572880 | tf_op jit(solution)/shard_map/all_gather | solution.py:197
  472.5 3.4 gather_fusion.1
  475.9 3.4 gather_fusion
  487.3 3.7 fusion.11
  491.6 5.4 fusion.9
  497.0 19.8 %convert_reduce_fusion = (f32[1536]{0:T(1024)S(1)}, bf16[2048,1536]{1,0:T(8,128)(2,1)}) fusion(f32[2048,1536]{1,0:T(8,128)} %get-tuple-element.144, bf16[768,1536]{1,0:T(8,128)(2,1)} %all-gather.6.cloned.1.call-done, f32[2048,768]{1,0:T(8,128)} %fusion.9, f32[2048,1536]{1,0:T(8,128)} %get-tuple-element.155, f32[1536]{0:T(1024)S(1)} %copy-done.28), kind=kOutput, calls=%fused_computation.4 | convolution fusion | flops 4886886912 | bytes 40120320 | tf_op jit(solution)/shard_map/dot_general | solution.py:19
  516.8 9.4 convolution_convert_fusion.1
  526.6 21.4 %all-reduce.10.cloned.1.call-done = bf16[2048,768]{1,0:T(8,128)(2,1)} async-done(((bf16[2048,768]{1,0:T(8,128)(2,1)}), bf16[2048,768]{1,0:T(8,128)(2,1)}) %all-reduce.10.cloned.1.call-update) | async-done | bytes 3145744 | tf_op jit(solution)/shard_map/psum | solution.py:215
  548.1 7.2 multiply_reduce_fusion
  555.4 5.5 fusion.48
  563.5 2.9 convolution_convert_fusion.3
  566.5 6.1 reshape.262
  572.5 10.7 multiply_reduce_fusion.1
  583.3 3.3 convert_reduce_fusion.1
  586.6 5.1 multiply_convert_fusion.3
  591.8 3.4 convert_reduce_fusion.2
  595.2 3.5 fusion.16
  598.6 4.2 copy.113
  602.9 3.4 reshape.231
  606.3 4.2 copy.109
  610.5 3.4 reshape.230
  613.9 4.2 copy.115
  618.1 3.6 reshape.232
  621.8 3.5 fusion.51
  627.2 3.7 add_convert_fusion.1
  631.0 6.2 fusion.25
  637.3 4.3 convolution_bitcast_fusion.1
  641.5 2.7 copy.125
  644.3 3.8 convolution_bitcast_fusion.2
  648.1 2.7 copy.123
  650.9 4.0 convolution_bitcast_fusion
  654.9 2.7 copy.127
  657.7 10.8 fusion.28
  668.6 11.7 fusion.37
  681.1 77.8 %all-reduce = (f32[384]{0:T(512)}, f32[384]{0:T(512)}, f32[768]{0:T(1024)}, f32[768]{0:T(1024)}, f32[768]{0:T(1024)}, /*index=5*/f32[1536]{0:T(1024)}, f32[768]{0:T(1024)}, f32[768]{0:T(1024)}, f32[768]{0:T(1024)}) all-reduce(f32[384]{0:T(512)S(1)} %reduce_sum.309, ...), channel_id=1, replica_groups=mesh['dp'=16,'tensor'=2] {'dp'}, use_global_device_ids=true, to_apply=%region_37.39 | all-reduce | flops 6912 | bytes 55296 | tf_op jit(solution)/shard_map/psum | solution.py:277
  759.0 7.0 convert_add_fusion
  766.0 124.3 %reduce-scatter.21.cloned.1.call-done = f32[48,384]{1,0:T(8,128)} async-done(((f32[768,384]{1,0:T(8,128)}), f32[48,384]{1,0:T(8,128)}) %reduce-scatter.21.cloned.1.call-update) | async-done | bytes 73744
  890.3 128.1 %reduce-scatter.19.cloned.1.call-done = f32[48,384]{1,0:T(8,128)} async-done(((f32[768,384]{1,0:T(8,128)}), f32[48,384]{1,0:T(8,128)}) %reduce-scatter.19.cloned.1.call-update) | async-done | bytes 73744
  1018.4 127.9 %reduce-scatter.23.cloned.1.call-done = f32[48,384]{1,0:T(8,128)} async-done(((f32[768,384]{1,0:T(8,128)}), f32[48,384]{1,0:T(8,128)}) %reduce-scatter.23.cloned.1.call-update) | async-done | bytes 73744
  1146.3 142.1 %reduce-scatter.17.cloned.1.call-done = f32[48,1536]{1,0:T(8,128)} async-done(((f32[768,1536]{1,0:T(8,128)}), f32[48,1536]{1,0:T(8,128)}) %reduce-scatter.17.cloned.1.call-update) | async-done | bytes 294928 | tf_op jit(solution)/shard_map/reduce_scatter | solution.py:265
  1288.4 142.8 %reduce-scatter.15.cloned.1.call-done = f32[48,1536]{1,0:T(8,128)} async-done(((f32[768,1536]{1,0:T(8,128)}), f32[48,1536]{1,0:T(8,128)}) %reduce-scatter.15.cloned.1.call-update) | async-done | bytes 294928 | tf_op jit(solution)/shard_map/reduce_scatter | solution.py:264
  (141 shorter events, 32.0 us)
Async XLA Ops:
  8.0 255.9 %all-reduce.6.cloned.1.call-start = ((), (), s32[]{:S(2)}) async-start(), calls=%async_computation.6 | async-start | bytes 6291456 | tf_op jit(solution)/shard_map/psum | solution.py:185
  95.7 85.3 %copy-start.17 = (bf16[768,384]{1,0:T(8,128)(2,1)}, bf16[768,384]{1,0:T(8,128)(2,1)S(1)}, u32[]{:S(2)}) copy-start(bf16[768,384]{1,0:T(8,128)(2,1)S(1)} %all_gather.23) | copy-start | bytes 1769476
  181.0 10.9 copy-start.3
  181.0 10.9 copy-start.29
  191.9 9.9 copy-start.30
  222.7 6.2 copy-start
  222.7 4.5 copy-start.8
  227.2 1.7 copy-start.14
  238.2 25.7 %copy-start.20 = (f32[768]{0:T(1024)S(1)}, f32[768]{0:T(1024)}, u32[]{:S(2)}) copy-start(f32[768]{0:T(1024)} %param.29) | copy-start | bytes 9220
  243.3 63.1 %all-gather.4.cloned.1.call-start = ((), (), s32[]{:S(2)}) async-start(), calls=%async_computation.7 | async-start | bytes 2506752 | tf_op jit(solution)/shard_map/all_gather | solution.py:159
  243.8 126.0 %all-gather.6.cloned.1.call-start = ((), (), s32[]{:S(2)}) async-start(), calls=%async_computation.8 | async-start | bytes 2506752 | tf_op jit(solution)/shard_map/all_gather | solution.py:160
  244.4 62.0 %copy-start.22 = (f32[768]{0:T(1024)S(1)}, f32[768]{0:T(1024)}, u32[]{:S(2)}) copy-start(f32[768]{0:T(1024)} %param.30) | copy-start | bytes 9220
  244.4 61.9 %copy-start.26 = (f32[768]{0:T(1024)S(1)}, f32[768]{0:T(1024)}, u32[]{:S(2)}) copy-start(f32[768]{0:T(1024)} %param.31) | copy-start | bytes 9220
  244.4 61.9 %copy-start.28 = (f32[1536]{0:T(1024)S(1)}, f32[1536]{0:T(1024)}, u32[]{:S(2)}) copy-start(f32[1536]{0:T(1024)} %param.32) | copy-start | bytes 18436
  244.5 156.1 %all-reduce.8.cloned.1.call-start = ((), (), s32[]{:S(2)}) async-start(), calls=%async_computation.9 | async-start | bytes 6291456 | tf_op jit(solution)/shard_map/psum | solution.py:193
  263.9 3.1 copy-start.5
  369.9 30.7 %copy-start.24 = (f32[768]{0:T(1024)S(1)}, f32[768]{0:T(1024)}, u32[]{:S(2)}) copy-start(f32[768]{0:T(1024)} %param.33) | copy-start | bytes 9220
  379.0 89.5 %all-gather.8.cloned.1.call-start = ((), (), s32[]{:S(2)}) async-start(), calls=%async_computation.10 | async-start | bytes 1671168 | tf_op jit(solution)/shard_map/all_gather | solution.py:197
  405.5 2.7 copy-start.2
  405.5 0.9 copy-start.21
  405.5 0.9 copy-start.25
  405.5 3.7 copy-start.31
  405.6 3.9 copy-start.23
  409.0 139.1 %all-reduce.10.cloned.1.call-start = ((), (), s32[]{:S(2)}) async-start(), calls=%async_computation.11 | async-start | bytes 6291456 | tf_op jit(solution)/shard_map/psum | solution.py:215
  497.0 19.8 %copy-start.27 = (bf16[768,1536]{1,0:T(8,128)(2,1)S(1)}, bf16[768,1536]{1,0:T(8,128)(2,1)}, u32[]{:S(2)}) copy-start(bf16[768,1536]{1,0:T(8,128)(2,1)} %all-gather.4.cloned.1.call-done) | copy-start | bytes 7077892
  526.2 232.8 %all-reduce.12.cloned.1.call-start = ((), (), s32[]{:S(2)}) async-start(), calls=%async_computation.12 | async-start | bytes 6291456 | tf_op jit(solution)/shard_map/psum | solution.py:258
  548.1 7.3 copy-start.6
  548.1 7.3 copy-start.11
  555.3 8.2 copy-start.19
  560.8 2.7 copy-start.1
  563.5 9.0 copy-start.15
  566.5 16.8 %slice-start = ((s8[6291456]{0:T(1024)(128)(4,1)}), s8[2097152]{0:T(1024)(128)(4,1)S(1)}, s32[]{:S(2)}) async-start(s8[6291456]{0:T(1024)(128)(4,1)} %bitcast.88), calls=%async_computation.19 | async-start | bytes 4194304
  572.5 10.7 slice-start.1
  572.5 10.7 copy-start.9
  586.6 5.1 copy-start.10
  591.8 3.4 copy-start.7
  621.7 3.5 copy-start.12
  621.8 3.5 copy-start.18
  625.3 1.9 copy-start.13
  625.3 1.9 copy-start.16
  630.9 6.4 copy-start.4
  630.9 135.1 %reduce-scatter.13.cloned.1.call-start = ((), (), s32[]{:S(2)}) async-start(), calls=%async_computation.13 | async-start | bytes 1253376 | tf_op jit(solution)/shard_map/reduce_scatter | solution.py:263
  637.2 253.1 %reduce-scatter.21.cloned.1.call-start = ((), (), s32[]{:S(2)}) async-start(), calls=%async_computation.17 | async-start | bytes 1253376
  644.3 374.1 %reduce-scatter.19.cloned.1.call-start = ((), (), s32[]{:S(2)}) async-start(), calls=%async_computation.16 | async-start | bytes 1253376
  650.8 495.5 %reduce-scatter.23.cloned.1.call-start = ((), (), s32[]{:S(2)}) async-start(), calls=%async_computation.18 | async-start | bytes 1253376
  657.6 630.8 %reduce-scatter.17.cloned.1.call-start = ((), (), s32[]{:S(2)}) async-start(), calls=%async_computation.15 | async-start | bytes 5013504 | tf_op jit(solution)/shard_map/reduce_scatter | solution.py:265
  668.5 762.6 %reduce-scatter.15.cloned.1.call-start = ((), (), s32[]{:S(2)}) async-start(), calls=%async_computation.14 | async-start | bytes 5013504 | tf_op jit(solution)/shard_map/reduce_scatter | solution.py:264
Sparse Core Ops, SparseCore 0:
  243.4 20.4 all-reduce.5
  379.1 21.4 all-reduce.7
  526.3 21.7 all-reduce.9
  631.0 24.3 all-reduce.11
Sparse Core Ops, SparseCore 1:
  246.5 59.8 all-gather.3
  309.0 60.8 all-gather.5
  409.1 59.3 all-gather.7
  637.3 124.9 reduce-scatter.12
  767.6 122.7 reduce-scatter.20
  895.7 122.7 reduce-scatter.18
  1023.6 122.7 reduce-scatter.22
  1151.9 136.4 reduce-scatter.16
  1294.8 136.3 reduce-scatter.14
where the time goes:
time: 1450 us; the launch traced here: 1440 us
  waiting for transfers between devices  852 us (59%)
  blocking collectives  251 us (17%)
  matrix products  180 us (12%)
  local copies, waits for them, and re-layouts  83.2 us (6%)
  other arithmetic  55.4 us (4%)
  between operations  18.4 us (1%)
    unnamed x16, waiting for transfers between devices  382 us
    reduce_scatter x1, waiting for transfers between devices, local(): lax.psum_scatter(grad_up_weight, 'dp', scatter_dimension=0, tiled=True)  143 us
    reduce_scatter x1, waiting for transfers between devices, local(): lax.psum_scatter(grad_down_weight, 'dp', scatter_dimension=0, tiled=True)  142 us
    psum x1, blocking collectives, local(): lax.psum((grad_query_bias, grad_value_bias, grad_output_bias, grad_first_...  77.8 us
    dot_general x8, matrix products, product(): return jnp.dot(left, right, preferred_element_type=jnp.float32)  75 us
    all_gather x1, waiting for transfers between devices, local(): gathered = lax.all_gather(pooled, 'dp', axis=0, tiled=True)  58.4 us
    all_gather x1, blocking collectives, local(): lax.all_gather(query_weight, 'dp', axis=0, tiled=True)  48.6 us
    all_gather x1, blocking collectives, local(): lax.all_gather(value_weight, 'dp', axis=0, tiled=True)  43.6 us
  transfers between devices with their start and end apart: 13, of which 11 were waited for; matrix products, arithmetic and copies ran while one was open for 7% of the time, Pallas kernels for 0%

commit v1 on v0

v1 whole, which is shorter than its diff:
```python
import functools

import jax
import jax.numpy as jnp
from jax import lax
from jax.experimental import pallas as pl
from jax.experimental.pallas import tpu as pltpu
from jax.sharding import PartitionSpec as P

D = 768
HD = 64
SEQ = 64

score_scale = 40.0
margin = 0.3
loss_scale = 65536.0
norm_eps = 1e-06
masked_score = -30000.0

bf16 = jnp.bfloat16
f32 = jnp.float32

ALONG_Z = (4, 8, 12)
IN_PLANE = (1, 2, 3)


def contract(left, right, left_dim, right_dim):
    return lax.dot_general(
        left, right, (((left_dim,), (right_dim,)), ((), ())), preferred_element_type=f32
    )


def product(left, right):
    return contract(left, right, 1, 0)


def contract_last(left, right):
    return contract(left, right, 1, 1)


def contract_first(left, right):
    return contract(left, right, 0, 0)


def swap_cores(array):
    return lax.ppermute(array, "tensor", [(0, 1), (1, 0)])


def swap_chips(array, mask):
    count = lax.axis_size("dp")
    return lax.ppermute(array, "dp", [(i, i ^ mask) for i in range(count)])


def gather_pieces(shard, first, second):
    near = jnp.concatenate([shard] + [swap_chips(shard, mask) for mask in first], axis=0)
    return [near] + [swap_chips(near, mask) for mask in second]


def reduce_pieces(slabs, first, second):
    total = slabs[0].astype(f32)
    for slab, mask in zip(slabs[1:], first):
        total = total + swap_chips(slab, mask).astype(f32)
    rows = total.shape[0] // 4
    total = total.astype(bf16)
    own = total[:rows].astype(f32)
    for i, mask in enumerate(second):
        part = lax.slice_in_dim(total, (i + 1) * rows, (i + 2) * rows, axis=0)
        own = own + swap_chips(part, mask).astype(f32)
    return own


def sum_small(array):
    for group in (ALONG_Z, IN_PLANE):
        a, b, c = [swap_chips(array, mask) for mask in group]
        array = (array + a) + (b + c)
    return array


def ordered(first, second):
    return [(j, i, a ^ b) for j, b in enumerate((0, *second)) for i, a in enumerate((0, *first))]


def place_kernel(order, rows, me_ref, *refs):
    pieces, full, sem = refs[:4], refs[4], refs[5]
    me = me_ref[0]
    copies = []
    for k, (j, i, mask) in enumerate(order):
        to = pl.multiple_of((me ^ mask) * rows, 16)
        copies.append(
            pltpu.make_async_copy(pieces[j].at[pl.ds(i * rows, rows)], full.at[pl.ds(to, rows)], sem.at[k])
        )
    for copy in copies:
        copy.start()
    for copy in copies:
        copy.wait()


def place_rows(pieces, first, second, me):
    rows = pieces[0].shape[0] // 4
    width = pieces[0].shape[1]
    return pl.pallas_call(
        functools.partial(place_kernel, ordered(first, second), rows),
        out_shape=jax.ShapeDtypeStruct((rows * 16, width), pieces[0].dtype),
        in_specs=[pl.BlockSpec(memory_space=pltpu.SMEM)] + [pl.BlockSpec(memory_space=pl.ANY)] * 4,
        out_specs=pl.BlockSpec(memory_space=pl.ANY),
        scratch_shapes=[pltpu.SemaphoreType.DMA((16,))],
        name="place_rows",
    )(me, *pieces)


def split_kernel(order, rows, me_ref, full, *refs):
    pieces, sem = refs[:4], refs[4]
    me = me_ref[0]
    copies = []
    for k, (j, i, mask) in enumerate(order):
        at = pl.multiple_of((me ^ mask) * rows, 16)
        copies.append(
            pltpu.make_async_copy(full.at[pl.ds(at, rows)], pieces[j].at[pl.ds(i * rows, rows)], sem.at[k])
        )
    for copy in copies:
        copy.start()
    for copy in copies:
        copy.wait()


def split_rows(full, first, second, me):
    rows = full.shape[0] // 16
    width = full.shape[1]
    return pl.pallas_call(
        functools.partial(split_kernel, ordered(second, first), rows),
        out_shape=[jax.ShapeDtypeStruct((rows * 4, width), full.dtype)] * 4,
        in_specs=[pl.BlockSpec(memory_space=pltpu.SMEM), pl.BlockSpec(memory_space=pl.ANY)],
        out_specs=[pl.BlockSpec(memory_space=pl.ANY)] * 4,
        scratch_shapes=[pltpu.SemaphoreType.DMA((16,))],
        name="split_rows",
    )(me, full)


def exact_gelu(values):
    return jax.nn.gelu(values, approximate=False)


def norm_forward(values, gain_vec, shift_vec):
    centre = jnp.mean(values, axis=-1, keepdims=True)
    spread = jnp.mean(jnp.square(values - centre), axis=-1, keepdims=True)
    inv_scale = lax.rsqrt(spread + norm_eps)
    normed = (values - centre) * inv_scale
    return (normed * gain_vec + shift_vec, normed, inv_scale)


def norm_backward(upstream, normed, inv_scale, gain_vec):
    scaled = upstream * gain_vec
    first_mean = jnp.mean(scaled, axis=-1, keepdims=True)
    second_mean = jnp.mean(scaled * normed, axis=-1, keepdims=True)
    grad_in = inv_scale * (scaled - first_mean - normed * second_mean)
    return (grad_in, jnp.sum(upstream * normed, axis=0), jnp.sum(upstream, axis=0))


def pair_objective(unit_low, pooled, group_sizes, sentence_order, device):
    total_sent = unit_low.shape[0]
    pair_count = total_sent // 2
    own_count = pooled.shape[0]
    sources = jnp.take(unit_low, sentence_order[:pair_count], axis=0)
    targets = jnp.take(unit_low, sentence_order[pair_count:], axis=0)
    group_ends = jnp.cumsum(group_sizes)
    pair_ids = jnp.arange(pair_count, dtype=jnp.int32)
    group_of = jnp.sum((pair_ids[:, None] >= group_ends[None, :]).astype(jnp.int32), axis=1)
    block_rows = min(512, pair_count)

    def scan_step(carried, offset):
        col_peak, col_total = carried
        row_ids = offset + jnp.arange(block_rows, dtype=jnp.int32)
        row_units = lax.dynamic_slice_in_dim(sources, offset, block_rows, 0)
        row_groups = lax.dynamic_slice_in_dim(group_of, offset, block_rows, 0)
        is_same = row_ids[:, None] == pair_ids[None, :]
        scores = score_scale * contract_last(row_units, targets)
        scores = scores - score_scale * margin * is_same.astype(jnp.float32)
        scores = jnp.where(row_groups[:, None] == group_of[None, :], scores, masked_score)
        row_peak = jnp.max(scores, axis=1, keepdims=True)
        row_lse = row_peak[:, 0] + jnp.log(jnp.sum(jnp.exp(scores - row_peak), axis=1))
        diagonal = jnp.sum(jnp.where(is_same, scores, 0.0), axis=1)
        new_peak = jnp.maximum(col_peak, jnp.max(scores, axis=0))
        new_total = col_total * jnp.exp(col_peak - new_peak) + jnp.sum(
            jnp.exp(scores - new_peak[None, :]), axis=0
        )
        return ((new_peak, new_total), (row_lse, diagonal))

    offsets = jnp.arange(pair_count // block_rows, dtype=jnp.int32) * block_rows
    start_state = (
        jnp.full((pair_count,), -1e30, jnp.float32),
        jnp.zeros((pair_count,), jnp.float32),
    )
    (col_peak, col_total), (row_lse, diagonal) = lax.scan(scan_step, start_state, offsets)
    col_lse = col_peak + jnp.log(col_total)
    row_lse = row_lse.reshape(pair_count)
    diagonal = diagonal.reshape(pair_count)
    loss_value = jnp.mean(row_lse + col_lse - 2.0 * diagonal)
    own_ids = device * own_count + jnp.arange(own_count, dtype=jnp.int32)
    matches = sentence_order[None, :] == own_ids[:, None]
    position = jnp.sum(
        jnp.where(matches, jnp.arange(total_sent, dtype=jnp.int32)[None, :], 0), axis=1
    )
    is_source = position < pair_count
    own_pair = jnp.where(is_source, position, position - pair_count)
    own_inverse = lax.rsqrt(jnp.sum(pooled * pooled, axis=-1, keepdims=True) + norm_eps)
    own_unit = pooled * own_inverse
    own_low = own_unit.astype(jnp.bfloat16)
    source_rows = is_source[:, None]
    pair_match = own_pair[:, None] == pair_ids[None, :]
    toward_targets = score_scale * contract_last(own_low, targets)
    toward_sources = score_scale * contract_last(own_low, sources)
    own_scores = jnp.where(source_rows, toward_targets, toward_sources)
    own_scores = own_scores - score_scale * margin * pair_match.astype(jnp.float32)
    own_group = jnp.sum(jnp.where(pair_match, group_of[None, :], 0), axis=1)
    own_scores = jnp.where(own_group[:, None] == group_of[None, :], own_scores, masked_score)
    own_lse = jnp.sum(
        jnp.where(pair_match, jnp.where(source_rows, row_lse[None, :], col_lse[None, :]), 0.0),
        axis=1,
    )
    other_lse = jnp.where(source_rows, col_lse[None, :], row_lse[None, :])
    grad_coeff = loss_scale / pair_count
    grad_scores = grad_coeff * (
        jnp.exp(own_scores - own_lse[:, None])
        + jnp.exp(own_scores - other_lse)
        - 2.0 * pair_match.astype(jnp.float32)
    )
    grad_low = grad_scores.astype(jnp.bfloat16)
    grad_unit = score_scale * jnp.where(
        source_rows, product(grad_low, targets), product(grad_low, sources)
    )
    grad_pooled = own_inverse * (
        grad_unit - own_unit * jnp.sum(grad_unit * own_unit, axis=-1, keepdims=True)
    )
    return (loss_value, grad_pooled)


def gather_units(own, core, me):
    if lax.axis_size("dp") != 16:
        return lax.all_gather(own, ("dp", "tensor"), axis=0, tiled=True)
    mine = place_rows(gather_pieces(own, ALONG_Z, IN_PLANE), ALONG_Z, IN_PLANE, me)
    other = swap_cores(mine)
    rows = own.shape[0]
    parts = both_cores(mine.reshape(16, rows, D), other.reshape(16, rows, D), core, 1)
    return parts.reshape(32 * rows, D)


def gather_full(shard, me):
    if lax.axis_size("dp") != 16:
        return lax.all_gather(shard, "dp", axis=0, tiled=True)
    return place_rows(gather_pieces(shard, ALONG_Z, IN_PLANE), ALONG_Z, IN_PLANE, me)


def reduce_full(partial, me):
    if lax.axis_size("dp") != 16:
        return lax.psum_scatter(partial.astype(f32), "dp", scatter_dimension=0, tiled=True)
    slabs = split_rows(partial.astype(bf16), IN_PLANE, ALONG_Z, me)
    return reduce_pieces(slabs, IN_PLANE, ALONG_Z)


def own_half(array, index, axis=0):
    size = array.shape[axis] // 2
    return lax.dynamic_slice_in_dim(array, index * size, size, axis)


def both_cores(own, other, core, axis):
    left = jnp.where(core == 0, own, other)
    right = jnp.where(core == 0, other, own)
    return jnp.concatenate([left, right], axis=axis)


def local(
    tokens, query_weight, key_weight, value_weight, output_weight, up_weight, down_weight,
    query_bias, value_bias, output_bias, first_gain, first_shift, up_bias, down_bias,
    second_gain, second_shift, group_sizes, sentence_order,
):
    core = lax.axis_index("tensor")
    dp_index = lax.axis_index("dp")
    me = dp_index.astype(jnp.int32).reshape(1)
    head_cols = query_weight.shape[1]
    hidden_cols = up_weight.shape[1]
    qkv_shard = jnp.concatenate([query_weight, key_weight, value_weight], axis=1)
    out_up_shard = jnp.concatenate([output_weight, up_weight], axis=1)
    full_qkv = gather_full(qkv_shard, me)
    full_out_up = gather_full(out_up_shard, me)
    down_own = gather_full(down_weight, me)
    out_up_other = swap_cores(full_out_up)
    down_other = swap_cores(down_own)
    out_own, up_own = full_out_up[:, :head_cols], full_out_up[:, head_cols:]
    out_other, up_other = out_up_other[:, :head_cols], out_up_other[:, head_cols:]
    full_up = both_cores(up_own, up_other, core, 1)
    full_down = both_cores(down_own, down_other, core, 1)
    up_bias_other = swap_cores(up_bias)
    full_up_bias = both_cores(up_bias, up_bias_other, core, 0)

    row_count = tokens.shape[0]
    sentences = row_count // SEQ
    head_shape = (sentences, SEQ, head_cols // HD, HD)
    attn_scale = HD ** (-0.5)
    projected = product(tokens, full_qkv)
    queries = (projected[:, :head_cols] + query_bias).astype(bf16)
    key_rows = projected[:, head_cols : 2 * head_cols].astype(bf16)
    values = (projected[:, 2 * head_cols :] + value_bias).astype(bf16)
    query_heads = queries.reshape(head_shape)
    key_heads = key_rows.reshape(head_shape)
    value_heads = values.reshape(head_shape)
    scores = (
        jnp.einsum("sqhd,skhd->shqk", query_heads, key_heads, preferred_element_type=f32) * attn_scale
    )
    row_peak = jnp.max(scores, axis=-1, keepdims=True)
    log_norm = row_peak + jnp.log(jnp.sum(jnp.exp(scores - row_peak), axis=-1, keepdims=True))
    probs = jnp.exp(scores - log_norm)
    probs_low = probs.astype(bf16)
    context = jnp.einsum("shqk,skhd->sqhd", probs_low, value_heads, preferred_element_type=f32)
    context = context.astype(bf16).reshape(row_count, head_cols)

    context_own = own_half(context, core)
    context_other = swap_cores(own_half(context, 1 - core))
    my_tokens = own_half(tokens, core)
    attended = contract_last(context_own, out_own) + contract_last(context_other, out_other)
    residual = my_tokens.astype(f32) + attended + output_bias
    hidden_first, normed_first, inv_first = norm_forward(residual, first_gain, first_shift)
    hidden_low = hidden_first.astype(bf16)
    pre_act = product(hidden_low, full_up) + full_up_bias
    activation, gelu_back = jax.vjp(exact_gelu, pre_act)
    act_low = activation.astype(bf16)
    second = hidden_first + contract_last(act_low, full_down) + down_bias
    output, normed_two, inv_two = norm_forward(second, second_gain, second_shift)
    my_sentences = sentences // 2
    pooled = jnp.mean(output.reshape(my_sentences, SEQ, D), axis=1)
    pooled_low = (
        pooled * lax.rsqrt(jnp.sum(pooled * pooled, axis=-1, keepdims=True) + norm_eps)
    ).astype(bf16)
    unit_low = gather_units(pooled_low, core, me)
    device = dp_index * 2 + core
    loss_value, grad_pooled = pair_objective(unit_low, pooled, group_sizes, sentence_order, device)
    grad_output = jnp.broadcast_to((grad_pooled / SEQ)[:, None, :], (my_sentences, SEQ, D)).reshape(
        row_count // 2, D
    )
    grad_second, grad_second_gain, grad_second_shift = norm_backward(
        grad_output, normed_two, inv_two, second_gain
    )
    grad_down_bias = jnp.sum(grad_second, axis=0)
    grad_ffn_low = grad_second.astype(bf16)
    grad_down_weight = contract_first(grad_ffn_low, act_low)
    (grad_pre,) = gelu_back(product(grad_ffn_low, full_down))
    grad_pre_low = grad_pre.astype(bf16)
    grad_up_bias = jnp.sum(grad_pre_low.astype(f32), axis=0)
    grad_up_weight = contract_first(hidden_low, grad_pre_low)
    grad_hidden = grad_second + contract_last(grad_pre_low, full_up)
    grad_residual, grad_first_gain, grad_first_shift = norm_backward(
        grad_hidden, normed_first, inv_first, first_gain
    )
    grad_output_bias = jnp.sum(grad_residual, axis=0)
    grad_attn_low = grad_residual.astype(bf16)
    grad_output_own = contract_first(grad_attn_low, context_own)
    grad_output_other = contract_first(grad_attn_low, context_other)
    grad_context_own = product(grad_attn_low, out_own).astype(bf16)
    grad_context_other = swap_cores(product(grad_attn_low, out_other).astype(bf16))
    grad_context = both_cores(grad_context_own, grad_context_other, core, 0).reshape(head_shape)

    def chip_sum(own, other):
        return own + swap_cores(other.astype(bf16)).astype(f32)

    shard_down = reduce_full(chip_sum(own_half(grad_down_weight, core, 1), own_half(grad_down_weight, 1 - core, 1)), me)
    shard_up = reduce_full(chip_sum(own_half(grad_up_weight, core, 1), own_half(grad_up_weight, 1 - core, 1)), me)
    shard_output = reduce_full(chip_sum(grad_output_own, grad_output_other), me)

    grad_values = jnp.einsum("shqk,sqhd->skhd", probs_low, grad_context, preferred_element_type=f32)
    grad_values = grad_values.astype(bf16).reshape(row_count, head_cols)
    grad_probs = jnp.einsum("sqhd,skhd->shqk", grad_context, value_heads, preferred_element_type=f32)
    grad_scores = probs * (grad_probs - jnp.sum(grad_probs * probs, axis=-1, keepdims=True))
    grad_scores_low = grad_scores.astype(bf16)
    grad_queries = jnp.einsum("shqk,skhd->sqhd", grad_scores_low, key_heads, preferred_element_type=f32)
    grad_queries = (grad_queries * attn_scale).astype(bf16).reshape(row_count, head_cols)
    grad_keys = jnp.einsum("shqk,sqhd->skhd", grad_scores_low, query_heads, preferred_element_type=f32)
    grad_keys = (grad_keys * attn_scale).astype(bf16).reshape(row_count, head_cols)
    grad_query_bias = jnp.sum(grad_queries.astype(f32), axis=0)
    grad_value_bias = jnp.sum(grad_values.astype(f32), axis=0)
    grad_qkv = jnp.concatenate([grad_queries, grad_keys, grad_values], axis=1)
    grad_qkv_weight = contract_first(tokens, grad_qkv)
    shard_qkv = reduce_full(grad_qkv_weight, me)
    shard_query = shard_qkv[:, :head_cols]
    shard_key = shard_qkv[:, head_cols : 2 * head_cols]
    shard_value = shard_qkv[:, 2 * head_cols :]
    input_terms = contract_last(grad_qkv, full_qkv)
    my_grad = grad_residual + own_half(input_terms, core) + swap_cores(
        own_half(input_terms, 1 - core).astype(bf16)
    ).astype(f32)
    grad_tokens = both_cores(my_grad, swap_cores(my_grad), core, 0)

    chip_vectors = jnp.concatenate(
        [grad_output_bias, grad_first_gain, grad_first_shift, grad_down_bias, grad_second_gain, grad_second_shift]
    )
    chip_vectors = chip_vectors + swap_cores(chip_vectors)
    up_vector = own_half(grad_up_bias, core) + swap_cores(own_half(grad_up_bias, 1 - core))
    vectors = jnp.concatenate([chip_vectors, up_vector, grad_query_bias, grad_value_bias])
    if lax.axis_size("dp") != 16:
        vectors = lax.psum(vectors, "dp")
    else:
        vectors = sum_small(vectors)
    (
        sum_output_bias, sum_first_gain, sum_first_shift, sum_down_bias, sum_second_gain, sum_second_shift,
        sum_up_bias, sum_query_bias, sum_value_bias,
    ) = jnp.split(
        vectors, [D, 2 * D, 3 * D, 4 * D, 5 * D, 6 * D, 6 * D + hidden_cols, 6 * D + hidden_cols + head_cols]
    )
    return (
        loss_value, grad_tokens, shard_query, shard_key, shard_value, shard_output, shard_up, shard_down,
        sum_query_bias, sum_value_bias, sum_output_bias, sum_first_gain, sum_first_shift, sum_up_bias,
        sum_down_bias, sum_second_gain, sum_second_shift,
    )


def solution(mesh):
    placed = (
        P("dp", None),
        P("dp", "tensor"),
        P("dp", "tensor"),
        P("dp", "tensor"),
        P("dp", "tensor"),
        P("dp", "tensor"),
        P("dp", "tensor"),
        P("tensor"),
        P("tensor"),
        P(),
        P(),
        P(),
        P("tensor"),
        P(),
        P(),
        P(),
        P(),
        P(),
    )
    return jax.shard_map(
        local,
        mesh=mesh,
        in_specs=placed,
        out_specs=(
            P(),
            P("dp", None),
            P("dp", "tensor"),
            P("dp", "tensor"),
            P("dp", "tensor"),
            P("dp", "tensor"),
            P("dp", "tensor"),
            P("dp", "tensor"),
            P("tensor"),
            P("tensor"),
            P(),
            P(),
            P(),
            P("tensor"),
            P(),
            P(),
            P(),
        ),
        check_vma=False,
    )
```

time: 1450 us -> 973 us (0.67)
  waiting for transfers between devices: 852 us -> 116 us
  Pallas kernels: 0 us -> 451 us
  blocking collectives: 251 us -> 0 us
  starting transfers between devices: 1.17 us -> 82.3 us
    pallas_call x0 -> x8, Pallas kernels: none -> 451 us  [the longest x4 231 us: place_rows(): pl.pallas_call(functools.partial(place_kernel, ordered(first, second), ro...]
    unnamed x16 -> x0, waiting for transfers between devices: 382 us -> none
    reduce_scatter x3 -> x0, waiting for transfers between devices: 285 us -> none  [the longest x1 143 us: local(): lax.psum_scatter(grad_up_weight, 'dp', scatter_dimension=0, tiled=True)]
    all_gather x4 -> x0, blocking collectives: 173 us -> none  [the longest x1 48.6 us: local(): lax.all_gather(query_weight, 'dp', axis=0, tiled=True)]
    all_gather x3 -> x0, waiting for transfers between devices: 123 us -> none  [the longest x1 58.4 us: local(): gathered = lax.all_gather(pooled, 'dp', axis=0, tiled=True)]
    ppermute x0 -> x67, waiting for transfers between devices: none -> 116 us  [the longest x54 114 us: swap_chips(): return lax.ppermute(array, 'dp', [(i, i ^ mask) for i in range(count)])]
    ppermute x0 -> x67, starting transfers between devices: none -> 82.3 us  [the longest x54 80.1 us: swap_chips(): return lax.ppermute(array, 'dp', [(i, i ^ mask) for i in range(count)])]
    psum x1 -> x0, blocking collectives: 77.8 us -> none  [local(): lax.psum((grad_query_bias, grad_value_bias, grad_output_bias, grad_first_...]
  transfers between devices with their start and end apart: 13 -> 67, of which waited for: 11 -> 24; matrix products, arithmetic and copies ran while one was open for 7% -> 14% of each run, Pallas kernels for 0% -> 45%
where the time goes in v1:
time: 973 us; the launch traced here: 970 us
  Pallas kernels  451 us (46%)
  matrix products  173 us (18%)
  waiting for transfers between devices  116 us (12%)
  local copies, waits for them, and re-layouts  91.1 us (9%)
  starting transfers between devices  82.3 us (8%)
  other arithmetic  53 us (5%)
    pallas_call x4, Pallas kernels, place_rows(): pl.pallas_call(functools.partial(place_kernel, ordered(first, second), ro...  231 us
    pallas_call x4, Pallas kernels, split_rows(): pl.pallas_call(functools.partial(split_kernel, ordered(second, first), ro...  219 us
    dot_general x20, matrix products, contract(): lax.dot_general(left, right, (((left_dim,), (right_dim,)), ((), ())), pre...  141 us
    ppermute x54, waiting for transfers between devices, swap_chips(): return lax.ppermute(array, 'dp', [(i, i ^ mask) for i in range(count)])  114 us
    ppermute x54, starting transfers between devices, swap_chips(): return lax.ppermute(array, 'dp', [(i, i ^ mask) for i in range(count)])  80.1 us
  transfers between devices with their start and end apart: 67, of which 24 were waited for; matrix products, arithmetic and copies ran while one was open for 14% of the time, Pallas kernels for 45%

profile of v1, /device:TPU:0, one launch (start us, length us, event | category | flops | bytes accessed | tf_op | source)
XLA Modules:
  0.0 969.8 jit_solution(7626559599322017029)
XLA Ops:
  2.4 5.1 collective-permute-start.8
  17.7 5.6 collective-permute-done.15
  24.6 14.3 %collective-permute-done.16 = bf16[48,1536]{1,0:T(8,128)(2,1)S(1)} collective-permute-done((bf16[48,1536]{1,0:T(8,128)(2,1)}, bf16[48,1536]{1,0:T(8,128)(2,1)S(1)}, u32[]{:S(2)}, u32[]{:S(2)}) %collective-permute-start.16) | collective-permute-done | bytes 147488 | tf_op jit(solution)/shard_map/ppermute | solution.py:51
  41.4 4.7 collective-permute-done.17
  48.2 2.9 collective-permute-done
  58.5 18.3 %collective-permute-done.3.refs_1_ = bf16[192,1152]{1,0:T(8,128)(2,1)S(1)} collective-permute-done((bf16[192,1152]{1,0:T(8,128)(2,1)S(1)}, bf16[192,1152]{1,0:T(8,128)(2,1)S(1)}, u32[]{:S(2)}, u32[]{:S(2)}) %collective-permute-start.3) | collective-permute-done | bytes 442400 | tf_op jit(solution)/shard_map/ppermute | solution.py:51
  79.8 7.5 collective-permute-done.5.refs_3_
  88.2 54.9 %place_rows.4 = bf16[768,1152]{1,0:T(8,128)(2,1)} custom-call(s32[1]{0:T(128)} %bitcast.2.me_ref, bf16[192,1152]{1,0:T(8,128)(2,1)} %copy-done.29, bf16[192,1152]{1,0:T(8,128)(2,1)} %copy-done.39, bf16[192,1152]{1,0:T(8,128)(2,1)} %copy-done.40, bf16[192,1152]{1,0:T(8,128)(2,1)} %copy-done.41), custom_call_target="tpu_custom_call" | custom-call | tf_op jit(solution)/shard_map/place_rows/pallas_call | solution.py:101
  145.3 10.0 %convolution_bitcast_fusion = f32[2048,1152]{0,1:T(8,128)} fusion(bf16[768,1152]{1,0:T(8,128)(2,1)} %place_rows.4, bf16[2048,768]{1,0:T(8,128)(2,1)} %param.20), kind=kOutput, calls=%fused_computation.20 | convolution fusion | flops 3623878656 | bytes 14352384 | tf_op jit(solution)/shard_map/dot_general | solution.py:28
  155.3 72.7 %place_rows.6 = bf16[768,1536]{1,0:T(8,128)(2,1)} custom-call(s32[1]{0:T(128)} %bitcast.2.me_ref, bf16[192,1536]{1,0:T(8,128)(2,1)} %copy-done.30, bf16[192,1536]{1,0:T(8,128)(2,1)} %collective-permute-done.18.refs_1_, bf16[192,1536]{1,0:T(8,128)(2,1)} %collective-permute-done.19.refs_2_, bf16[192,1536]{1,0:T(8,128)(2,1)} %collective-permute-done.20.refs_3_), custom_call_target="tpu_custom_call" | custom-call | tf_op jit(solution)/shard_map/place_rows/pallas_call | solution.py:101
  229.2 90.6 %place_rows.5 = bf16[768,1920]{1,0:T(8,128)(2,1)} custom-call(s32[1]{0:T(128)} %bitcast.2.me_ref, bf16[192,1920]{1,0:T(8,128)(2,1)} %copy-done.22, bf16[192,1920]{1,0:T(8,128)(2,1)} %copy-done.35, bf16[192,1920]{1,0:T(8,128)(2,1)} %copy-done.36, bf16[192,1920]{1,0:T(8,128)(2,1)} %collective-permute-done.11.refs_3_), custom_call_target="tpu_custom_call" | custom-call | tf_op jit(solution)/shard_map/place_rows/pallas_call | solution.py:101
  320.4 4.4 fusion.15
  324.8 3.2 slice.172
  328.0 4.2 reshape.230
  332.2 3.9 copy.73
  336.1 6.0 reshape.232
  342.1 5.0 copy.67
  347.1 5.9 reshape.231
  353.0 6.6 multiply_reduce_fusion.1
  366.2 3.4 reshape.233
  370.9 2.8 broadcast_select_fusion.1
  373.8 2.8 fusion.45
  380.2 2.6 broadcast_select_fusion.3
  382.9 48.1 %multiply_convert_fusion = (bf16[1024,3072]{1,0:T(8,128)(2,1)S(1)}, f32[1024,3072]{1,0:T(8,128)}, f32[1024,3072]{1,0:T(8,128)}) fusion(f32[3072]{0:T(1024)S(1)} %pad_maximum_fusion.17, bf16[768,1536]{1,0:T(8,128)(2,1)S(1)} %get-tuple-element.104, bf16[768,1536]{1,0:T(8,128)(2,1)S(1)} %get-tuple-element.103, f32[1024,768]{1,0:T(8,128)S(1)} %get-tuple-element.145, ...), kind=kOutput, calls=%fused_computation.6 | convolution fusion | flops 5052825600 | bytes 39348224 | tf_op jit(solution)/shard_map/dot_general | solution.py:28
  431.1 5.5 fusion.76
  452.9 13.2 %place_rows.7 = bf16[256,768]{1,0:T(8,128)(2,1)} custom-call(s32[1]{0:T(128)} %bitcast.2.me_ref, bf16[64,768]{1,0:T(8,128)(2,1)} %copy-done.42, bf16[64,768]{1,0:T(8,128)(2,1)} %copy-done.44, bf16[64,768]{1,0:T(8,128)(2,1)} %copy-done.45, bf16[64,768]{1,0:T(8,128)(2,1)} %copy-done.46), custom_call_target="tpu_custom_call" | custom-call | tf_op jit(solution)/shard_map/place_rows/pallas_call | solution.py:101
  483.7 18.1 %convert_reduce_fusion = (f32[3072]{0:T(1024)S(1)}, bf16[1024,3072]{1,0:T(8,128)(2,1)}) fusion(f32[1024,3072]{1,0:T(8,128)} %get-tuple-element.98, bf16[768,1536]{1,0:T(8,128)(2,1)} %copy-done.25, bf16[768,1536]{1,0:T(8,128)(2,1)} %copy-done.24, f32[1024,768]{1,0:T(8,128)} %get-tuple-element.91, f32[1024,3072]{1,0:T(8,128)} %get-tuple-element.146, ...), kind=kOutput, calls=%fused_computation.4 | convolution fusion | flops 4895536128 | bytes 39346176 | tf_op jit(solution)/shard_map/dot_general | solution.py:28
  501.9 11.2 %multiply_reduce_fusion.2 = (f32[768]{0:T(1024)S(1)}, f32[1024]{0:T(1024)S(1)}, f32[1024]{0:T(1024)S(1)}, f32[768]{0:T(1024)S(1)}, f32[1024,768]{1,0:T(8,128)S(1)}) fusion(f32[1024,768]{1,0:T(8,128)S(1)} %copy-done.2, f32[1024]{0:T(1024)S(1)} %add_rsqrt_fusion.1, f32[1024]{0:T(1024)S(1)} %broadcast_multiply_fusion.5, f32[768]{0:T(1024)S(1)} %copy-done.47, ...), kind=kOutput, calls=%fused_computation.55 | convolution fusion | flops 4849135616 | bytes 20472832 | tf_op jit(solution)/shard_map/dot_general | solution.py:28
  513.1 5.6 fusion.60
  518.7 9.6 fusion.38
  530.1 4.0 convolution_convert_fusion.1
  541.5 19.1 %split_rows.5 = (bf16[192,384]{1,0:T(8,128)(2,1)}, bf16[192,384]{1,0:T(8,128)(2,1)}, bf16[192,384]{1,0:T(8,128)(2,1)}, bf16[192,384]{1,0:T(8,128)(2,1)}) custom-call(s32[1]{0:T(128)} %bitcast.2.me_ref, bf16[768,384]{1,0:T(8,128)(2,1)} %add_convert_fusion.5.full), custom_call_target="tpu_custom_call" | custom-call | tf_op jit(solution)/shard_map/split_rows/pallas_call | solution.py:129
  565.0 3.4 collective-permute-done.41
  572.1 2.9 collective-permute-start.44
  583.9 6.0 reshape.263
  589.9 9.7 %multiply_reduce_fusion = (f32[32,6,64]{2,1,0:T(8,128)S(1)}, f32[32,6,64,64]{2,3,1,0:T(8,128)}) fusion(f32[32,6,64,64]{2,3,1,0:T(8,128)} %copy-done, f32[32,6,64]{2,1,0:T(8,128)S(1)} %copy-done.20, bf16[32,64,6,64]{3,1,2,0:T(8,128)(2,1)} %copy-done.6, bf16[32,64,6,64]{3,2,1,0:T(8,128)(2,1)} %reshape.263), kind=kOutput, calls=%fused_computation.27 | convolution fusion | flops 103796736 | bytes 9535488 | tf_op jit(solution)/shard_map/sqhd,skhd->shqk/dot_general | solution.py:370
  599.7 6.8 multiply_convert_fusion.3
  606.5 5.2 convert_reduce_fusion.2
  611.7 5.3 fusion.14
  617.0 3.2 convert_reduce_fusion.1
  623.9 4.2 copy.76
  628.1 3.4 reshape.238
  631.5 2.7 constant_dynamic-update-slice_fusion.11
  634.2 4.4 copy.80
  638.6 3.4 reshape.239
  642.0 4.2 copy.82
  646.3 3.4 reshape.240
  649.7 2.9 constant_dynamic-update-slice_fusion.10
  653.8 8.0 fusion.20.full
  661.8 54.9 %split_rows.4 = (bf16[192,1152]{1,0:T(8,128)(2,1)}, bf16[192,1152]{1,0:T(8,128)(2,1)}, bf16[192,1152]{1,0:T(8,128)(2,1)}, bf16[192,1152]{1,0:T(8,128)(2,1)}) custom-call(s32[1]{0:T(128)} %bitcast.2.me_ref, bf16[768,1152]{1,0:T(8,128)(2,1)} %fusion.20.full), custom_call_target="tpu_custom_call" | custom-call | tf_op jit(solution)/shard_map/split_rows/pallas_call | solution.py:129
  721.2 6.6 fusion.77
  729.5 9.3 collective-permute-done.65
  739.5 3.2 collective-permute-done.64
  747.2 3.7 collective-permute-done.37
  750.9 4.8 collective-permute-start.35
  762.5 72.7 %split_rows.6 = (bf16[192,1536]{1,0:T(8,128)(2,1)}, bf16[192,1536]{1,0:T(8,128)(2,1)}, bf16[192,1536]{1,0:T(8,128)(2,1)}, bf16[192,1536]{1,0:T(8,128)(2,1)}) custom-call(s32[1]{0:T(128)} %bitcast.2.me_ref, bf16[768,1536]{1,0:T(8,128)(2,1)} %add_convert_fusion.2.full), custom_call_target="tpu_custom_call" | custom-call | tf_op jit(solution)/shard_map/split_rows/pallas_call | solution.py:129
  838.8 5.2 add_convert_fusion.1.full
  844.0 72.7 %split_rows.7 = (bf16[192,1536]{1,0:T(8,128)(2,1)}, bf16[192,1536]{1,0:T(8,128)(2,1)}, bf16[192,1536]{1,0:T(8,128)(2,1)}, bf16[192,1536]{1,0:T(8,128)(2,1)}) custom-call(s32[1]{0:T(128)} %bitcast.2.me_ref, bf16[768,1536]{1,0:T(8,128)(2,1)} %add_convert_fusion.1.full), custom_call_target="tpu_custom_call" | custom-call | tf_op jit(solution)/shard_map/split_rows/pallas_call | solution.py:129
  922.2 2.7 collective-permute-start.51
  925.0 9.3 collective-permute-done.55
  936.7 8.8 collective-permute-done.54
  952.7 4.6 collective-permute-done.58
  957.3 5.0 collective-permute-done.57
  965.4 3.1 pad_maximum_fusion
  (349 shorter events, 148.1 us)
Async XLA Ops:
  2.4 50.9 %collective-permute-start.8 = (bf16[48,1920]{1,0:T(8,128)(2,1)S(1)}, bf16[48,1920]{1,0:T(8,128)(2,1)S(1)}, u32[]{:S(2)}, u32[]{:S(2)}) collective-permute-start(bf16[48,1920]{1,0:T(8,128)(2,1)S(1)} %constant_dynamic-update-slice_fusion.3), channel_id=1, source_target_pairs={{0,24},{2,26},{4,28},{6,30},{8,16},{10,18},{12,20},{14,22},{16,8},... | collective-permute-start | bytes 552968 | tf_op jit(solution)/shard_map/ppermute | solution.py:51
  7.5 47.3 %collective-permute-start.7 = (bf16[48,1920]{1,0:T(8,128)(2,1)S(1)}, bf16[48,1920]{1,0:T(8,128)(2,1)S(1)}, u32[]{:S(2)}, u32[]{:S(2)}) collective-permute-start(bf16[48,1920]{1,0:T(8,128)(2,1)S(1)} %constant_dynamic-update-slice_fusion.3), channel_id=1, source_target_pairs={{0,16},{2,18},{4,20},{6,22},{8,24},{10,26},{12,28},{14,30},{16,0},... | collective-permute-start | bytes 552968 | tf_op jit(solution)/shard_map/ppermute | solution.py:51
  9.8 37.4 %collective-permute-start.2 = (bf16[48,1152]{1,0:T(8,128)(2,1)S(1)}, bf16[48,1152]{1,0:T(8,128)(2,1)S(1)}, u32[]{:S(2)}, u32[]{:S(2)}) collective-permute-start(bf16[48,1152]{1,0:T(8,128)(2,1)S(1)} %constant_dynamic-update-slice_fusion), channel_id=1, source_target_pairs={{0,24},{2,26},{4,28},{6,30},{8,16},{10,18},{12,20},{14,22},{16,8},... | collective-permute-start | bytes 331784 | tf_op jit(solution)/shard_map/ppermute | solution.py:51
  11.7 36.5 %collective-permute-start.1 = (bf16[48,1152]{1,0:T(8,128)(2,1)S(1)}, bf16[48,1152]{1,0:T(8,128)(2,1)S(1)}, u32[]{:S(2)}, u32[]{:S(2)}) collective-permute-start(bf16[48,1152]{1,0:T(8,128)(2,1)S(1)} %constant_dynamic-update-slice_fusion), channel_id=1, source_target_pairs={{0,16},{2,18},{4,20},{6,22},{8,24},{10,26},{12,28},{14,30},{16,0},... | collective-permute-start | bytes 331784 | tf_op jit(solution)/shard_map/ppermute | solution.py:51
  12.8 10.6 %collective-permute-start.15 = (bf16[48,1536]{1,0:T(8,128)(2,1)}, bf16[48,1536]{1,0:T(8,128)(2,1)S(1)}, u32[]{:S(2)}, u32[]{:S(2)}) collective-permute-start(bf16[48,1536]{1,0:T(8,128)(2,1)} %param.26), channel_id=1, source_target_pairs={{0,8},{2,10},{4,12},{6,14},{8,0},{10,2},{12,4},{14,6},{16,24},{18,... | collective-permute-start | bytes 442376 | tf_op jit(solution)/shard_map/ppermute | solution.py:51
  23.4 15.5 %collective-permute-start.16 = (bf16[48,1536]{1,0:T(8,128)(2,1)}, bf16[48,1536]{1,0:T(8,128)(2,1)S(1)}, u32[]{:S(2)}, u32[]{:S(2)}) collective-permute-start(bf16[48,1536]{1,0:T(8,128)(2,1)} %param.26), channel_id=1, source_target_pairs={{0,16},{2,18},{4,20},{6,22},{8,24},{10,26},{12,28},{14,30},{16,0},... | collective-permute-start | bytes 442376 | tf_op jit(solution)/shard_map/ppermute | solution.py:51
  38.9 7.2 collective-permute-start.17
  46.1 5.0 collective-permute-start
  47.2 9.7 %collective-permute-start.6 = (bf16[48,1920]{1,0:T(8,128)(2,1)S(1)}, bf16[48,1920]{1,0:T(8,128)(2,1)S(1)}, u32[]{:S(2)}, u32[]{:S(2)}) collective-permute-start(bf16[48,1920]{1,0:T(8,128)(2,1)S(1)} %constant_dynamic-update-slice_fusion.3), channel_id=1, source_target_pairs={{0,8},{2,10},{4,12},{6,14},{8,0},{10,2},{12,4},{14,6},{16,24},{18,... | collective-permute-start | bytes 552968 | tf_op jit(solution)/shard_map/ppermute | solution.py:51
  48.2 4.4 collective-permute-start.14
  51.1 91.9 %collective-permute-start.18 = (bf16[192,1536]{1,0:T(8,128)(2,1)S(1)}, bf16[192,1536]{1,0:T(8,128)(2,1)}, u32[]{:S(2)}, u32[]{:S(2)}) collective-permute-start(bf16[192,1536]{1,0:T(8,128)(2,1)S(1)} %constant_dynamic-update-slice_fusion.5.refs_0_), channel_id=1, source_target_pairs={{0,2},{2,0},{4,6},{6,4},{8,10},{10,8},{12,14},{14,12},{16,18},{18,... | collective-permute-start | bytes 1769480 | tf_op jit(solution)/shard_map/ppermute | solution.py:51
  52.7 24.2 %collective-permute-start.3 = (bf16[192,1152]{1,0:T(8,128)(2,1)S(1)}, bf16[192,1152]{1,0:T(8,128)(2,1)S(1)}, u32[]{:S(2)}, u32[]{:S(2)}) collective-permute-start(bf16[192,1152]{1,0:T(8,128)(2,1)S(1)} %pad_maximum_fusion.14.refs_0_), channel_id=1, source_target_pairs={{0,2},{2,0},{4,6},{6,4},{8,10},{10,8},{12,14},{14,12},{16,18},{18,... | collective-permute-start | bytes 1327112 | tf_op jit(solution)/shard_map/ppermute | solution.py:51
  53.3 26.0 %collective-permute-start.4 = (bf16[192,1152]{1,0:T(8,128)(2,1)S(1)}, bf16[192,1152]{1,0:T(8,128)(2,1)S(1)}, u32[]{:S(2)}, u32[]{:S(2)}) collective-permute-start(bf16[192,1152]{1,0:T(8,128)(2,1)S(1)} %pad_maximum_fusion.14.refs_0_), channel_id=1, source_target_pairs={{0,4},{2,6},{4,0},{6,2},{8,12},{10,14},{12,8},{14,10},{16,20},{18,... | collective-permute-start | bytes 1327112 | tf_op jit(solution)/shard_map/ppermute | solution.py:51
  54.8 32.6 %collective-permute-start.5 = (bf16[192,1152]{1,0:T(8,128)(2,1)S(1)}, bf16[192,1152]{1,0:T(8,128)(2,1)S(1)}, u32[]{:S(2)}, u32[]{:S(2)}) collective-permute-start(bf16[192,1152]{1,0:T(8,128)(2,1)S(1)} %pad_maximum_fusion.14.refs_0_), channel_id=1, source_target_pairs={{0,6},{2,4},{4,2},{6,0},{8,14},{10,12},{12,10},{14,8},{16,22},{18,... | collective-permute-start | bytes 1327112 | tf_op jit(solution)/shard_map/ppermute | solution.py:51
  56.9 98.4 %collective-permute-start.19 = (bf16[192,1536]{1,0:T(8,128)(2,1)S(1)}, bf16[192,1536]{1,0:T(8,128)(2,1)}, u32[]{:S(2)}, u32[]{:S(2)}) collective-permute-start(bf16[192,1536]{1,0:T(8,128)(2,1)S(1)} %constant_dynamic-update-slice_fusion.5.refs_0_), channel_id=1, source_target_pairs={{0,4},{2,6},{4,0},{6,2},{8,12},{10,14},{12,8},{14,10},{16,20},{18,... | collective-permute-start | bytes 1769480 | tf_op jit(solution)/shard_map/ppermute | solution.py:51
  76.9 78.4 %collective-permute-start.20 = (bf16[192,1536]{1,0:T(8,128)(2,1)S(1)}, bf16[192,1536]{1,0:T(8,128)(2,1)}, u32[]{:S(2)}, u32[]{:S(2)}) collective-permute-start(bf16[192,1536]{1,0:T(8,128)(2,1)S(1)} %constant_dynamic-update-slice_fusion.5.refs_0_), channel_id=1, source_target_pairs={{0,6},{2,4},{4,2},{6,0},{8,14},{10,12},{12,10},{14,8},{16,22},{18,... | collective-permute-start | bytes 1769480 | tf_op jit(solution)/shard_map/ppermute | solution.py:51
  79.3 148.8 %collective-permute-start.9 = (bf16[192,1920]{1,0:T(8,128)(2,1)S(1)}, bf16[192,1920]{1,0:T(8,128)(2,1)S(1)}, u32[]{:S(2)}, u32[]{:S(2)}) collective-permute-start(bf16[192,1920]{1,0:T(8,128)(2,1)S(1)} %pad_maximum_fusion.13.refs_0_), channel_id=1, source_target_pairs={{0,2},{2,0},{4,6},{6,4},{8,10},{10,8},{12,14},{14,12},{16,18},{18,... | collective-permute-start | bytes 2211848 | tf_op jit(solution)/shard_map/ppermute | solution.py:51
  87.4 140.8 %collective-permute-start.10 = (bf16[192,1920]{1,0:T(8,128)(2,1)S(1)}, bf16[192,1920]{1,0:T(8,128)(2,1)S(1)}, u32[]{:S(2)}, u32[]{:S(2)}) collective-permute-start(bf16[192,1920]{1,0:T(8,128)(2,1)S(1)} %pad_maximum_fusion.13.refs_0_), channel_id=1, source_target_pairs={{0,4},{2,6},{4,0},{6,2},{8,12},{10,14},{12,8},{14,10},{16,20},{18,... | collective-permute-start | bytes 2211848 | tf_op jit(solution)/shard_map/ppermute | solution.py:51
  143.1 85.1 %collective-permute-start.11 = (bf16[192,1920]{1,0:T(8,128)(2,1)S(1)}, bf16[192,1920]{1,0:T(8,128)(2,1)}, u32[]{:S(2)}, u32[]{:S(2)}) collective-permute-start(bf16[192,1920]{1,0:T(8,128)(2,1)S(1)} %pad_maximum_fusion.13.refs_0_), channel_id=1, source_target_pairs={{0,6},{2,4},{4,2},{6,0},{8,14},{10,12},{12,10},{14,8},{16,22},{18,... | collective-permute-start | bytes 2211848 | tf_op jit(solution)/shard_map/ppermute | solution.py:51
  228.0 142.8 %collective-permute-start.21 = (bf16[768,1536]{1,0:T(8,128)(2,1)}, bf16[768,1536]{1,0:T(8,128)(2,1)}, u32[]{:S(2)}, u32[]{:S(2)}) collective-permute-start(bf16[768,1536]{1,0:T(8,128)(2,1)} %place_rows.6), channel_id=1, source_target_pairs={{0,1},{1,0},{2,3},{3,2},{4,5},{5,4},{6,7},{7,6},{8,9},{9,8},{10,11... | collective-permute-start | bytes 7077896 | tf_op jit(solution)/shard_map/ppermute | solution.py:46
  319.8 54.0 %collective-permute-start.13 = (bf16[768,1920]{1,0:T(8,128)(2,1)}, bf16[768,1920]{1,0:T(8,128)(2,1)}, u32[]{:S(2)}, u32[]{:S(2)}) collective-permute-start(bf16[768,1920]{1,0:T(8,128)(2,1)} %place_rows.5), channel_id=1, source_target_pairs={{0,1},{1,0},{2,3},{3,2},{4,5},{5,4},{6,7},{7,6},{8,9},{9,8},{10,11... | collective-permute-start | bytes 8847368 | tf_op jit(solution)/shard_map/ppermute | solution.py:46
  438.4 5.7 collective-permute-start.24
  440.6 4.7 collective-permute-start.23
  440.7 4.6 collective-permute-start.22
  445.4 5.5 collective-permute-start.25
  445.9 5.3 collective-permute-start.26
  446.7 5.5 collective-permute-start.27
  534.1 46.5 %collective-permute-start.29 = (bf16[1024,384]{1,0:T(8,128)(2,1)}, bf16[1024,384]{1,0:T(8,128)(2,1)S(1)}, u32[]{:S(2)}, u32[]{:S(2)}) collective-permute-start(bf16[1024,384]{1,0:T(8,128)(2,1)} %convolution_convert_fusion.1), channel_id=1, source_target_pairs={{0,1},{1,0},{2,3},{3,2},{4,5},{5,4},{6,7},{7,6},{8,9},{9,8},{10,11... | collective-permute-start | bytes 2359304 | tf_op jit(solution)/shard_map/ppermute | solution.py:46
  535.3 5.2 collective-permute-start.38
  537.5 37.5 %collective-permute-start.60 = (f32[1536]{0:T(1024)S(1)}, f32[1536]{0:T(1024)S(1)}, u32[]{:S(2)}, u32[]{:S(2)}) collective-permute-start(f32[1536]{0:T(1024)S(1)} %dynamic_slice.50), channel_id=1, source_target_pairs={{0,1},{1,0},{2,3},{3,2},{4,5},{5,4},{6,7},{7,6},{8,9},{9,8},{10,11... | collective-permute-start | bytes 18440 | tf_op jit(solution)/shard_map/ppermute | solution.py:46
  560.6 7.9 collective-permute-start.41
  562.8 8.2 collective-permute-start.40
  564.4 6.7 collective-permute-start.39
  568.5 8.1 collective-permute-start.59
  572.1 6.1 collective-permute-start.44
  575.0 4.9 collective-permute-start.43
  575.0 4.9 collective-permute-start.42
  620.3 98.9 %collective-permute-start.62 = (f32[6912]{0:T(1024)S(1)}, f32[6912]{0:T(1024)S(1)}, u32[]{:S(2)}, u32[]{:S(2)}) collective-permute-start(f32[6912]{0:T(1024)S(1)} %pad_maximum_fusion.16), channel_id=1, source_target_pairs={{0,16},{2,18},{4,20},{6,22},{8,24},{10,26},{12,28},{14,30},{16,0},... | collective-permute-start | bytes 82952 | tf_op jit(solution)/shard_map/ppermute | solution.py:51
  622.4 97.8 %collective-permute-start.63 = (f32[6912]{0:T(1024)S(1)}, f32[6912]{0:T(1024)S(1)}, u32[]{:S(2)}, u32[]{:S(2)}) collective-permute-start(f32[6912]{0:T(1024)S(1)} %pad_maximum_fusion.16), channel_id=1, source_target_pairs={{0,24},{2,26},{4,28},{6,30},{8,16},{10,18},{12,20},{14,22},{16,8},... | collective-permute-start | bytes 82952 | tf_op jit(solution)/shard_map/ppermute | solution.py:51
  623.3 96.9 %collective-permute-start.61 = (f32[6912]{0:T(1024)S(1)}, f32[6912]{0:T(1024)S(1)}, u32[]{:S(2)}, u32[]{:S(2)}) collective-permute-start(f32[6912]{0:T(1024)S(1)} %pad_maximum_fusion.16), channel_id=1, source_target_pairs={{0,8},{2,10},{4,12},{6,14},{8,0},{10,2},{12,4},{14,6},{16,24},{18,... | collective-permute-start | bytes 82952 | tf_op jit(solution)/shard_map/ppermute | solution.py:51
  716.7 26.0 %collective-permute-start.34 = (bf16[192,1152]{1,0:T(8,128)(2,1)}, bf16[192,1152]{1,0:T(8,128)(2,1)S(1)}, u32[]{:S(2)}, u32[]{:S(2)}) collective-permute-start(bf16[192,1152]{1,0:T(8,128)(2,1)} %get-tuple-element.64), channel_id=1, source_target_pairs={{0,6},{2,4},{4,2},{6,0},{8,14},{10,12},{12,10},{14,8},{16,22},{18,... | collective-permute-start | bytes 1327112 | tf_op jit(solution)/shard_map/ppermute | solution.py:51
  718.5 24.8 %collective-permute-start.33 = (bf16[192,1152]{1,0:T(8,128)(2,1)}, bf16[192,1152]{1,0:T(8,128)(2,1)S(1)}, u32[]{:S(2)}, u32[]{:S(2)}) collective-permute-start(bf16[192,1152]{1,0:T(8,128)(2,1)} %get-tuple-element.63), channel_id=1, source_target_pairs={{0,4},{2,6},{4,0},{6,2},{8,12},{10,14},{12,8},{14,10},{16,20},{18,... | collective-permute-start | bytes 1327112 | tf_op jit(solution)/shard_map/ppermute | solution.py:51
  719.2 24.0 %collective-permute-start.32 = (bf16[192,1152]{1,0:T(8,128)(2,1)}, bf16[192,1152]{1,0:T(8,128)(2,1)S(1)}, u32[]{:S(2)}, u32[]{:S(2)}) collective-permute-start(bf16[192,1152]{1,0:T(8,128)(2,1)} %get-tuple-element.62), channel_id=1, source_target_pairs={{0,2},{2,0},{4,6},{6,4},{8,10},{10,8},{12,14},{14,12},{16,18},{18,... | collective-permute-start | bytes 1327112 | tf_op jit(solution)/shard_map/ppermute | solution.py:51
  720.2 18.5 %collective-permute-start.65 = (f32[6912]{0:T(1024)S(1)}, f32[6912]{0:T(1024)S(1)}, u32[]{:S(2)}, u32[]{:S(2)}) collective-permute-start(f32[6912]{0:T(1024)S(1)} %add_add_fusion.3), channel_id=1, source_target_pairs={{0,4},{2,6},{4,0},{6,2},{8,12},{10,14},{12,8},{14,10},{16,20},{18,... | collective-permute-start | bytes 82952 | tf_op jit(solution)/shard_map/ppermute | solution.py:51
  727.8 11.6 %collective-permute-start.66 = (f32[6912]{0:T(1024)S(1)}, f32[6912]{0:T(1024)S(1)}, u32[]{:S(2)}, u32[]{:S(2)}) collective-permute-start(f32[6912]{0:T(1024)S(1)} %add_add_fusion.3), channel_id=1, source_target_pairs={{0,6},{2,4},{4,2},{6,0},{8,14},{10,12},{12,10},{14,8},{16,22},{18,... | collective-permute-start | bytes 82952 | tf_op jit(solution)/shard_map/ppermute | solution.py:51
  739.4 20.9 %collective-permute-start.45 = (bf16[768,1536]{1,0:T(8,128)(2,1)S(1)}, bf16[768,1536]{1,0:T(8,128)(2,1)S(1)}, u32[]{:S(2)}, u32[]{:S(2)}) collective-permute-start(bf16[768,1536]{1,0:T(8,128)(2,1)S(1)} %copy-done.23), channel_id=1, source_target_pairs={{0,1},{1,0},{2,3},{3,2},{4,5},{5,4},{6,7},{7,6},{8,9},{9,8},{10,11... | collective-permute-start | bytes 7077896 | tf_op jit(solution)/shard_map/ppermute | solution.py:46
  742.6 96.2 %collective-permute-start.52 = (bf16[768,1536]{1,0:T(8,128)(2,1)}, bf16[768,1536]{1,0:T(8,128)(2,1)}, u32[]{:S(2)}, u32[]{:S(2)}) collective-permute-start(bf16[768,1536]{1,0:T(8,128)(2,1)} %dynamic-slice_convert_fusion), channel_id=1, source_target_pairs={{0,1},{1,0},{2,3},{3,2},{4,5},{5,4},{6,7},{7,6},{8,9},{9,8},{10,11... | collective-permute-start | bytes 7077896 | tf_op jit(solution)/shard_map/ppermute | solution.py:46
  742.7 17.0 %collective-permute-start.30 = (bf16[1024,768]{1,0:T(8,128)(2,1)S(1)}, bf16[1024,768]{1,0:T(8,128)(2,1)S(1)}, u32[]{:S(2)}, u32[]{:S(2)}) collective-permute-start(bf16[1024,768]{1,0:T(8,128)(2,1)S(1)} %dynamic-slice_convert_fusion.2), channel_id=1, source_target_pairs={{0,1},{1,0},{2,3},{3,2},{4,5},{5,4},{6,7},{7,6},{8,9},{9,8},{10,11... | collective-permute-start | bytes 4718600 | tf_op jit(solution)/shard_map/ppermute | solution.py:46
  743.5 7.4 collective-permute-start.37
  746.5 10.5 %collective-permute-start.36 = (bf16[48,1152]{1,0:T(8,128)(2,1)S(1)}, bf16[48,1152]{1,0:T(8,128)(2,1)S(1)}, u32[]{:S(2)}, u32[]{:S(2)}) collective-permute-start(bf16[48,1152]{1,0:T(8,128)(2,1)S(1)} %get-tuple-element.119), channel_id=1, source_target_pairs={{0,16},{2,18},{4,20},{6,22},{8,24},{10,26},{12,28},{14,30},{16,0},... | collective-permute-start | bytes 331784 | tf_op jit(solution)/shard_map/ppermute | solution.py:51
  750.9 8.0 collective-permute-start.35
  760.2 202.8 %collective-permute-start.31 = (f32[1024,768]{1,0:T(8,128)S(1)}, f32[1024,768]{1,0:T(8,128)}, u32[]{:S(2)}, u32[]{:S(2)}) collective-permute-start(f32[1024,768]{1,0:T(8,128)S(1)} %convert_add_fusion), channel_id=1, source_target_pairs={{0,1},{1,0},{2,3},{3,2},{4,5},{5,4},{6,7},{7,6},{8,9},{9,8},{10,11... | collective-permute-start | bytes 9437192 | tf_op jit(solution)/shard_map/ppermute | solution.py:46
  835.3 83.5 %collective-permute-start.48 = (bf16[192,1536]{1,0:T(8,128)(2,1)}, bf16[192,1536]{1,0:T(8,128)(2,1)}, u32[]{:S(2)}, u32[]{:S(2)}) collective-permute-start(bf16[192,1536]{1,0:T(8,128)(2,1)} %get-tuple-element.72), channel_id=1, source_target_pairs={{0,6},{2,4},{4,2},{6,0},{8,14},{10,12},{12,10},{14,8},{16,22},{18,... | collective-permute-start | bytes 1769480 | tf_op jit(solution)/shard_map/ppermute | solution.py:51
  837.2 81.5 %collective-permute-start.47 = (bf16[192,1536]{1,0:T(8,128)(2,1)}, bf16[192,1536]{1,0:T(8,128)(2,1)}, u32[]{:S(2)}, u32[]{:S(2)}) collective-permute-start(bf16[192,1536]{1,0:T(8,128)(2,1)} %get-tuple-element.71), channel_id=1, source_target_pairs={{0,4},{2,6},{4,0},{6,2},{8,12},{10,14},{12,8},{14,10},{16,20},{18,... | collective-permute-start | bytes 1769480 | tf_op jit(solution)/shard_map/ppermute | solution.py:51
  837.2 83.1 %collective-permute-start.46 = (bf16[192,1536]{1,0:T(8,128)(2,1)}, bf16[192,1536]{1,0:T(8,128)(2,1)}, u32[]{:S(2)}, u32[]{:S(2)}) collective-permute-start(bf16[192,1536]{1,0:T(8,128)(2,1)} %get-tuple-element.70), channel_id=1, source_target_pairs={{0,2},{2,0},{4,6},{6,4},{8,10},{10,8},{12,14},{14,12},{16,18},{18,... | collective-permute-start | bytes 1769480 | tf_op jit(solution)/shard_map/ppermute | solution.py:51
  916.7 17.5 %collective-permute-start.55 = (bf16[192,1536]{1,0:T(8,128)(2,1)}, bf16[192,1536]{1,0:T(8,128)(2,1)S(1)}, u32[]{:S(2)}, u32[]{:S(2)}) collective-permute-start(bf16[192,1536]{1,0:T(8,128)(2,1)} %get-tuple-element.76), channel_id=1, source_target_pairs={{0,6},{2,4},{4,2},{6,0},{8,14},{10,12},{12,10},{14,8},{16,22},{18,... | collective-permute-start | bytes 1769480 | tf_op jit(solution)/shard_map/ppermute | solution.py:51
  918.7 26.7 %collective-permute-start.54 = (bf16[192,1536]{1,0:T(8,128)(2,1)}, bf16[192,1536]{1,0:T(8,128)(2,1)S(1)}, u32[]{:S(2)}, u32[]{:S(2)}) collective-permute-start(bf16[192,1536]{1,0:T(8,128)(2,1)} %get-tuple-element.75), channel_id=1, source_target_pairs={{0,4},{2,6},{4,0},{6,2},{8,12},{10,14},{12,8},{14,10},{16,20},{18,... | collective-permute-start | bytes 1769480 | tf_op jit(solution)/shard_map/ppermute | solution.py:51
  918.7 28.3 %collective-permute-start.53 = (bf16[192,1536]{1,0:T(8,128)(2,1)}, bf16[192,1536]{1,0:T(8,128)(2,1)S(1)}, u32[]{:S(2)}, u32[]{:S(2)}) collective-permute-start(bf16[192,1536]{1,0:T(8,128)(2,1)} %get-tuple-element.74), channel_id=1, source_target_pairs={{0,2},{2,0},{4,6},{6,4},{8,10},{10,8},{12,14},{14,12},{16,18},{18,... | collective-permute-start | bytes 1769480 | tf_op jit(solution)/shard_map/ppermute | solution.py:51
  922.2 27.5 %collective-permute-start.51 = (bf16[48,1536]{1,0:T(8,128)(2,1)S(1)}, bf16[48,1536]{1,0:T(8,128)(2,1)S(1)}, u32[]{:S(2)}, u32[]{:S(2)}) collective-permute-start(bf16[48,1536]{1,0:T(8,128)(2,1)S(1)} %get-tuple-element.115), channel_id=1, source_target_pairs={{0,24},{2,26},{4,28},{6,30},{8,16},{10,18},{12,20},{14,22},{16,8},... | collective-permute-start | bytes 442376 | tf_op jit(solution)/shard_map/ppermute | solution.py:51
  934.2 15.6 %collective-permute-start.50 = (bf16[48,1536]{1,0:T(8,128)(2,1)S(1)}, bf16[48,1536]{1,0:T(8,128)(2,1)S(1)}, u32[]{:S(2)}, u32[]{:S(2)}) collective-permute-start(bf16[48,1536]{1,0:T(8,128)(2,1)S(1)} %get-tuple-element.116), channel_id=1, source_target_pairs={{0,16},{2,18},{4,20},{6,22},{8,24},{10,26},{12,28},{14,30},{16,0},... | collective-permute-start | bytes 442376 | tf_op jit(solution)/shard_map/ppermute | solution.py:51
  945.4 6.4 collective-permute-start.49
  947.4 9.9 %collective-permute-start.58 = (bf16[48,1536]{1,0:T(8,128)(2,1)S(1)}, bf16[48,1536]{1,0:T(8,128)(2,1)S(1)}, u32[]{:S(2)}, u32[]{:S(2)}) collective-permute-start(bf16[48,1536]{1,0:T(8,128)(2,1)S(1)} %get-tuple-element.112), channel_id=1, source_target_pairs={{0,24},{2,26},{4,28},{6,30},{8,16},{10,18},{12,20},{14,22},{16,8},... | collective-permute-start | bytes 442376 | tf_op jit(solution)/shard_map/ppermute | solution.py:51
  949.8 12.5 %collective-permute-start.57 = (bf16[48,1536]{1,0:T(8,128)(2,1)S(1)}, bf16[48,1536]{1,0:T(8,128)(2,1)S(1)}, u32[]{:S(2)}, u32[]{:S(2)}) collective-permute-start(bf16[48,1536]{1,0:T(8,128)(2,1)S(1)} %get-tuple-element.113), channel_id=1, source_target_pairs={{0,16},{2,18},{4,20},{6,22},{8,24},{10,26},{12,28},{14,30},{16,0},... | collective-permute-start | bytes 442376 | tf_op jit(solution)/shard_map/ppermute | solution.py:51
  949.8 12.5 %collective-permute-start.56 = (bf16[48,1536]{1,0:T(8,128)(2,1)S(1)}, bf16[48,1536]{1,0:T(8,128)(2,1)S(1)}, u32[]{:S(2)}, u32[]{:S(2)}) collective-permute-start(bf16[48,1536]{1,0:T(8,128)(2,1)S(1)} %get-tuple-element.111), channel_id=1, source_target_pairs={{0,8},{2,10},{4,12},{6,14},{8,0},{10,2},{12,4},{14,6},{16,24},{18,... | collective-permute-start | bytes 442376 | tf_op jit(solution)/shard_map/ppermute | solution.py:51
  (65 other events, 1304.9 us)

commit v2 on v1

v2 whole, which is shorter than its diff:
```python
import functools

import jax
import jax.numpy as jnp
from jax import lax
from jax.experimental import pallas as pl
from jax.experimental.pallas import tpu as pltpu
from jax.sharding import PartitionSpec as P

D = 768
HD = 64
SEQ = 64

score_scale = 40.0
margin = 0.3
loss_scale = 65536.0
norm_eps = 1e-06
masked_score = -30000.0

bf16 = jnp.bfloat16
f32 = jnp.float32

ALONG_Z = (4, 8, 12)
IN_PLANE = (1, 2, 3)


def contract(left, right, left_dim, right_dim):
    return lax.dot_general(
        left, right, (((left_dim,), (right_dim,)), ((), ())), preferred_element_type=f32
    )


def product(left, right):
    return contract(left, right, 1, 0)


def contract_last(left, right):
    return contract(left, right, 1, 1)


def contract_first(left, right):
    return contract(left, right, 0, 0)


def swap_cores(array):
    return lax.ppermute(array, "tensor", [(0, 1), (1, 0)])


def swap_chips(array, mask):
    count = lax.axis_size("dp")
    return lax.ppermute(array, "dp", [(i, i ^ mask) for i in range(count)])


def rows_orders(dp):
    if dp != 16:
        return ((0,), (0,))
    return tuple(tuple(j ^ i for j in plane for i in (0, *ALONG_Z)) for plane in ((0, 1, 2, 3), (0, 2, 1, 3)))


def gather_rows(shard, split):
    if lax.axis_size("dp") != 16:
        full = lax.all_gather(shard, "dp", axis=0, tiled=True)
        return full[:, :split], full[:, split:]
    near = jnp.concatenate([shard] + [swap_chips(shard, mask) for mask in ALONG_Z], axis=0)
    near_a, near_b = near[:, :split], near[:, split:]
    low_a = jnp.concatenate([near_a, swap_chips(near_a, 1)], axis=0)
    low_b = jnp.concatenate([near_b, swap_chips(near_b, 2)], axis=0)
    return (
        jnp.concatenate([low_a, swap_chips(low_a, 2)], axis=0),
        jnp.concatenate([low_b, swap_chips(low_b, 1)], axis=0),
    )


def reduce_rows(part_a, part_b):
    if lax.axis_size("dp") != 16:
        both = jnp.concatenate([part_a, part_b], axis=1).astype(f32)
        return lax.psum_scatter(both, "dp", scatter_dimension=0, tiled=True)

    def halve(array, mask):
        rows = array.shape[0] // 2
        return (array[:rows].astype(f32) + swap_chips(array[rows:], mask).astype(f32)).astype(bf16)

    part_a, part_b = halve(part_a, 2), halve(part_b, 1)
    part_a, part_b = halve(part_a, 1), halve(part_b, 2)
    near = jnp.concatenate([part_a, part_b], axis=1)
    rows = near.shape[0] // 4
    total = near[:rows].astype(f32)
    for i, mask in enumerate(ALONG_Z):
        total = total + swap_chips(near[(i + 1) * rows : (i + 2) * rows], mask).astype(f32)
    return total


def gather_units(own):
    if lax.axis_size("dp") != 16:
        mine = lax.all_gather(own, "dp", axis=0, tiled=True)
    else:
        near = jnp.concatenate([own] + [swap_chips(own, mask) for mask in ALONG_Z], axis=0)
        mine = jnp.concatenate([near] + [swap_chips(near, mask) for mask in IN_PLANE], axis=0)
    return mine, swap_cores(mine)


def sum_small(array):
    if lax.axis_size("dp") != 16:
        return lax.psum(array, "dp")
    for group in (ALONG_Z, IN_PLANE):
        a, b, c = [swap_chips(array, mask) for mask in group]
        array = (array + a) + (b + c)
    return array


def column_mask():
    row = lax.broadcasted_iota(jnp.int32, (2 * SEQ, 2 * HD), 0) // SEQ
    column = lax.broadcasted_iota(jnp.int32, (2 * SEQ, 2 * HD), 1) // HD
    return (row == column).astype(f32).astype(bf16)


def two_heads(pair, mask):
    return jnp.concatenate([pair, pair], axis=0) * mask


def pick_heads(both, first):
    return jnp.where(first, both[:SEQ], both[SEQ:])


def block_copies(source, target, order, me, sem):
    rows = source.shape[0] // len(order)
    copies = []
    for k, mask in enumerate(order):
        to = pl.multiple_of((me ^ mask) * rows, 16) if len(order) > 1 else 0
        copies.append(
            pltpu.make_async_copy(source.at[pl.ds(k * rows, rows)], target.at[pl.ds(to, rows)], sem)
        )
    return copies


def start_all(copies):
    for copy in copies:
        copy.start()


def wait_whole(target, sem):
    pltpu.make_async_copy(target, target, sem).wait()


def attention_forward_kernel(
    orders, where_ref, tokens_ref, query_bias_ref, value_bias_ref, part_a, part_b,
    query_ref, key_ref, value_ref, context_ref, probs_ref, weight, sem,
):
    width_a = part_a.shape[1]
    head_cols = query_ref.shape[1]

    @pl.when(pl.program_id(0) == 0)
    def _():
        me = where_ref[0]
        start_all(block_copies(part_a, weight.at[:, pl.ds(0, width_a)], orders[0], me, sem.at[0]))
        start_all(block_copies(part_b, weight.at[:, pl.ds(width_a, part_b.shape[1])], orders[1], me, sem.at[0]))
        wait_whole(weight, sem.at[0])

    rows = tokens_ref.shape[0]
    projected = product(tokens_ref[...], weight[...])
    query_ref[...] = (projected[:, :head_cols] + query_bias_ref[...]).astype(bf16)
    key_ref[...] = projected[:, head_cols : 2 * head_cols].astype(bf16)
    value_ref[...] = (projected[:, 2 * head_cols :] + value_bias_ref[...]).astype(bf16)
    mask = column_mask()
    first = lax.broadcasted_iota(jnp.int32, (SEQ, 2 * HD), 1) < HD
    for sentence in range(rows // SEQ):
        at = slice(sentence * SEQ, (sentence + 1) * SEQ)
        for pair in range(head_cols // (2 * HD)):
            columns = slice(pair * 2 * HD, (pair + 1) * 2 * HD)
            scores = contract_last(key_ref[at, columns], two_heads(query_ref[at, columns], mask)) * HD ** (-0.5)
            powers = jnp.exp(scores - jnp.max(scores, axis=0, keepdims=True))
            probs = powers / jnp.sum(powers, axis=0, keepdims=True)
            probs_ref[at, columns] = probs
            both = contract_first(probs.astype(bf16), value_ref[at, columns])
            context_ref[at, columns] = pick_heads(both, first).astype(bf16)


def any_spec():
    return pl.BlockSpec(memory_space=pl.ANY)


def whole_spec(shape):
    return pl.BlockSpec(shape, lambda *_: (0,) * len(shape), pipeline_mode=pl.Buffered(1))


def kernel_params():
    return pltpu.CompilerParams(vmem_limit_bytes=60 * 1024 * 1024, dimension_semantics=("arbitrary",))


def attention_forward(orders, where, tokens, query_bias, value_bias, part_a, part_b):
    rows = tokens.shape[0]
    head_cols = query_bias.shape[1]
    block = 4 * SEQ
    by_rows = lambda i, where: (i, 0)
    out = lambda dtype: jax.ShapeDtypeStruct((rows, head_cols), dtype)
    return pl.pallas_call(
        functools.partial(attention_forward_kernel, orders),
        out_shape=[out(bf16)] * 4 + [out(f32)],
        grid_spec=pltpu.PrefetchScalarGridSpec(
            num_scalar_prefetch=1,
            grid=(rows // block,),
            in_specs=[
                pl.BlockSpec((block, D), by_rows),
                whole_spec((1, head_cols)), whole_spec((1, head_cols)), any_spec(), any_spec(),
            ],
            out_specs=[pl.BlockSpec((block, head_cols), by_rows)] * 5,
            scratch_shapes=[pltpu.VMEM((D, 3 * head_cols), bf16), pltpu.SemaphoreType.DMA((1,))],
        ),
        compiler_params=kernel_params(),
        cost_estimate=pl.CostEstimate(
            flops=2 * rows * D * 3 * head_cols * 2, bytes_accessed=rows * head_cols * 30, transcendentals=0
        ),
        name="attention_forward",
    )(where, tokens, query_bias, value_bias, part_a, part_b)


TAIL = (0.1167079709, 0.07627463045, 0.2455670143, -0.1994404095, 0.3630729868, -0.1021822206)


def normal_parts(values):
    bell = jnp.exp(values * values * -0.5)
    ratio = 1.0 / (1.0 + (0.4 * 0.5**0.5) * jnp.abs(values))
    tail = jnp.full_like(values, TAIL[5])
    for factor in TAIL[4::-1]:
        tail = tail * ratio + factor
    tail = tail * ratio * bell
    return jnp.where(values < 0.0, tail, 1.0 - tail), bell * 0.3989422804014327


def feed_forward_kernel(
    orders, where_ref, tokens_ref, context_own_ref, context_other_ref, output_bias_ref, gain_one_ref, shift_one_ref,
    up_bias_own_ref, up_bias_other_ref, down_bias_ref, gain_two_ref, shift_two_ref,
    up_own_a, up_own_b, up_other_a, up_other_b, down_own_a, down_own_b, down_other_a, down_other_b,
    hidden_ref, normed_one_ref, inv_one_ref, act_ref, slope_ref, normed_two_ref, inv_two_ref, pooled_ref, unit_ref,
    out_up, down, sem,
):
    head_cols = context_own_ref.shape[1]
    hidden_cols = up_bias_own_ref.shape[1]

    @pl.when(pl.program_id(0) == 0)
    def _():
        me = where_ref[0]
        for half, (part_a, part_b) in enumerate(((up_own_a, up_own_b), (up_other_a, up_other_b))):
            at = out_up.at[half]
            start_all(block_copies(part_a, at.at[:, pl.ds(0, part_a.shape[1])], orders[0], me, sem.at[half]))
            start_all(block_copies(part_b, at.at[:, pl.ds(part_a.shape[1], part_b.shape[1])], orders[1], me, sem.at[half]))
        for half, (part_a, part_b) in enumerate(((down_own_a, down_own_b), (down_other_a, down_other_b))):
            at = down.at[half]
            start_all(block_copies(part_a, at.at[:, pl.ds(0, part_a.shape[1])], orders[0], me, sem.at[2 + half]))
            start_all(block_copies(part_b, at.at[:, pl.ds(part_a.shape[1], part_b.shape[1])], orders[1], me, sem.at[2 + half]))
        for half in range(2):
            wait_whole(out_up.at[half], sem.at[half])
            wait_whole(down.at[half], sem.at[2 + half])

    attended = contract_last(context_own_ref[...], out_up[0, :, :head_cols]) + contract_last(
        context_other_ref[...], out_up[1, :, :head_cols]
    )
    residual = tokens_ref[...].astype(f32) + attended + output_bias_ref[...]
    centred = residual - jnp.mean(residual, axis=1, keepdims=True)
    inv_one = lax.rsqrt(jnp.mean(centred * centred, axis=1, keepdims=True) + norm_eps)
    normed = centred * inv_one
    normed_one_ref[...] = normed.astype(bf16)
    inv_one_ref[...] = inv_one
    hidden = normed * gain_one_ref[...] + shift_one_ref[...]
    hidden_low = hidden.astype(bf16)
    hidden_ref[...] = hidden_low
    second = hidden + down_bias_ref[...]
    step = 512
    for half, bias_ref in enumerate((up_bias_own_ref, up_bias_other_ref)):
        for start in range(0, hidden_cols, step):
            columns = slice(start, start + step)
            pre_act = product(hidden_low, out_up[half, :, head_cols + start : head_cols + start + step])
            pre_act = pre_act + bias_ref[:, columns]
            below, density = normal_parts(pre_act)
            act = (pre_act * below).astype(bf16)
            to = slice(half * hidden_cols + start, half * hidden_cols + start + step)
            act_ref[:, to] = act
            slope_ref[:, to] = (below + pre_act * density).astype(bf16)
            second = second + contract_last(act, down[half, :, columns])
    centred = second - jnp.mean(second, axis=1, keepdims=True)
    inv_two = lax.rsqrt(jnp.mean(centred * centred, axis=1, keepdims=True) + norm_eps)
    normed = centred * inv_two
    normed_two_ref[...] = normed.astype(bf16)
    inv_two_ref[...] = inv_two
    output = normed * gain_two_ref[...] + shift_two_ref[...]
    count = output.shape[0] // SEQ
    pooled = jnp.concatenate(
        [jnp.mean(output[s * SEQ : (s + 1) * SEQ], axis=0, keepdims=True) for s in range(count)], axis=0
    )
    unit = pooled * lax.rsqrt(jnp.sum(pooled * pooled, axis=1, keepdims=True) + norm_eps)
    pooled_ref[0] = pooled
    unit_ref[0] = unit.astype(bf16).astype(f32)


def feed_forward(orders, where, tokens, context, context_other, vectors, parts):
    rows = tokens.shape[0] // 2
    head_cols = context.shape[1]
    hidden_cols = vectors[3].shape[1]
    block = 4 * SEQ
    blocks = rows // block
    by_rows = lambda i, where: (i, 0)
    mine = lambda i, where: (where[1] * blocks + i, 0)
    out = lambda width, dtype: jax.ShapeDtypeStruct((rows, width), dtype)
    pooled_shape = jax.ShapeDtypeStruct((blocks, block // SEQ, D), f32)
    pooled_spec = pl.BlockSpec((1, block // SEQ, D), lambda i, where: (i, 0, 0))
    return pl.pallas_call(
        functools.partial(feed_forward_kernel, orders),
        out_shape=[
            out(D, bf16), out(D, bf16), out(1, f32), out(2 * hidden_cols, bf16), out(2 * hidden_cols, bf16),
            out(D, bf16), out(1, f32), pooled_shape, pooled_shape,
        ],
        grid_spec=pltpu.PrefetchScalarGridSpec(
            num_scalar_prefetch=1,
            grid=(blocks,),
            in_specs=[
                pl.BlockSpec((block, D), mine), pl.BlockSpec((block, head_cols), mine),
                pl.BlockSpec((block, head_cols), by_rows),
            ]
            + [whole_spec(vector.shape) for vector in vectors]
            + [any_spec()] * 8,
            out_specs=[
                pl.BlockSpec((block, D), by_rows), pl.BlockSpec((block, D), by_rows), pl.BlockSpec((block, 1), by_rows),
                pl.BlockSpec((block, 2 * hidden_cols), by_rows), pl.BlockSpec((block, 2 * hidden_cols), by_rows),
                pl.BlockSpec((block, D), by_rows), pl.BlockSpec((block, 1), by_rows), pooled_spec, pooled_spec,
            ],
            scratch_shapes=[
                pltpu.VMEM((2, D, head_cols + hidden_cols), bf16), pltpu.VMEM((2, D, hidden_cols), bf16),
                pltpu.SemaphoreType.DMA((4,)),
            ],
        ),
        compiler_params=kernel_params(),
        cost_estimate=pl.CostEstimate(
            flops=2 * rows * D * 2 * (2 * hidden_cols + head_cols), bytes_accessed=30_000_000, transcendentals=0
        ),
        name="feed_forward",
    )(where, tokens, context, context_other, *vectors, *parts)


def pair_kernel(
    order, where_ref, sizes_ref, own_ref, other_ref, pooled_ref, order_row_ref, order_column_ref,
    loss_ref, grad_ref, units, coeffs,
):
    me, core = where_ref[0], where_ref[1]
    count = units.shape[0]
    pairs = count // 2
    rows = own_ref.shape[0] // len(order)
    for k, mask in enumerate(order):
        at = slice(k * rows, (k + 1) * rows)
        units[pl.ds(pl.multiple_of(((me ^ mask) * 2 + core) * rows, 16), rows), :] = own_ref[at, :]
        units[pl.ds(pl.multiple_of(((me ^ mask) * 2 + 1 - core) * rows, 16), rows), :] = other_ref[at, :]
    along_rows = lax.broadcasted_iota(jnp.int32, (count, count), 0)
    along_columns = lax.broadcasted_iota(jnp.int32, (count, count), 1)
    place_column = jnp.sum(jnp.where(order_row_ref[...] == along_rows, along_columns, 0), axis=1, keepdims=True)
    place_row = jnp.sum(jnp.where(order_column_ref[...] == along_columns, along_rows, 0), axis=0, keepdims=True)

    def describe(place):
        source = (place < pairs).astype(jnp.int32)
        pair = place - pairs * (1 - source)
        group = jnp.zeros_like(pair)
        end = jnp.int32(0)
        for g in range(sizes_ref.shape[0]):
            end = end + sizes_ref[g]
            group = group + (pair >= end).astype(jnp.int32)
        return source, pair, group

    source_column, pair_column, group_column = describe(place_column)
    source_row, pair_row, group_row = describe(place_row)
    across = source_column != source_row
    partner = across & (pair_column == pair_row)
    scores = score_scale * contract_last(units[...], units[...])
    scores = scores - score_scale * margin * partner.astype(f32)
    scores = jnp.where(across & (group_column == group_row), scores, masked_score)

    def log_total(axis):
        peak = jnp.max(scores, axis=axis, keepdims=True)
        return peak + jnp.log(jnp.sum(jnp.exp(scores - peak), axis=axis, keepdims=True))

    lse_column, lse_row = log_total(1), log_total(0)
    matched = jnp.sum(jnp.where(partner, scores, 0.0), axis=1, keepdims=True)
    loss = jnp.sum(lse_column - matched, axis=0, keepdims=True) * (1.0 / pairs)
    loss_ref[...] = jnp.broadcast_to(loss, loss_ref.shape)
    coeffs[...] = (loss_scale / pairs) * (
        jnp.exp(scores - lse_column) + jnp.exp(scores - lse_row) - 2.0 * partner.astype(f32)
    )
    mine = pl.ds(pl.multiple_of((me * 2 + core) * rows, 16), rows)
    grad_unit = score_scale * product(coeffs[mine, :].astype(bf16), units[...])
    pooled = pooled_ref[...]
    inverse = lax.rsqrt(jnp.sum(pooled * pooled, axis=1, keepdims=True) + norm_eps)
    unit = pooled * inverse
    grad_ref[...] = inverse * (grad_unit - unit * jnp.sum(grad_unit * unit, axis=1, keepdims=True))


def pair_gradient(order, where, group_sizes, sentence_order, own, other, pooled):
    count = sentence_order.shape[0]
    return pl.pallas_call(
        functools.partial(pair_kernel, order),
        out_shape=[jax.ShapeDtypeStruct((8, 128), f32), jax.ShapeDtypeStruct(pooled.shape, f32)],
        grid_spec=pltpu.PrefetchScalarGridSpec(
            num_scalar_prefetch=2,
            grid=(1,),
            in_specs=[
                whole_spec(own.shape), whole_spec(other.shape), whole_spec(pooled.shape),
                whole_spec((1, count)), whole_spec((count, 1)),
            ],
            out_specs=[whole_spec((8, 128)), whole_spec(pooled.shape)],
            scratch_shapes=[pltpu.VMEM((count, D), bf16), pltpu.VMEM((count, count), f32)],
        ),
        compiler_params=kernel_params(),
        cost_estimate=pl.CostEstimate(flops=2 * count * count * D, bytes_accessed=2_000_000, transcendentals=0),
        name="pair_gradient",
    )(where, group_sizes, own, other, pooled, sentence_order.reshape(1, count), sentence_order.reshape(count, 1))


def turn_rows(values, orders, me, turned, target_a, target_b):
    turned[...] = values.T
    for order, target in ((orders[0], target_a), (orders[1], target_b)):
        rows = turned.shape[0] // len(order)
        for k, mask in enumerate(order):
            at = pl.multiple_of((me ^ mask) * rows, 16) if len(order) > 1 else 0
            target[k * rows : (k + 1) * rows, :] = turned[pl.ds(at, rows), :]


def down_gradient_kernel(
    orders, where_ref, grad_pooled_ref, normed_ref, inv_ref, gain_ref, act_ref,
    second_ref, low_ref, weight_ref, sums_ref, turned, turned_both,
):
    @pl.when(pl.program_id(0) == 0)
    def _():
        gain = gain_ref[...]
        gain_sum = jnp.zeros((1, D), f32)
        shift_sum = jnp.zeros((1, D), f32)
        bias_sum = jnp.zeros((1, D), f32)
        for sentence in range(grad_pooled_ref.shape[0]):
            at = slice(sentence * SEQ, (sentence + 1) * SEQ)
            upstream = grad_pooled_ref[sentence : sentence + 1, :] * (1.0 / SEQ)
            scaled = upstream * gain
            normed = normed_ref[at, :].astype(f32)
            second_mean = jnp.mean(scaled * normed, axis=1, keepdims=True)
            grad = inv_ref[at, :] * (scaled - jnp.mean(scaled, axis=1, keepdims=True) - normed * second_mean)
            second_ref[at, :] = grad
            low_ref[at, :] = grad.astype(bf16)
            gain_sum = gain_sum + upstream * jnp.sum(normed, axis=0, keepdims=True)
            shift_sum = shift_sum + upstream * SEQ
            bias_sum = bias_sum + jnp.sum(grad, axis=0, keepdims=True)
        sums_ref[0:1, :] = gain_sum
        sums_ref[1:2, :] = shift_sum
        sums_ref[2:3, :] = bias_sum
        turn_rows(low_ref[...], orders, where_ref[0], turned, turned_both.at[0], turned_both.at[1])

    which = lax.rem(pl.program_id(0), 2)
    weight_ref[0] = product(turned_both[which], act_ref[...]).astype(bf16)


def down_gradient(orders, where, grad_pooled, normed, inv, gain, act):
    rows, hidden = act.shape
    chunk = hidden // 4
    return pl.pallas_call(
        functools.partial(down_gradient_kernel, orders),
        out_shape=[
            jax.ShapeDtypeStruct((rows, D), f32), jax.ShapeDtypeStruct((rows, D), bf16),
            jax.ShapeDtypeStruct((4, D, chunk), bf16), jax.ShapeDtypeStruct((8, D), f32),
        ],
        grid_spec=pltpu.PrefetchScalarGridSpec(
            num_scalar_prefetch=1,
            grid=(4,),
            in_specs=[
                whole_spec(grad_pooled.shape), whole_spec((rows, D)), whole_spec((rows, 1)), whole_spec((1, D)),
                pl.BlockSpec((rows, chunk), lambda i, where: (0, i)),
            ],
            out_specs=[
                whole_spec((rows, D)), whole_spec((rows, D)),
                pl.BlockSpec((1, D, chunk), lambda i, where: (i, 0, 0)), whole_spec((8, D)),
            ],
            scratch_shapes=[pltpu.VMEM((D, rows), bf16), pltpu.VMEM((2, D, rows), bf16)],
        ),
        compiler_params=kernel_params(),
        cost_estimate=pl.CostEstimate(flops=2 * rows * D * hidden, bytes_accessed=20_000_000, transcendentals=0),
        name="down_gradient",
    )(where, grad_pooled, normed, inv, gain, act)


def up_gradient_kernel(
    orders, where_ref, second_ref, low_ref, slope_ref, hidden_ref, normed_ref, inv_ref, gain_ref,
    context_own_ref, context_other_ref,
    up_own_a, up_own_b, up_other_a, up_other_b, down_own_a, down_own_b, down_other_a, down_other_b,
    weight_ref, bias_ref, residual_ref, context_grad_own_ref, context_grad_other_ref, out_weight_ref, sums_ref,
    out_up, down, total, attn_low, turned, turned_both, sem,
):
    me = where_ref[0]
    step = pl.program_id(0)
    head_cols = context_own_ref.shape[1]
    chunk = slope_ref.shape[1]

    @pl.when(step == 0)
    def _():
        for half, (part_a, part_b) in enumerate(((up_own_a, up_own_b), (up_other_a, up_other_b))):
            at = out_up.at[half]
            start_all(block_copies(part_a, at.at[:, pl.ds(0, part_a.shape[1])], orders[0], me, sem.at[half]))
            start_all(block_copies(part_b, at.at[:, pl.ds(part_a.shape[1], part_b.shape[1])], orders[1], me, sem.at[half]))
        for half, (part_a, part_b) in enumerate(((down_own_a, down_own_b), (down_other_a, down_other_b))):
            at = down.at[half]
            start_all(block_copies(part_a, at.at[:, pl.ds(0, part_a.shape[1])], orders[0], me, sem.at[2 + half]))
            start_all(block_copies(part_b, at.at[:, pl.ds(part_a.shape[1], part_b.shape[1])], orders[1], me, sem.at[2 + half]))
        turn_rows(hidden_ref[...], orders, me, turned, turned_both.at[0], turned_both.at[1])
        total[...] = second_ref[...]
        for half in range(2):
            wait_whole(out_up.at[half], sem.at[half])
            wait_whole(down.at[half], sem.at[2 + half])

    half, which = step // 2, lax.rem(step, 2)
    grad_act = product(low_ref[...], down[half, :, pl.ds(pl.multiple_of(which * chunk, 128), chunk)])
    grad_pre = (grad_act * slope_ref[...].astype(f32)).astype(bf16)
    bias_ref[0] = jnp.broadcast_to(jnp.sum(grad_pre.astype(f32), axis=0, keepdims=True), bias_ref.shape[1:])
    weight_ref[0] = product(turned_both[which], grad_pre).astype(bf16)
    total[...] += contract_last(grad_pre, out_up[half, :, pl.ds(pl.multiple_of(head_cols + which * chunk, 128), chunk)])

    @pl.when(step == 3)
    def _():
        gain = gain_ref[...]
        gain_sum = jnp.zeros((1, D), f32)
        shift_sum = jnp.zeros((1, D), f32)
        bias_sum = jnp.zeros((1, D), f32)
        rows = 128
        for start in range(0, total.shape[0], rows):
            at = slice(start, start + rows)
            upstream = total[at, :]
            normed = normed_ref[at, :].astype(f32)
            scaled = upstream * gain
            first_mean = jnp.mean(scaled, axis=1, keepdims=True)
            second_mean = jnp.mean(scaled * normed, axis=1, keepdims=True)
            grad = inv_ref[at, :] * (scaled - first_mean - normed * second_mean)
            residual_ref[at, :] = grad
            low = grad.astype(bf16)
            attn_low[at, :] = low
            gain_sum = gain_sum + jnp.sum(upstream * normed, axis=0, keepdims=True)
            shift_sum = shift_sum + jnp.sum(upstream, axis=0, keepdims=True)
            bias_sum = bias_sum + jnp.sum(grad, axis=0, keepdims=True)
            context_grad_own_ref[at, :] = product(low, out_up[0, :, :head_cols]).astype(bf16)
            context_grad_other_ref[at, :] = product(low, out_up[1, :, :head_cols]).astype(bf16)
        sums_ref[0:1, :] = gain_sum
        sums_ref[1:2, :] = shift_sum
        sums_ref[2:3, :] = bias_sum
        turn_rows(attn_low[...], orders, me, turned, turned_both.at[0], turned_both.at[1])
        split = OUT_SPLIT
        for k, context_ref in enumerate((context_own_ref, context_other_ref)):
            out_weight_ref[k, :, :split] = product(turned_both[0], context_ref[:, :split]).astype(bf16)
            out_weight_ref[k, :, split:] = product(turned_both[1], context_ref[:, split:]).astype(bf16)


OUT_SPLIT = 128


def up_gradient(orders, where, second, low, slope, hidden_low, normed, inv, gain, context, context_other, parts):
    rows, hidden = slope.shape
    head_cols = context.shape[1]
    chunk = hidden // 4
    mine = lambda i, where: (where[1], 0)
    return pl.pallas_call(
        functools.partial(up_gradient_kernel, orders),
        out_shape=[
            jax.ShapeDtypeStruct((4, D, chunk), bf16), jax.ShapeDtypeStruct((4, 8, chunk), f32),
            jax.ShapeDtypeStruct((rows, D), f32),
            jax.ShapeDtypeStruct((rows, head_cols), bf16), jax.ShapeDtypeStruct((rows, head_cols), bf16),
            jax.ShapeDtypeStruct((2, D, head_cols), bf16), jax.ShapeDtypeStruct((8, D), f32),
        ],
        grid_spec=pltpu.PrefetchScalarGridSpec(
            num_scalar_prefetch=1,
            grid=(4,),
            in_specs=[
                whole_spec((rows, D)), whole_spec((rows, D)),
                pl.BlockSpec((rows, chunk), lambda i, where: (0, i)),
                whole_spec((rows, D)), whole_spec((rows, D)), whole_spec((rows, 1)), whole_spec((1, D)),
                pl.BlockSpec((rows, head_cols), mine, pipeline_mode=pl.Buffered(1)), whole_spec((rows, head_cols)),
            ]
            + [any_spec()] * 8,
            out_specs=[
                pl.BlockSpec((1, D, chunk), lambda i, where: (i, 0, 0)),
                pl.BlockSpec((1, 8, chunk), lambda i, where: (i, 0, 0)),
                whole_spec((rows, D)), whole_spec((rows, head_cols)), whole_spec((rows, head_cols)),
                whole_spec((2, D, head_cols)), whole_spec((8, D)),
            ],
            scratch_shapes=[
                pltpu.VMEM((2, D, head_cols + hidden // 2), bf16), pltpu.VMEM((2, D, hidden // 2), bf16),
                pltpu.VMEM((rows, D), f32), pltpu.VMEM((rows, D), bf16), pltpu.VMEM((D, rows), bf16),
                pltpu.VMEM((2, D, rows), bf16), pltpu.SemaphoreType.DMA((4,)),
            ],
        ),
        compiler_params=kernel_params(),
        cost_estimate=pl.CostEstimate(flops=6 * rows * D * hidden, bytes_accessed=40_000_000, transcendentals=0),
        name="up_gradient",
    )(where, second, low, slope, hidden_low, normed, inv, gain, context, context_other, *parts)


def attention_backward_kernel(
    orders, where_ref, tokens_ref, query_ref, key_ref, value_ref, probs_ref, grad_other_ref, grad_own_ref,
    residual_ref, part_a, part_b,
    terms_other_ref, tokens_grad_ref, weight_a_ref, weight_b_ref, bias_ref,
    weight, grads, turned, turned_a, turned_b, sem,
):
    me = where_ref[0]
    step = pl.program_id(0)
    blocks = pl.num_programs(0)
    rows, head_cols = query_ref.shape
    width_a = part_a.shape[1]

    @pl.when(step == 0)
    def _():
        start_all(block_copies(part_a, weight.at[:, pl.ds(0, width_a)], orders[0], me, sem.at[0]))
        start_all(block_copies(part_b, weight.at[:, pl.ds(width_a, part_b.shape[1])], orders[1], me, sem.at[0]))
        bias_ref[...] = jnp.zeros_like(bias_ref)

    at_block = pl.ds(pl.multiple_of(step * rows, rows), rows)
    turn_rows(tokens_ref[...], orders, me, turned, turned_a.at[:, at_block], turned_b.at[:, at_block])
    other = step < blocks // 2
    mask = column_mask()
    first = lax.broadcasted_iota(jnp.int32, (SEQ, 2 * HD), 1) < HD
    scale = HD ** (-0.5)
    for sentence in range(rows // SEQ):
        at = slice(sentence * SEQ, (sentence + 1) * SEQ)
        to = pl.ds(pl.multiple_of(step * rows + sentence * SEQ, SEQ), SEQ)
        for pair in range(head_cols // (2 * HD)):
            columns = slice(pair * 2 * HD, (pair + 1) * 2 * HD)
            upstream = jnp.where(other, grad_other_ref[at, columns], grad_own_ref[at, columns])
            upstream = two_heads(upstream, mask)
            probs = probs_ref[at, columns]
            grad_probs = contract_last(value_ref[at, columns], upstream)
            inner = jnp.sum(grad_probs * probs, axis=0, keepdims=True)
            grad_scores = (probs * (grad_probs - inner)).astype(bf16)
            grad_value = product(probs.astype(bf16), upstream)
            grad_key = product(grad_scores, two_heads(query_ref[at, columns], mask)) * scale
            grad_query = pick_heads(contract_first(grad_scores, key_ref[at, columns]), first) * scale
            for k, grad in enumerate((grad_query, grad_key, grad_value)):
                grads[to, k * head_cols + pair * 2 * HD : k * head_cols + (pair + 1) * 2 * HD] = grad.astype(bf16)

    @pl.when(step == 0)
    def _():
        wait_whole(weight, sem.at[0])

    here = grads[at_block, :]
    bias_ref[...] += jnp.broadcast_to(jnp.sum(here.astype(f32), axis=0, keepdims=True), bias_ref.shape)
    terms = contract_last(here, weight[...])

    @pl.when(other)
    def _():
        terms_other_ref[...] = terms.astype(bf16)

    @pl.when(jnp.logical_not(other))
    def _():
        tokens_grad_ref[...] = terms + residual_ref[...]

    @pl.when(step == blocks - 1)
    def _():
        weight_a_ref[...] = product(turned_a[...], grads[:, :width_a]).astype(bf16)
        weight_b_ref[...] = product(turned_b[...], grads[:, width_a:]).astype(bf16)


def attention_backward(orders, where, tokens, queries, key_rows, values, probs, grad_other, grad_own, residual, part_a, part_b):
    rows = tokens.shape[0]
    head_cols = queries.shape[1]
    block = 4 * SEQ
    half = rows // block // 2
    split, rest = part_a.shape[1], part_b.shape[1]
    by_rows = lambda i, where: (jnp.where(i < half, (1 - where[1]) * half + i, where[1] * half + i - half), 0)
    early = lambda i, where: (jnp.minimum(i, half - 1), 0)
    late = lambda i, where: (jnp.maximum(i - half, 0), 0)
    heads = pl.BlockSpec((block, head_cols), by_rows)
    return pl.pallas_call(
        functools.partial(attention_backward_kernel, orders),
        out_shape=[
            jax.ShapeDtypeStruct((rows // 2, D), bf16), jax.ShapeDtypeStruct((rows // 2, D), f32),
            jax.ShapeDtypeStruct((D, split), bf16), jax.ShapeDtypeStruct((D, rest), bf16),
            jax.ShapeDtypeStruct((8, 3 * head_cols), f32),
        ],
        grid_spec=pltpu.PrefetchScalarGridSpec(
            num_scalar_prefetch=1,
            grid=(2 * half,),
            in_specs=[
                pl.BlockSpec((block, D), by_rows), heads, heads, heads, heads,
                pl.BlockSpec((block, head_cols), early), pl.BlockSpec((block, head_cols), late),
                pl.BlockSpec((block, D), late), any_spec(), any_spec(),
            ],
            out_specs=[
                pl.BlockSpec((block, D), early), pl.BlockSpec((block, D), late),
                whole_spec((D, split)), whole_spec((D, rest)), whole_spec((8, 3 * head_cols)),
            ],
            scratch_shapes=[
                pltpu.VMEM((D, 3 * head_cols), bf16), pltpu.VMEM((rows, 3 * head_cols), bf16),
                pltpu.VMEM((D, block), bf16), pltpu.VMEM((D, rows), bf16), pltpu.VMEM((D, rows), bf16),
                pltpu.SemaphoreType.DMA((1,)),
            ],
        ),
        compiler_params=kernel_params(),
        cost_estimate=pl.CostEstimate(
            flops=2 * rows * D * 3 * head_cols * 2, bytes_accessed=30_000_000, transcendentals=0
        ),
        name="attention_backward",
    )(where, tokens, queries, key_rows, values, probs, grad_other, grad_own, residual, part_a, part_b)


def pair_objective(unit_low, pooled, group_sizes, sentence_order, device):
    total_sent = unit_low.shape[0]
    pair_count = total_sent // 2
    own_count = pooled.shape[0]
    sources = jnp.take(unit_low, sentence_order[:pair_count], axis=0)
    targets = jnp.take(unit_low, sentence_order[pair_count:], axis=0)
    group_ends = jnp.cumsum(group_sizes)
    pair_ids = jnp.arange(pair_count, dtype=jnp.int32)
    group_of = jnp.sum((pair_ids[:, None] >= group_ends[None, :]).astype(jnp.int32), axis=1)
    block_rows = min(512, pair_count)

    def scan_step(carried, offset):
        col_peak, col_total = carried
        row_ids = offset + jnp.arange(block_rows, dtype=jnp.int32)
        row_units = lax.dynamic_slice_in_dim(sources, offset, block_rows, 0)
        row_groups = lax.dynamic_slice_in_dim(group_of, offset, block_rows, 0)
        is_same = row_ids[:, None] == pair_ids[None, :]
        scores = score_scale * contract_last(row_units, targets)
        scores = scores - score_scale * margin * is_same.astype(jnp.float32)
        scores = jnp.where(row_groups[:, None] == group_of[None, :], scores, masked_score)
        row_peak = jnp.max(scores, axis=1, keepdims=True)
        row_lse = row_peak[:, 0] + jnp.log(jnp.sum(jnp.exp(scores - row_peak), axis=1))
        diagonal = jnp.sum(jnp.where(is_same, scores, 0.0), axis=1)
        new_peak = jnp.maximum(col_peak, jnp.max(scores, axis=0))
        new_total = col_total * jnp.exp(col_peak - new_peak) + jnp.sum(
            jnp.exp(scores - new_peak[None, :]), axis=0
        )
        return ((new_peak, new_total), (row_lse, diagonal))

    offsets = jnp.arange(pair_count // block_rows, dtype=jnp.int32) * block_rows
    start_state = (
        jnp.full((pair_count,), -1e30, jnp.float32),
        jnp.zeros((pair_count,), jnp.float32),
    )
    (col_peak, col_total), (row_lse, diagonal) = lax.scan(scan_step, start_state, offsets)
    col_lse = col_peak + jnp.log(col_total)
    row_lse = row_lse.reshape(pair_count)
    diagonal = diagonal.reshape(pair_count)
    loss_value = jnp.mean(row_lse + col_lse - 2.0 * diagonal)
    own_ids = device * own_count + jnp.arange(own_count, dtype=jnp.int32)
    matches = sentence_order[None, :] == own_ids[:, None]
    position = jnp.sum(
        jnp.where(matches, jnp.arange(total_sent, dtype=jnp.int32)[None, :], 0), axis=1
    )
    is_source = position < pair_count
    own_pair = jnp.where(is_source, position, position - pair_count)
    own_inverse = lax.rsqrt(jnp.sum(pooled * pooled, axis=-1, keepdims=True) + norm_eps)
    own_unit = pooled * own_inverse
    own_low = own_unit.astype(jnp.bfloat16)
    source_rows = is_source[:, None]
    pair_match = own_pair[:, None] == pair_ids[None, :]
    toward_targets = score_scale * contract_last(own_low, targets)
    toward_sources = score_scale * contract_last(own_low, sources)
    own_scores = jnp.where(source_rows, toward_targets, toward_sources)
    own_scores = own_scores - score_scale * margin * pair_match.astype(jnp.float32)
    own_group = jnp.sum(jnp.where(pair_match, group_of[None, :], 0), axis=1)
    own_scores = jnp.where(own_group[:, None] == group_of[None, :], own_scores, masked_score)
    own_lse = jnp.sum(
        jnp.where(pair_match, jnp.where(source_rows, row_lse[None, :], col_lse[None, :]), 0.0),
        axis=1,
    )
    other_lse = jnp.where(source_rows, col_lse[None, :], row_lse[None, :])
    grad_coeff = loss_scale / pair_count
    grad_scores = grad_coeff * (
        jnp.exp(own_scores - own_lse[:, None])
        + jnp.exp(own_scores - other_lse)
        - 2.0 * pair_match.astype(jnp.float32)
    )
    grad_low = grad_scores.astype(jnp.bfloat16)
    grad_unit = score_scale * jnp.where(
        source_rows, product(grad_low, targets), product(grad_low, sources)
    )
    grad_pooled = own_inverse * (
        grad_unit - own_unit * jnp.sum(grad_unit * own_unit, axis=-1, keepdims=True)
    )
    return (loss_value, grad_pooled)


def local(
    tokens, query_weight, key_weight, value_weight, output_weight, up_weight, down_weight,
    query_bias, value_bias, output_bias, first_gain, first_shift, up_bias, down_bias,
    second_gain, second_shift, group_sizes, sentence_order,
):
    dp = lax.axis_size("dp")
    orders = rows_orders(dp)
    core = lax.axis_index("tensor").astype(jnp.int32)
    dp_index = lax.axis_index("dp").astype(jnp.int32)
    where = jnp.stack([dp_index, core])
    head_cols = query_weight.shape[1]
    hidden_cols = up_weight.shape[1]
    line = lambda vector: vector.reshape(1, -1)

    qkv_a, qkv_b = gather_rows(
        jnp.concatenate([query_weight, key_weight, value_weight], axis=1), QKV_SPLIT
    )
    up_a, up_b = gather_rows(jnp.concatenate([output_weight, up_weight], axis=1), UP_SPLIT)
    down_a, down_b = gather_rows(down_weight, hidden_cols // 2)
    parts = (
        up_a, up_b, swap_cores(up_a), swap_cores(up_b), down_a, down_b, swap_cores(down_a), swap_cores(down_b),
    )

    queries, key_rows, values, context, probs = attention_forward(
        orders, where, tokens, line(query_bias), line(value_bias), qkv_a, qkv_b
    )
    context_other = swap_cores(half_of(context, 1 - core))
    vectors = (
        line(output_bias), line(first_gain), line(first_shift), line(up_bias), line(swap_cores(up_bias)),
        line(down_bias), line(second_gain), line(second_shift),
    )
    hidden_low, normed_one, inv_one, act, slope, normed_two, inv_two, pooled, unit = feed_forward(
        orders, where, tokens, context, context_other, vectors, parts
    )
    pooled = pooled.reshape(-1, D)
    unit_low = unit.reshape(-1, D).astype(bf16)
    if dp == 16:
        units_own, units_other = gather_units(unit_low)
        loss, grad_pooled = pair_gradient(
            orders[0], where, group_sizes, sentence_order, units_own, units_other, pooled
        )
        loss_value = loss[0, 0]
    else:
        units = lax.all_gather(unit_low, ("dp", "tensor"), axis=0, tiled=True)
        loss_value, grad_pooled = pair_objective(units, pooled, group_sizes, sentence_order, dp_index * 2 + core)

    second, ffn_low, down_grad, sums_two = down_gradient(
        orders, where, grad_pooled, normed_two, inv_two, line(second_gain), act
    )
    down_other = swap_cores(down_grad[2:])
    up_grad, up_sums, residual, context_grad_own, context_grad_other, out_grad, sums_one = up_gradient(
        orders, where, second, ffn_low, slope, hidden_low, normed_one, inv_one, line(first_gain),
        context, context_other, parts,
    )
    context_grad = swap_cores(context_grad_other)
    chip_down = add_low(down_grad[:2], down_other)
    shard_down = reduce_rows(chip_down[0], chip_down[1])
    chip_up = add_low(up_grad[:2], swap_cores(up_grad[2:]))
    chip_out = add_low(out_grad[0], swap_cores(out_grad[1]))
    shard_up_out = reduce_rows(
        jnp.concatenate([chip_up[0], chip_out[:, :OUT_SPLIT]], axis=1),
        jnp.concatenate([chip_up[1], chip_out[:, OUT_SPLIT:]], axis=1),
    )
    half = hidden_cols // 2
    shard_up = jnp.concatenate(
        [shard_up_out[:, :half], shard_up_out[:, half + OUT_SPLIT : 2 * half + OUT_SPLIT]], axis=1
    )
    shard_output = jnp.concatenate(
        [shard_up_out[:, half : half + OUT_SPLIT], shard_up_out[:, 2 * half + OUT_SPLIT :]], axis=1
    )

    terms_other, my_grad, grad_a, grad_b, qkv_sums = attention_backward(
        orders, where, tokens, queries, key_rows, values, probs, context_grad, context_grad_own, residual,
        qkv_a, qkv_b,
    )
    shard_qkv = reduce_rows(grad_a, grad_b)
    shard_query = shard_qkv[:, :head_cols]
    shard_key = shard_qkv[:, head_cols : 2 * head_cols]
    shard_value = shard_qkv[:, 2 * head_cols :]
    my_grad = my_grad + swap_cores(terms_other).astype(f32)
    their_grad = swap_cores(my_grad)
    grad_tokens = jnp.concatenate(
        [jnp.where(core == 0, my_grad, their_grad), jnp.where(core == 0, their_grad, my_grad)], axis=0
    )

    sums = jnp.concatenate([sums_two[:3], sums_one[:3]], axis=0)
    sums = sums + swap_cores(sums)
    up_sums = up_sums[:, 0, :]
    up_sums = up_sums[:2] + swap_cores(up_sums[2:])
    early = sum_small(jnp.concatenate([sums, up_sums], axis=0))
    qkv_sums = sum_small(qkv_sums[0])
    return (
        loss_value, grad_tokens, shard_query, shard_key, shard_value, shard_output, shard_up, shard_down,
        qkv_sums[:head_cols], qkv_sums[2 * head_cols :], early[5], early[3], early[4], early[6:8].reshape(-1),
        early[2], early[0], early[1],
    )


def half_of(array, index):
    rows = array.shape[0] // 2
    return lax.dynamic_slice_in_dim(array, index * rows, rows, 0)


def add_low(own, other):
    return (own.astype(f32) + other.astype(f32)).astype(bf16)


QKV_SPLIT = 640
UP_SPLIT = 1024


def solution(mesh):
    placed = (
        P("dp", None),
        P("dp", "tensor"),
        P("dp", "tensor"),
        P("dp", "tensor"),
        P("dp", "tensor"),
        P("dp", "tensor"),
        P("dp", "tensor"),
        P("tensor"),
        P("tensor"),
        P(),
        P(),
        P(),
        P("tensor"),
        P(),
        P(),
        P(),
        P(),
        P(),
    )
    return jax.shard_map(
        local,
        mesh=mesh,
        in_specs=placed,
        out_specs=(
            P(),
            P("dp", None),
            P("dp", "tensor"),
            P("dp", "tensor"),
            P("dp", "tensor"),
            P("dp", "tensor"),
            P("dp", "tensor"),
            P("dp", "tensor"),
            P("tensor"),
            P("tensor"),
            P(),
            P(),
            P(),
            P("tensor"),
            P(),
            P(),
            P(),
        ),
        check_vma=False,
    )
```

time: 973 us -> 421 us (0.43)
  Pallas kernels: 451 us -> 148 us
  matrix products: 173 us -> 0 us
  local copies, waits for them, and re-layouts: 91.1 us -> 35.1 us
  other arithmetic: 53 us -> 17.5 us
  waiting for transfers between devices: 116 us -> 132 us
    pallas_call x8 -> x6, Pallas kernels: 451 us -> 148 us  [the longest x1 34.6 us: attention_backward(): pl.pallas_call(functools.partial(attention_backward_kernel, orders), out_...]
    dot_general x26 -> x0, matrix products: 173 us -> none  [the longest x20 141 us: contract(): lax.dot_general(left, right, (((left_dim,), (right_dim,)), ((), ())), pre...]
    reshape x10 -> x13, local copies, waits for them, and re-layouts: 44.7 us -> 10.1 us  [the longest x10 7.17 us: local(): line = lambda vector: vector.reshape(1, -1)]
    convert_element_type x7 -> x1, local copies, waits for them, and re-layouts: 18.5 us -> 0.01 us  [local(): unit_low = unit.reshape(-1, D).astype(bf16)]
    convert_element_type x11 -> x15, other arithmetic: 23.2 us -> 5.63 us  [the longest x3 3.42 us: add_low(): return (own.astype(f32) + other.astype(f32)).astype(bf16)]
    ppermute x54 -> x60, waiting for transfers between devices: 114 us -> 130 us  [swap_chips(): return lax.ppermute(array, 'dp', [(i, i ^ mask) for i in range(count)])]
    reduce_sum x15 -> x0, other arithmetic: 10.9 us -> none  [the longest x1 2.21 us: local(): grad_down_bias = jnp.sum(grad_second, axis=0)]
    select_n x7 -> x1, other arithmetic: 10.3 us -> 0.41 us  [local(): jnp.where(core == 0, my_grad, their_grad)]
  transfers between devices with their start and end apart: 67 -> 75, of which waited for: 24 -> 37; matrix products, arithmetic and copies ran while one was open for 14% -> 9% of each run, Pallas kernels for 45% -> 16%
where the time goes in v2:
time: 421 us; the launch traced here: 417 us
  Pallas kernels  148 us (35%)
  waiting for transfers between devices  132 us (31%)
  starting transfers between devices  82.7 us (20%)
  local copies, waits for them, and re-layouts  35.1 us (8%)
  other arithmetic  17.5 us (4%)
    ppermute x60, waiting for transfers between devices, swap_chips(): return lax.ppermute(array, 'dp', [(i, i ^ mask) for i in range(count)])  130 us
    ppermute x60, starting transfers between devices, swap_chips(): return lax.ppermute(array, 'dp', [(i, i ^ mask) for i in range(count)])  80.7 us
    pallas_call x1, Pallas kernels, attention_backward(): pl.pallas_call(functools.partial(attention_backward_kernel, orders), out_...  34.6 us
    pallas_call x1, Pallas kernels, up_gradient(): pl.pallas_call(functools.partial(up_gradient_kernel, orders), out_shape=[...  33.9 us
    pallas_call x1, Pallas kernels, feed_forward(): pl.pallas_call(functools.partial(feed_forward_kernel, orders), out_shape=...  32.6 us
    pallas_call x1, Pallas kernels, attention_forward(): pl.pallas_call(functools.partial(attention_forward_kernel, orders), out_s...  30.1 us
    pallas_call x1, Pallas kernels, down_gradient(): pl.pallas_call(functools.partial(down_gradient_kernel, orders), out_shape...  12.3 us
  transfers between devices with their start and end apart: 75, of which 37 were waited for; matrix products, arithmetic and copies ran while one was open for 9% of the time, Pallas kernels for 16%

profile of v2, /device:TPU:0, one launch (start us, length us, event | category | flops | bytes accessed | tf_op | source)
XLA Modules:
  0.0 417.1 jit_solution(14812815085050157484)
XLA Ops:
  3.0 5.0 %collective-permute-start.2 = (bf16[48,1152]{1,0:T(8,128)(2,1)S(1)}, bf16[48,1152]{1,0:T(8,128)(2,1)S(1)}, u32[]{:S(2)}, u32[]{:S(2)}) collective-permute-start(bf16[48,1152]{1,0:T(8,128)(2,1)S(1)} %constant_dynamic-update-slice_fusion), channel_id=1, source_target_pairs={{0,24},{2,26},{4,28},{6,30},{8,16},{10,18},{12,20},{14,22},{16,8},... | collective-permute-start | bytes 331784 | tf_op jit(solution)/shard_map/ppermute | solution.py:51
  8.7 2.3 collective-permute-start.19
  11.0 2.0 collective-permute-start.18
  18.2 3.3 collective-permute-done.1
  21.5 2.6 collective-permute-start.11
  24.2 1.8 collective-permute-start.9
  26.1 9.6 %collective-permute-done.19 = bf16[48,1536]{1,0:T(8,128)(2,1)S(1)} collective-permute-done((bf16[48,1536]{1,0:T(8,128)(2,1)}, bf16[48,1536]{1,0:T(8,128)(2,1)S(1)}, u32[]{:S(2)}, u32[]{:S(2)}) %collective-permute-start.19) | collective-permute-done | bytes 147488 | tf_op jit(solution)/shard_map/ppermute | solution.py:51
  35.7 1.5 collective-permute-start.5
  37.3 1.6 collective-permute-start.3
  39.5 6.4 %collective-permute-done.10 = bf16[48,1920]{1,0:T(8,128)(2,1)S(1)} collective-permute-done((bf16[48,1920]{1,0:T(8,128)(2,1)S(1)}, bf16[48,1920]{1,0:T(8,128)(2,1)S(1)}, u32[]{:S(2)}, u32[]{:S(2)}) %collective-permute-start.10) | collective-permute-done | bytes 184352 | tf_op jit(solution)/shard_map/ppermute | solution.py:51
  47.5 1.6 collective-permute-start.14
  49.6 1.6 collective-permute-start.6
  51.9 3.9 collective-permute-done.21
  55.8 1.5 collective-permute-start.24
  58.5 1.5 collective-permute-start.22
  60.1 4.1 collective-permute-done.12
  64.2 1.5 collective-permute-start.15
  65.8 6.9 %collective-permute-done.6 = bf16[384,512]{1,0:T(8,128)(2,1)S(1)} collective-permute-done((bf16[384,512]{1,0:T(8,128)(2,1)S(1)}, bf16[384,512]{1,0:T(8,128)(2,1)S(1)}, u32[]{:S(2)}, u32[]{:S(2)}) %collective-permute-start.6) | collective-permute-done | bytes 393248 | tf_op jit(solution)/shard_map/ppermute | solution.py:51
  72.6 1.5 collective-permute-start.13
  76.8 4.9 %collective-permute-done.22 = bf16[384,768]{1,0:T(8,128)(2,1)S(1)} collective-permute-done((bf16[384,768]{1,0:T(8,128)(2,1)S(1)}, bf16[384,768]{1,0:T(8,128)(2,1)S(1)}, u32[]{:S(2)}, u32[]{:S(2)}) %collective-permute-start.22) | collective-permute-done | bytes 589856 | tf_op jit(solution)/shard_map/ppermute | solution.py:51
  82.8 2.5 collective-permute-done.24
  86.4 11.8 %collective-permute-done.15 = bf16[384,896]{1,0:T(8,128)(2,1)S(1)} collective-permute-done((bf16[384,896]{1,0:T(8,128)(2,1)S(1)}, bf16[384,896]{1,0:T(8,128)(2,1)S(1)}, u32[]{:S(2)}, u32[]{:S(2)}) %collective-permute-start.15) | collective-permute-done | bytes 688160 | tf_op jit(solution)/shard_map/ppermute | solution.py:51
  99.4 30.1 %attention_forward.1 = (bf16[2048,384]{1,0:T(8,128)(2,1)}, bf16[2048,384]{1,0:T(8,128)(2,1)}, bf16[2048,384]{1,0:T(8,128)(2,1)}, bf16[2048,384]{1,0:T(8,128)(2,1)}, f32[2048,384]{1,0:T(8,128)}) custom-call(s32[2]{0:T(128)} %pad_add_fusion.where_ref, bf16[2048,768]{1,0:T(8,128)(2,1)} %tokens_ref.5, f32[1,384]{1,0:T(1,128)} %reshape.92.query_bias_ref, ...), custom_call_target="tpu_custom_call" | custom-call | flops 7247757312 | bytes 23592960 | tf_op jit(solution)/shard_map/attention_forward/pallas_call | solution.py:196
  137.0 32.6 %feed_forward.1 = (bf16[1024,768]{1,0:T(8,128)(2,1)}, bf16[1024,768]{1,0:T(8,128)(2,1)}, f32[1024,1]{1,0:T(8,128)}, bf16[1024,3072]{1,0:T(8,128)(2,1)}, bf16[102...) custom-call(s32[2]{0:T(128)} %pad_add_fusion.where_ref, ...), custom_call_target="tpu_custom_call" | custom-call | flops 10871635968 | bytes 30000000 | tf_op jit(solution)/shard_map/feed_forward/pallas_call | solution.py:306
  170.4 2.3 collective-permute-start.29
  172.7 2.1 collective-permute-start.27
  174.9 2.0 collective-permute-done.27
  177.5 1.6 collective-permute-start.30
  179.0 1.5 collective-permute-start.32
  181.0 2.0 collective-permute-done.30
  183.0 2.6 collective-permute-done.31
  188.8 4.9 %pair_gradient.1 = (f32[8,128]{1,0:T(8,128)}, f32[16,768]{1,0:T(8,128)}) custom-call(s32[2]{0:T(128)} %pad_add_fusion.where_ref, s32[8]{0:T(128)} %sizes_ref.1, bf16[256,768]{1,0:T(8,128)(2,1)} %copy-done.18, bf16[256,768]{1,0:T(8,128)(2,1)} %copy-done.21, f32[16,768]{1,0:T(8,128)} %reshape.102.pooled_ref, s32[1,512]{1,0:T(1,128)} %bitcast.36, ...), custom_call_target="tpu_custom_call" | custom-call | flops 402653184 | bytes 2000000 | tf_op jit(solution)/shard_map/pair_gradient/pallas_call | solution.py:395
  193.7 12.3 %down_gradient.1 = (f32[1024,768]{1,0:T(8,128)}, bf16[1024,768]{1,0:T(8,128)(2,1)}, bf16[4,768,768]{2,1,0:T(8,128)(2,1)}, f32[8,768]{1,0:T(8,128)}) custom-call(s32[2]{0:T(128)} %pad_add_fusion.where_ref, f32[16,768]{1,0:T(8,128)} %get-tuple-element.57.grad_pooled_ref, bf16[1024,768]{1,0:T(8,128)(2,1)} %get-tuple-element.58.normed_ref, ...), custom_call_target="tpu_custom_call" | custom-call | flops 4831838208 | bytes 20000000 | tf_op jit(solution)/shard_map/down_gradient/pallas_call | solution.py:457
  206.0 33.9 %up_gradient.1 = (bf16[4,768,768]{2,1,0:T(8,128)(2,1)}, f32[4,8,768]{2,1,0:T(8,128)}, f32[1024,768]{1,0:T(8,128)}, bf16[1024,384]{1,0:T(8,128)(2,1)}, bf16[1024,...) custom-call(s32[2]{0:T(128)} %pad_add_fusion.where_ref, ...), custom_call_target="tpu_custom_call" | custom-call | flops 14495514624 | bytes 40000000 | tf_op jit(solution)/shard_map/up_gradient/pallas_call | solution.py:558
  243.4 1.8 collective-permute-start.71
  246.2 1.7 collective-permute-start.69
  250.3 1.6 collective-permute-start.74
  256.1 2.0 slice.268
  259.2 1.6 slice.292
  262.0 1.6 slice_reduce_fusion.1
  263.6 34.6 %attention_backward.1 = (bf16[1024,768]{1,0:T(8,128)(2,1)}, f32[1024,768]{1,0:T(8,128)}, bf16[768,640]{1,0:T(8,128)(2,1)}, bf16[768,512]{1,0:T(8,128)(2,1)}, f32[8,1152]{1,0:T(8,128)}) custom-call(s32[2]{0:T(128)} %pad_add_fusion.where_ref, bf16[2048,768]{1,0:T(8,128)(2,1)} %tokens_ref.5, bf16[2048,384]{1,0:T(8,128)(2,1)} %get-tuple-element.53.query_ref, ...), custom_call_target="tpu_custom_call" | custom-call | flops 7247757312 | bytes 30000000 | tf_op jit(solution)/shard_map/attention_backward/pallas_call | solution.py:667
  299.2 2.2 collective-permute-start.63
  309.2 1.6 collective-permute-start.66
  310.8 4.7 %collective-permute-done.39 = bf16[384,512]{1,0:T(8,128)(2,1)S(1)} collective-permute-done((bf16[384,512]{1,0:T(8,128)(2,1)S(1)}, bf16[384,512]{1,0:T(8,128)(2,1)S(1)}, u32[]{:S(2)}, u32[]{:S(2)}) %collective-permute-start.39) | collective-permute-done | bytes 393248 | tf_op jit(solution)/shard_map/ppermute | solution.py:51
  316.8 3.1 collective-permute-done.37
  323.6 3.1 collective-permute-done.40
  326.7 1.6 collective-permute-done.38
  329.1 1.8 collective-permute-start.43
  332.6 1.8 collective-permute-done.41
  335.8 3.1 collective-permute-done.42
  339.6 2.6 add_convert_fusion
  348.0 10.7 %collective-permute-done.54 = bf16[384,768]{1,0:T(8,128)(2,1)S(1)} collective-permute-done((bf16[384,768]{1,0:T(8,128)(2,1)S(1)}, bf16[384,768]{1,0:T(8,128)(2,1)S(1)}, u32[]{:S(2)}, u32[]{:S(2)}) %collective-permute-start.54) | collective-permute-done | bytes 589856 | tf_op jit(solution)/shard_map/ppermute | solution.py:51
  362.0 10.6 %collective-permute-done.46 = bf16[384,896]{1,0:T(8,128)(2,1)S(1)} collective-permute-done((bf16[384,896]{1,0:T(8,128)(2,1)S(1)}, bf16[384,896]{1,0:T(8,128)(2,1)S(1)}, u32[]{:S(2)}, u32[]{:S(2)}) %collective-permute-start.46) | collective-permute-done | bytes 688160 | tf_op jit(solution)/shard_map/ppermute | solution.py:51
  373.0 3.4 collective-permute-done.48
  378.9 3.8 collective-permute-done.55
  382.9 2.2 collective-permute-start.60
  385.1 1.6 collective-permute-done.47
  387.0 2.7 collective-permute-start.50
  389.7 2.0 collective-permute-done.58
  391.8 3.0 collective-permute-start.52
  394.8 3.0 collective-permute-start.51
  397.8 8.2 %collective-permute-done.59 = bf16[48,1536]{1,0:T(8,128)(2,1)S(1)} collective-permute-done((bf16[48,1536]{1,0:T(8,128)(2,1)S(1)}, bf16[48,1536]{1,0:T(8,128)(2,1)S(1)}, u32[]{:S(2)}, u32[]{:S(2)}) %collective-permute-start.59) | collective-permute-done | bytes 147488 | tf_op jit(solution)/shard_map/ppermute | solution.py:51
  406.8 5.0 %collective-permute-done.51 = bf16[48,1920]{1,0:T(8,128)(2,1)S(1)} collective-permute-done((bf16[48,1920]{1,0:T(8,128)(2,1)S(1)}, bf16[48,1920]{1,0:T(8,128)(2,1)S(1)}, u32[]{:S(2)}, u32[]{:S(2)}) %collective-permute-start.51) | collective-permute-done | bytes 184352 | tf_op jit(solution)/shard_map/ppermute | solution.py:51
  413.7 3.1 pad_maximum_fusion
  (256 shorter events, 78.4 us)
Async XLA Ops:
  3.0 15.2 %collective-permute-start.2 = (bf16[48,1152]{1,0:T(8,128)(2,1)S(1)}, bf16[48,1152]{1,0:T(8,128)(2,1)S(1)}, u32[]{:S(2)}, u32[]{:S(2)}) collective-permute-start(bf16[48,1152]{1,0:T(8,128)(2,1)S(1)} %constant_dynamic-update-slice_fusion), channel_id=1, source_target_pairs={{0,24},{2,26},{4,28},{6,30},{8,16},{10,18},{12,20},{14,22},{16,8},... | collective-permute-start | bytes 331784 | tf_op jit(solution)/shard_map/ppermute | solution.py:51
  8.0 13.5 %collective-permute-start.1 = (bf16[48,1152]{1,0:T(8,128)(2,1)S(1)}, bf16[48,1152]{1,0:T(8,128)(2,1)S(1)}, u32[]{:S(2)}, u32[]{:S(2)}) collective-permute-start(bf16[48,1152]{1,0:T(8,128)(2,1)S(1)} %constant_dynamic-update-slice_fusion), channel_id=1, source_target_pairs={{0,16},{2,18},{4,20},{6,22},{8,24},{10,26},{12,28},{14,30},{16,0},... | collective-permute-start | bytes 331784 | tf_op jit(solution)/shard_map/ppermute | solution.py:51
  8.0 16.1 %collective-permute-start = (bf16[48,1152]{1,0:T(8,128)(2,1)S(1)}, bf16[48,1152]{1,0:T(8,128)(2,1)S(1)}, u32[]{:S(2)}, u32[]{:S(2)}) collective-permute-start(bf16[48,1152]{1,0:T(8,128)(2,1)S(1)} %constant_dynamic-update-slice_fusion), channel_id=1, source_target_pairs={{0,8},{2,10},{4,12},{6,14},{8,0},{10,2},{12,4},{14,6},{16,24},{18,... | collective-permute-start | bytes 331784 | tf_op jit(solution)/shard_map/ppermute | solution.py:51
  8.7 27.1 %collective-permute-start.19 = (bf16[48,1536]{1,0:T(8,128)(2,1)}, bf16[48,1536]{1,0:T(8,128)(2,1)S(1)}, u32[]{:S(2)}, u32[]{:S(2)}) collective-permute-start(bf16[48,1536]{1,0:T(8,128)(2,1)} %param.24), channel_id=1, source_target_pairs={{0,16},{2,18},{4,20},{6,22},{8,24},{10,26},{12,28},{14,30},{16,0},... | collective-permute-start | bytes 442376 | tf_op jit(solution)/shard_map/ppermute | solution.py:51
  11.0 13.3 %collective-permute-start.18 = (bf16[48,1536]{1,0:T(8,128)(2,1)}, bf16[48,1536]{1,0:T(8,128)(2,1)S(1)}, u32[]{:S(2)}, u32[]{:S(2)}) collective-permute-start(bf16[48,1536]{1,0:T(8,128)(2,1)} %param.24), channel_id=1, source_target_pairs={{0,8},{2,10},{4,12},{6,14},{8,0},{10,2},{12,4},{14,6},{16,24},{18,... | collective-permute-start | bytes 442376 | tf_op jit(solution)/shard_map/ppermute | solution.py:51
  18.1 19.1 %collective-permute-start.20 = (bf16[48,1536]{1,0:T(8,128)(2,1)}, bf16[48,1536]{1,0:T(8,128)(2,1)S(1)}, u32[]{:S(2)}, u32[]{:S(2)}) collective-permute-start(bf16[48,1536]{1,0:T(8,128)(2,1)} %param.24), channel_id=1, source_target_pairs={{0,24},{2,26},{4,28},{6,30},{8,16},{10,18},{12,20},{14,22},{16,8},... | collective-permute-start | bytes 442376 | tf_op jit(solution)/shard_map/ppermute | solution.py:51
  21.5 17.4 %collective-permute-start.11 = (bf16[48,1920]{1,0:T(8,128)(2,1)S(1)}, bf16[48,1920]{1,0:T(8,128)(2,1)S(1)}, u32[]{:S(2)}, u32[]{:S(2)}) collective-permute-start(bf16[48,1920]{1,0:T(8,128)(2,1)S(1)} %constant_dynamic-update-slice_fusion.3), channel_id=1, source_target_pairs={{0,24},{2,26},{4,28},{6,30},{8,16},{10,18},{12,20},{14,22},{16,8},... | collective-permute-start | bytes 552968 | tf_op jit(solution)/shard_map/ppermute | solution.py:51
  24.1 21.7 %collective-permute-start.10 = (bf16[48,1920]{1,0:T(8,128)(2,1)S(1)}, bf16[48,1920]{1,0:T(8,128)(2,1)S(1)}, u32[]{:S(2)}, u32[]{:S(2)}) collective-permute-start(bf16[48,1920]{1,0:T(8,128)(2,1)S(1)} %constant_dynamic-update-slice_fusion.3), channel_id=1, source_target_pairs={{0,16},{2,18},{4,20},{6,22},{8,24},{10,26},{12,28},{14,30},{16,0},... | collective-permute-start | bytes 552968 | tf_op jit(solution)/shard_map/ppermute | solution.py:51
  24.2 23.1 %collective-permute-start.9 = (bf16[48,1920]{1,0:T(8,128)(2,1)S(1)}, bf16[48,1920]{1,0:T(8,128)(2,1)S(1)}, u32[]{:S(2)}, u32[]{:S(2)}) collective-permute-start(bf16[48,1920]{1,0:T(8,128)(2,1)S(1)} %constant_dynamic-update-slice_fusion.3), channel_id=1, source_target_pairs={{0,8},{2,10},{4,12},{6,14},{8,0},{10,2},{12,4},{14,6},{16,24},{18,... | collective-permute-start | bytes 552968 | tf_op jit(solution)/shard_map/ppermute | solution.py:51
  35.7 13.3 %collective-permute-start.5 = (bf16[192,512]{1,0:T(8,128)(2,1)S(1)}, bf16[192,512]{1,0:T(8,128)(2,1)S(1)}, u32[]{:S(2)}, u32[]{:S(2)}) collective-permute-start(bf16[192,512]{1,0:T(8,128)(2,1)S(1)} %pad_maximum_fusion.19), channel_id=1, source_target_pairs={{0,4},{2,6},{4,0},{6,2},{8,12},{10,14},{12,8},{14,10},{16,20},{18,... | collective-permute-start | bytes 589832 | tf_op jit(solution)/shard_map/ppermute | solution.py:51
  37.3 12.3 %collective-permute-start.3 = (bf16[192,640]{1,0:T(8,128)(2,1)S(1)}, bf16[192,640]{1,0:T(8,128)(2,1)S(1)}, u32[]{:S(2)}, u32[]{:S(2)}) collective-permute-start(bf16[192,640]{1,0:T(8,128)(2,1)S(1)} %slice.323), channel_id=1, source_target_pairs={{0,2},{2,0},{4,6},{6,4},{8,10},{10,8},{12,14},{14,12},{16,18},{18,... | collective-permute-start | bytes 737288 | tf_op jit(solution)/shard_map/ppermute | solution.py:51
  38.9 12.3 %collective-permute-start.23 = (bf16[192,768]{1,0:T(8,128)(2,1)S(1)}, bf16[192,768]{1,0:T(8,128)(2,1)S(1)}, u32[]{:S(2)}, u32[]{:S(2)}) collective-permute-start(bf16[192,768]{1,0:T(8,128)(2,1)S(1)} %get-tuple-element.101), channel_id=1, source_target_pairs={{0,4},{2,6},{4,0},{6,2},{8,12},{10,14},{12,8},{14,10},{16,20},{18,... | collective-permute-start | bytes 884744 | tf_op jit(solution)/shard_map/ppermute | solution.py:51
  45.8 9.9 %collective-permute-start.21 = (bf16[192,768]{1,0:T(8,128)(2,1)S(1)}, bf16[192,768]{1,0:T(8,128)(2,1)S(1)}, u32[]{:S(2)}, u32[]{:S(2)}) collective-permute-start(bf16[192,768]{1,0:T(8,128)(2,1)S(1)} %get-tuple-element.102), channel_id=1, source_target_pairs={{0,2},{2,0},{4,6},{6,4},{8,10},{10,8},{12,14},{14,12},{16,18},{18,... | collective-permute-start | bytes 884744 | tf_op jit(solution)/shard_map/ppermute | solution.py:51
  47.5 11.1 %collective-permute-start.14 = (bf16[192,896]{1,0:T(8,128)(2,1)S(1)}, bf16[192,896]{1,0:T(8,128)(2,1)S(1)}, u32[]{:S(2)}, u32[]{:S(2)}) collective-permute-start(bf16[192,896]{1,0:T(8,128)(2,1)S(1)} %pad_maximum_fusion.17), channel_id=1, source_target_pairs={{0,4},{2,6},{4,0},{6,2},{8,12},{10,14},{12,8},{14,10},{16,20},{18,... | collective-permute-start | bytes 1032200 | tf_op jit(solution)/shard_map/ppermute | solution.py:51
  49.1 15.1 %collective-permute-start.12 = (bf16[192,1024]{1,0:T(8,128)(2,1)S(1)}, bf16[192,1024]{1,0:T(8,128)(2,1)S(1)}, u32[]{:S(2)}, u32[]{:S(2)}) collective-permute-start(bf16[192,1024]{1,0:T(8,128)(2,1)S(1)} %slice.324), channel_id=1, source_target_pairs={{0,2},{2,0},{4,6},{6,4},{8,10},{10,8},{12,14},{14,12},{16,18},{18,... | collective-permute-start | bytes 1179656 | tf_op jit(solution)/shard_map/ppermute | solution.py:51
  49.6 23.0 %collective-permute-start.6 = (bf16[384,512]{1,0:T(8,128)(2,1)S(1)}, bf16[384,512]{1,0:T(8,128)(2,1)S(1)}, u32[]{:S(2)}, u32[]{:S(2)}) collective-permute-start(bf16[384,512]{1,0:T(8,128)(2,1)S(1)} %pad_maximum_fusion.16), channel_id=1, source_target_pairs={{0,2},{2,0},{4,6},{6,4},{8,10},{10,8},{12,14},{14,12},{16,18},{18,... | collective-permute-start | bytes 1179656 | tf_op jit(solution)/shard_map/ppermute | solution.py:51
  51.3 24.5 %collective-permute-start.4 = (bf16[384,640]{1,0:T(8,128)(2,1)S(1)}, bf16[384,640]{1,0:T(8,128)(2,1)S(1)}, u32[]{:S(2)}, u32[]{:S(2)}) collective-permute-start(bf16[384,640]{1,0:T(8,128)(2,1)S(1)} %pad_maximum_fusion.14), channel_id=1, source_target_pairs={{0,4},{2,6},{4,0},{6,2},{8,12},{10,14},{12,8},{14,10},{16,20},{18,... | collective-permute-start | bytes 1474568 | tf_op jit(solution)/shard_map/ppermute | solution.py:51
  55.8 29.5 %collective-permute-start.24 = (bf16[384,768]{1,0:T(8,128)(2,1)S(1)}, bf16[384,768]{1,0:T(8,128)(2,1)S(1)}, u32[]{:S(2)}, u32[]{:S(2)}) collective-permute-start(bf16[384,768]{1,0:T(8,128)(2,1)S(1)} %pad_maximum_fusion.13), channel_id=1, source_target_pairs={{0,2},{2,0},{4,6},{6,4},{8,10},{10,8},{12,14},{14,12},{16,18},{18,... | collective-permute-start | bytes 1769480 | tf_op jit(solution)/shard_map/ppermute | solution.py:51
  58.5 23.2 %collective-permute-start.22 = (bf16[384,768]{1,0:T(8,128)(2,1)S(1)}, bf16[384,768]{1,0:T(8,128)(2,1)S(1)}, u32[]{:S(2)}, u32[]{:S(2)}) collective-permute-start(bf16[384,768]{1,0:T(8,128)(2,1)S(1)} %pad_maximum_fusion.12), channel_id=1, source_target_pairs={{0,4},{2,6},{4,0},{6,2},{8,12},{10,14},{12,8},{14,10},{16,20},{18,... | collective-permute-start | bytes 1769480 | tf_op jit(solution)/shard_map/ppermute | solution.py:51
  64.2 33.9 %collective-permute-start.15 = (bf16[384,896]{1,0:T(8,128)(2,1)S(1)}, bf16[384,896]{1,0:T(8,128)(2,1)S(1)}, u32[]{:S(2)}, u32[]{:S(2)}) collective-permute-start(bf16[384,896]{1,0:T(8,128)(2,1)S(1)} %pad_maximum_fusion.11), channel_id=1, source_target_pairs={{0,2},{2,0},{4,6},{6,4},{8,10},{10,8},{12,14},{14,12},{16,18},{18,... | collective-permute-start | bytes 2064392 | tf_op jit(solution)/shard_map/ppermute | solution.py:51
  72.6 25.7 %collective-permute-start.13 = (bf16[384,1024]{1,0:T(8,128)(2,1)S(1)}, bf16[384,1024]{1,0:T(8,128)(2,1)S(1)}, u32[]{:S(2)}, u32[]{:S(2)}) collective-permute-start(bf16[384,1024]{1,0:T(8,128)(2,1)S(1)} %pad_maximum_fusion.8), channel_id=1, source_target_pairs={{0,4},{2,6},{4,0},{6,2},{8,12},{10,14},{12,8},{14,10},{16,20},{18,... | collective-permute-start | bytes 2359304 | tf_op jit(solution)/shard_map/ppermute | solution.py:51
  75.7 55.1 %collective-permute-start.8 = (f32[1536]{0:T(1024)S(1)}, f32[1536]{0:T(1024)S(1)}, u32[]{:S(2)}, u32[]{:S(2)}) collective-permute-start(f32[1536]{0:T(1024)S(1)} %copy-done.9), channel_id=1, source_target_pairs={{0,1},{1,0},{2,3},{3,2},{4,5},{5,4},{6,7},{7,6},{8,9},{9,8},{10,11... | collective-permute-start | bytes 18440 | tf_op jit(solution)/shard_map/ppermute | solution.py:46
  82.8 53.3 %collective-permute-start.25 = (bf16[768,768]{1,0:T(8,128)(2,1)}, bf16[768,768]{1,0:T(8,128)(2,1)}, u32[]{:S(2)}, u32[]{:S(2)}) collective-permute-start(bf16[768,768]{1,0:T(8,128)(2,1)} %pad_maximum_fusion.3.down_own_a), channel_id=1, source_target_pairs={{0,1},{1,0},{2,3},{3,2},{4,5},{5,4},{6,7},{7,6},{8,9},{9,8},{10,11... | collective-permute-start | bytes 3538952 | tf_op jit(solution)/shard_map/ppermute | solution.py:46
  86.4 49.7 %collective-permute-start.26 = (bf16[768,768]{1,0:T(8,128)(2,1)}, bf16[768,768]{1,0:T(8,128)(2,1)}, u32[]{:S(2)}, u32[]{:S(2)}) collective-permute-start(bf16[768,768]{1,0:T(8,128)(2,1)} %pad_maximum_fusion.4.down_own_b), channel_id=1, source_target_pairs={{0,1},{1,0},{2,3},{3,2},{4,5},{5,4},{6,7},{7,6},{8,9},{9,8},{10,11... | collective-permute-start | bytes 3538952 | tf_op jit(solution)/shard_map/ppermute | solution.py:46
  98.3 37.9 %collective-permute-start.17 = (bf16[768,896]{1,0:T(8,128)(2,1)S(1)}, bf16[768,896]{1,0:T(8,128)(2,1)}, u32[]{:S(2)}, u32[]{:S(2)}) collective-permute-start(bf16[768,896]{1,0:T(8,128)(2,1)S(1)} %pad_maximum_fusion.2.up_own_b), channel_id=1, source_target_pairs={{0,1},{1,0},{2,3},{3,2},{4,5},{5,4},{6,7},{7,6},{8,9},{9,8},{10,11... | collective-permute-start | bytes 4128776 | tf_op jit(solution)/shard_map/ppermute | solution.py:46
  99.4 36.8 %collective-permute-start.16 = (bf16[768,1024]{1,0:T(8,128)(2,1)S(1)}, bf16[768,1024]{1,0:T(8,128)(2,1)}, u32[]{:S(2)}, u32[]{:S(2)}) collective-permute-start(bf16[768,1024]{1,0:T(8,128)(2,1)S(1)} %pad_maximum_fusion.1.up_own_a), channel_id=1, source_target_pairs={{0,1},{1,0},{2,3},{3,2},{4,5},{5,4},{6,7},{7,6},{8,9},{9,8},{10,11... | collective-permute-start | bytes 4718600 | tf_op jit(solution)/shard_map/ppermute | solution.py:46
  170.4 7.1 %collective-permute-start.29 = (bf16[16,768]{1,0:T(8,128)(2,1)S(1)}, bf16[16,768]{1,0:T(8,128)(2,1)S(1)}, u32[]{:S(2)}, u32[]{:S(2)}) collective-permute-start(bf16[16,768]{1,0:T(8,128)(2,1)S(1)} %convert_element_type.190), channel_id=1, source_target_pairs={{0,24},{2,26},{4,28},{6,30},{8,16},{10,18},{12,20},{14,22},{16,8},... | collective-permute-start | bytes 73736 | tf_op jit(solution)/shard_map/ppermute | solution.py:51
  179.0 6.6 %collective-permute-start.32 = (bf16[64,768]{1,0:T(8,128)(2,1)S(1)}, bf16[64,768]{1,0:T(8,128)(2,1)S(1)}, u32[]{:S(2)}, u32[]{:S(2)}) collective-permute-start(bf16[64,768]{1,0:T(8,128)(2,1)S(1)} %get-tuple-element.111), channel_id=1, source_target_pairs={{0,6},{2,4},{4,2},{6,0},{8,14},{10,12},{12,10},{14,8},{16,22},{18,... | collective-permute-start | bytes 294920 | tf_op jit(solution)/shard_map/ppermute | solution.py:51
  243.4 5.9 %collective-permute-start.71 = (f32[8,768]{1,0:T(8,128)S(1)}, f32[8,768]{1,0:T(8,128)S(1)}, u32[]{:S(2)}, u32[]{:S(2)}) collective-permute-start(f32[8,768]{1,0:T(8,128)S(1)} %pad_maximum_fusion.25), channel_id=1, source_target_pairs={{0,24},{2,26},{4,28},{6,30},{8,16},{10,18},{12,20},{14,22},{16,8},... | collective-permute-start | bytes 73736 | tf_op jit(solution)/shard_map/ppermute | solution.py:51
  247.9 15.8 %collective-permute-start.34 = (bf16[1024,384]{1,0:T(8,128)(2,1)}, bf16[1024,384]{1,0:T(8,128)(2,1)}, u32[]{:S(2)}, u32[]{:S(2)}) collective-permute-start(bf16[1024,384]{1,0:T(8,128)(2,1)} %get-tuple-element.67), channel_id=1, source_target_pairs={{0,1},{1,0},{2,3},{3,2},{4,5},{5,4},{6,7},{7,6},{8,9},{9,8},{10,11... | collective-permute-start | bytes 2359304 | tf_op jit(solution)/shard_map/ppermute | solution.py:46
  250.3 10.5 %collective-permute-start.74 = (f32[8,768]{1,0:T(8,128)S(1)}, f32[8,768]{1,0:T(8,128)S(1)}, u32[]{:S(2)}, u32[]{:S(2)}) collective-permute-start(f32[8,768]{1,0:T(8,128)S(1)} %add_add_fusion.1), channel_id=1, source_target_pairs={{0,6},{2,4},{4,2},{6,0},{8,14},{10,12},{12,10},{14,8},{16,22},{18,... | collective-permute-start | bytes 73736 | tf_op jit(solution)/shard_map/ppermute | solution.py:51
  251.8 9.0 %collective-permute-start.73 = (f32[8,768]{1,0:T(8,128)S(1)}, f32[8,768]{1,0:T(8,128)S(1)}, u32[]{:S(2)}, u32[]{:S(2)}) collective-permute-start(f32[8,768]{1,0:T(8,128)S(1)} %add_add_fusion.1), channel_id=1, source_target_pairs={{0,4},{2,6},{4,0},{6,2},{8,12},{10,14},{12,8},{14,10},{16,20},{18,... | collective-permute-start | bytes 73736 | tf_op jit(solution)/shard_map/ppermute | solution.py:51
  252.9 7.9 %collective-permute-start.72 = (f32[8,768]{1,0:T(8,128)S(1)}, f32[8,768]{1,0:T(8,128)S(1)}, u32[]{:S(2)}, u32[]{:S(2)}) collective-permute-start(f32[8,768]{1,0:T(8,128)S(1)} %add_add_fusion.1), channel_id=1, source_target_pairs={{0,2},{2,0},{4,6},{6,4},{8,10},{10,8},{12,14},{14,12},{16,18},{18,... | collective-permute-start | bytes 73736 | tf_op jit(solution)/shard_map/ppermute | solution.py:51
  256.1 50.9 %collective-permute-start.45 = (bf16[768,384]{1,0:T(8,128)(2,1)S(1)}, bf16[768,384]{1,0:T(8,128)(2,1)S(1)}, u32[]{:S(2)}, u32[]{:S(2)}) collective-permute-start(bf16[768,384]{1,0:T(8,128)(2,1)S(1)} %slice_bitcast_fusion.6), channel_id=1, source_target_pairs={{0,1},{1,0},{2,3},{3,2},{4,5},{5,4},{6,7},{7,6},{8,9},{9,8},{10,11... | collective-permute-start | bytes 1769480 | tf_op jit(solution)/shard_map/ppermute | solution.py:46
  299.2 9.1 %collective-permute-start.63 = (f32[1152]{0:T(1024)S(1)}, f32[1152]{0:T(1024)S(1)}, u32[]{:S(2)}, u32[]{:S(2)}) collective-permute-start(f32[1152]{0:T(1024)S(1)} %slice_reduce_fusion), channel_id=1, source_target_pairs={{0,24},{2,26},{4,28},{6,30},{8,16},{10,18},{12,20},{14,22},{16,8},... | collective-permute-start | bytes 13832 | tf_op jit(solution)/shard_map/ppermute | solution.py:51
  301.4 7.3 %collective-permute-start.62 = (f32[1152]{0:T(1024)S(1)}, f32[1152]{0:T(1024)S(1)}, u32[]{:S(2)}, u32[]{:S(2)}) collective-permute-start(f32[1152]{0:T(1024)S(1)} %slice_reduce_fusion), channel_id=1, source_target_pairs={{0,16},{2,18},{4,20},{6,22},{8,24},{10,26},{12,28},{14,30},{16,0},... | collective-permute-start | bytes 13832 | tf_op jit(solution)/shard_map/ppermute | solution.py:51
  302.2 7.0 %collective-permute-start.61 = (f32[1152]{0:T(1024)S(1)}, f32[1152]{0:T(1024)S(1)}, u32[]{:S(2)}, u32[]{:S(2)}) collective-permute-start(f32[1152]{0:T(1024)S(1)} %slice_reduce_fusion), channel_id=1, source_target_pairs={{0,8},{2,10},{4,12},{6,14},{8,0},{10,2},{12,4},{14,6},{16,24},{18,... | collective-permute-start | bytes 13832 | tf_op jit(solution)/shard_map/ppermute | solution.py:51
  304.7 10.8 %collective-permute-start.39 = (bf16[384,512]{1,0:T(8,128)(2,1)S(1)}, bf16[384,512]{1,0:T(8,128)(2,1)S(1)}, u32[]{:S(2)}, u32[]{:S(2)}) collective-permute-start(bf16[384,512]{1,0:T(8,128)(2,1)S(1)} %slice.257), channel_id=1, source_target_pairs={{0,2},{2,0},{4,6},{6,4},{8,10},{10,8},{12,14},{14,12},{16,18},{18,... | collective-permute-start | bytes 1179656 | tf_op jit(solution)/shard_map/ppermute | solution.py:51
  307.0 12.8 %collective-permute-start.37 = (bf16[384,640]{1,0:T(8,128)(2,1)S(1)}, bf16[384,640]{1,0:T(8,128)(2,1)S(1)}, u32[]{:S(2)}, u32[]{:S(2)}) collective-permute-start(bf16[384,640]{1,0:T(8,128)(2,1)S(1)} %slice.253), channel_id=1, source_target_pairs={{0,4},{2,6},{4,0},{6,2},{8,12},{10,14},{12,8},{14,10},{16,20},{18,... | collective-permute-start | bytes 1474568 | tf_op jit(solution)/shard_map/ppermute | solution.py:51
  308.7 30.9 %collective-permute-start.53 = (bf16[2,768,768]{2,1,0:T(8,128)(2,1)S(1)}, bf16[2,768,768]{2,1,0:T(8,128)(2,1)S(1)}, u32[]{:S(2)}, u32[]{:S(2)}) collective-permute-start(bf16[2,768,768]{2,1,0:T(8,128)(2,1)S(1)} %copy-done.2), channel_id=1, source_target_pairs={{0,1},{1,0},{2,3},{3,2},{4,5},{5,4},{6,7},{7,6},{8,9},{9,8},{10,11... | collective-permute-start | bytes 7077896 | tf_op jit(solution)/shard_map/ppermute | solution.py:46
  308.7 35.7 %collective-permute-start.44 = (bf16[2,768,768]{2,1,0:T(8,128)(2,1)S(1)}, bf16[2,768,768]{2,1,0:T(8,128)(2,1)S(1)}, u32[]{:S(2)}, u32[]{:S(2)}) collective-permute-start(bf16[2,768,768]{2,1,0:T(8,128)(2,1)S(1)} %slice.268), channel_id=1, source_target_pairs={{0,1},{1,0},{2,3},{3,2},{4,5},{5,4},{6,7},{7,6},{8,9},{9,8},{10,11... | collective-permute-start | bytes 7077896 | tf_op jit(solution)/shard_map/ppermute | solution.py:46
  309.2 11.7 %collective-permute-start.66 = (f32[1152]{0:T(1024)S(1)}, f32[1152]{0:T(1024)S(1)}, u32[]{:S(2)}, u32[]{:S(2)}) collective-permute-start(f32[1152]{0:T(1024)S(1)} %add_add_fusion.3), channel_id=1, source_target_pairs={{0,6},{2,4},{4,2},{6,0},{8,14},{10,12},{12,10},{14,8},{16,22},{18,... | collective-permute-start | bytes 13832 | tf_op jit(solution)/shard_map/ppermute | solution.py:51
  315.5 6.7 %collective-permute-start.65 = (f32[1152]{0:T(1024)S(1)}, f32[1152]{0:T(1024)S(1)}, u32[]{:S(2)}, u32[]{:S(2)}) collective-permute-start(f32[1152]{0:T(1024)S(1)} %add_add_fusion.3), channel_id=1, source_target_pairs={{0,4},{2,6},{4,0},{6,2},{8,12},{10,14},{12,8},{14,10},{16,20},{18,... | collective-permute-start | bytes 13832 | tf_op jit(solution)/shard_map/ppermute | solution.py:51
  320.9 5.7 %collective-permute-start.40 = (bf16[192,512]{1,0:T(8,128)(2,1)S(1)}, bf16[192,512]{1,0:T(8,128)(2,1)S(1)}, u32[]{:S(2)}, u32[]{:S(2)}) collective-permute-start(bf16[192,512]{1,0:T(8,128)(2,1)S(1)} %slice.330), channel_id=1, source_target_pairs={{0,4},{2,6},{4,0},{6,2},{8,12},{10,14},{12,8},{14,10},{16,20},{18,... | collective-permute-start | bytes 589832 | tf_op jit(solution)/shard_map/ppermute | solution.py:51
  322.2 6.2 %collective-permute-start.38 = (bf16[192,640]{1,0:T(8,128)(2,1)S(1)}, bf16[192,640]{1,0:T(8,128)(2,1)S(1)}, u32[]{:S(2)}, u32[]{:S(2)}) collective-permute-start(bf16[192,640]{1,0:T(8,128)(2,1)S(1)} %slice.328), channel_id=1, source_target_pairs={{0,2},{2,0},{4,6},{6,4},{8,10},{10,8},{12,14},{14,12},{16,18},{18,... | collective-permute-start | bytes 737288 | tf_op jit(solution)/shard_map/ppermute | solution.py:51
  328.5 5.9 %collective-permute-start.41 = (bf16[48,1152]{1,0:T(8,128)(2,1)S(1)}, bf16[48,1152]{1,0:T(8,128)(2,1)S(1)}, u32[]{:S(2)}, u32[]{:S(2)}) collective-permute-start(bf16[48,1152]{1,0:T(8,128)(2,1)S(1)} %get-tuple-element.103), channel_id=1, source_target_pairs={{0,8},{2,10},{4,12},{6,14},{8,0},{10,2},{12,4},{14,6},{16,24},{18,... | collective-permute-start | bytes 331784 | tf_op jit(solution)/shard_map/ppermute | solution.py:51
  329.1 6.6 %collective-permute-start.43 = (bf16[48,1152]{1,0:T(8,128)(2,1)S(1)}, bf16[48,1152]{1,0:T(8,128)(2,1)S(1)}, u32[]{:S(2)}, u32[]{:S(2)}) collective-permute-start(bf16[48,1152]{1,0:T(8,128)(2,1)S(1)} %get-tuple-element.104), channel_id=1, source_target_pairs={{0,24},{2,26},{4,28},{6,30},{8,16},{10,18},{12,20},{14,22},{16,8},... | collective-permute-start | bytes 331784 | tf_op jit(solution)/shard_map/ppermute | solution.py:51
  330.9 7.9 %collective-permute-start.42 = (bf16[48,1152]{1,0:T(8,128)(2,1)S(1)}, bf16[48,1152]{1,0:T(8,128)(2,1)S(1)}, u32[]{:S(2)}, u32[]{:S(2)}) collective-permute-start(bf16[48,1152]{1,0:T(8,128)(2,1)S(1)} %get-tuple-element.105), channel_id=1, source_target_pairs={{0,16},{2,18},{4,20},{6,22},{8,24},{10,26},{12,28},{14,30},{16,0},... | collective-permute-start | bytes 331784 | tf_op jit(solution)/shard_map/ppermute | solution.py:51
  334.4 13.2 %collective-permute-start.35 = (bf16[1024,768]{1,0:T(8,128)(2,1)S(1)}, bf16[1024,768]{1,0:T(8,128)(2,1)S(1)}, u32[]{:S(2)}, u32[]{:S(2)}) collective-permute-start(bf16[1024,768]{1,0:T(8,128)(2,1)S(1)} %copy-done.19), channel_id=1, source_target_pairs={{0,1},{1,0},{2,3},{3,2},{4,5},{5,4},{6,7},{7,6},{8,9},{9,8},{10,11... | collective-permute-start | bytes 4718600 | tf_op jit(solution)/shard_map/ppermute | solution.py:46
  342.3 16.3 %collective-permute-start.54 = (bf16[384,768]{1,0:T(8,128)(2,1)S(1)}, bf16[384,768]{1,0:T(8,128)(2,1)S(1)}, u32[]{:S(2)}, u32[]{:S(2)}) collective-permute-start(bf16[384,768]{1,0:T(8,128)(2,1)S(1)} %get-tuple-element.91), channel_id=1, source_target_pairs={{0,4},{2,6},{4,0},{6,2},{8,12},{10,14},{12,8},{14,10},{16,20},{18,... | collective-permute-start | bytes 1769480 | tf_op jit(solution)/shard_map/ppermute | solution.py:51
  343.3 16.3 %collective-permute-start.56 = (bf16[384,768]{1,0:T(8,128)(2,1)S(1)}, bf16[384,768]{1,0:T(8,128)(2,1)S(1)}, u32[]{:S(2)}, u32[]{:S(2)}) collective-permute-start(bf16[384,768]{1,0:T(8,128)(2,1)S(1)} %get-tuple-element.92), channel_id=1, source_target_pairs={{0,2},{2,0},{4,6},{6,4},{8,10},{10,8},{12,14},{14,12},{16,18},{18,... | collective-permute-start | bytes 1769480 | tf_op jit(solution)/shard_map/ppermute | solution.py:51
  345.3 27.3 %collective-permute-start.46 = (bf16[384,896]{1,0:T(8,128)(2,1)S(1)}, bf16[384,896]{1,0:T(8,128)(2,1)S(1)}, u32[]{:S(2)}, u32[]{:S(2)}) collective-permute-start(bf16[384,896]{1,0:T(8,128)(2,1)S(1)} %pad_maximum_fusion.10), channel_id=1, source_target_pairs={{0,4},{2,6},{4,0},{6,2},{8,12},{10,14},{12,8},{14,10},{16,20},{18,... | collective-permute-start | bytes 2064392 | tf_op jit(solution)/shard_map/ppermute | solution.py:51
  346.4 30.0 %collective-permute-start.48 = (bf16[384,1024]{1,0:T(8,128)(2,1)S(1)}, bf16[384,1024]{1,0:T(8,128)(2,1)S(1)}, u32[]{:S(2)}, u32[]{:S(2)}) collective-permute-start(bf16[384,1024]{1,0:T(8,128)(2,1)S(1)} %pad_maximum_fusion.6), channel_id=1, source_target_pairs={{0,2},{2,0},{4,6},{6,4},{8,10},{10,8},{12,14},{14,12},{16,18},{18,... | collective-permute-start | bytes 2359304 | tf_op jit(solution)/shard_map/ppermute | solution.py:51
  347.9 65.4 %collective-permute-start.36 = (f32[1024,768]{1,0:T(8,128)S(1)}, f32[1024,768]{1,0:T(8,128)S(1)}, u32[]{:S(2)}, u32[]{:S(2)}) collective-permute-start(f32[1024,768]{1,0:T(8,128)S(1)} %convert_add_fusion), channel_id=1, source_target_pairs={{0,1},{1,0},{2,3},{3,2},{4,5},{5,4},{6,7},{7,6},{8,9},{9,8},{10,11... | collective-permute-start | bytes 9437192 | tf_op jit(solution)/shard_map/ppermute | solution.py:46
  359.9 18.9 %collective-permute-start.57 = (bf16[192,768]{1,0:T(8,128)(2,1)S(1)}, bf16[192,768]{1,0:T(8,128)(2,1)S(1)}, u32[]{:S(2)}, u32[]{:S(2)}) collective-permute-start(bf16[192,768]{1,0:T(8,128)(2,1)S(1)} %slice.369), channel_id=1, source_target_pairs={{0,4},{2,6},{4,0},{6,2},{8,12},{10,14},{12,8},{14,10},{16,20},{18,... | collective-permute-start | bytes 884744 | tf_op jit(solution)/shard_map/ppermute | solution.py:51
  361.1 21.6 %collective-permute-start.55 = (bf16[192,768]{1,0:T(8,128)(2,1)S(1)}, bf16[192,768]{1,0:T(8,128)(2,1)S(1)}, u32[]{:S(2)}, u32[]{:S(2)}) collective-permute-start(bf16[192,768]{1,0:T(8,128)(2,1)S(1)} %slice.365), channel_id=1, source_target_pairs={{0,2},{2,0},{4,6},{6,4},{8,10},{10,8},{12,14},{14,12},{16,18},{18,... | collective-permute-start | bytes 884744 | tf_op jit(solution)/shard_map/ppermute | solution.py:51
  372.8 13.9 %collective-permute-start.47 = (bf16[192,896]{1,0:T(8,128)(2,1)S(1)}, bf16[192,896]{1,0:T(8,128)(2,1)S(1)}, u32[]{:S(2)}, u32[]{:S(2)}) collective-permute-start(bf16[192,896]{1,0:T(8,128)(2,1)S(1)} %slice.345), channel_id=1, source_target_pairs={{0,2},{2,0},{4,6},{6,4},{8,10},{10,8},{12,14},{14,12},{16,18},{18,... | collective-permute-start | bytes 1032200 | tf_op jit(solution)/shard_map/ppermute | solution.py:51
  376.7 10.1 %collective-permute-start.49 = (bf16[192,1024]{1,0:T(8,128)(2,1)S(1)}, bf16[192,1024]{1,0:T(8,128)(2,1)S(1)}, u32[]{:S(2)}, u32[]{:S(2)}) collective-permute-start(bf16[192,1024]{1,0:T(8,128)(2,1)S(1)} %slice.351), channel_id=1, source_target_pairs={{0,4},{2,6},{4,0},{6,2},{8,12},{10,14},{12,8},{14,10},{16,20},{18,... | collective-permute-start | bytes 1179656 | tf_op jit(solution)/shard_map/ppermute | solution.py:51
  382.8 8.9 %collective-permute-start.58 = (bf16[48,1536]{1,0:T(8,128)(2,1)S(1)}, bf16[48,1536]{1,0:T(8,128)(2,1)S(1)}, u32[]{:S(2)}, u32[]{:S(2)}) collective-permute-start(bf16[48,1536]{1,0:T(8,128)(2,1)S(1)} %get-tuple-element.98), channel_id=1, source_target_pairs={{0,8},{2,10},{4,12},{6,14},{8,0},{10,2},{12,4},{14,6},{16,24},{18,... | collective-permute-start | bytes 442376 | tf_op jit(solution)/shard_map/ppermute | solution.py:51
  382.9 11.9 %collective-permute-start.60 = (bf16[48,1536]{1,0:T(8,128)(2,1)S(1)}, bf16[48,1536]{1,0:T(8,128)(2,1)S(1)}, u32[]{:S(2)}, u32[]{:S(2)}) collective-permute-start(bf16[48,1536]{1,0:T(8,128)(2,1)S(1)} %get-tuple-element.99), channel_id=1, source_target_pairs={{0,24},{2,26},{4,28},{6,30},{8,16},{10,18},{12,20},{14,22},{16,8},... | collective-permute-start | bytes 442376 | tf_op jit(solution)/shard_map/ppermute | solution.py:51
  386.7 19.3 %collective-permute-start.59 = (bf16[48,1536]{1,0:T(8,128)(2,1)S(1)}, bf16[48,1536]{1,0:T(8,128)(2,1)S(1)}, u32[]{:S(2)}, u32[]{:S(2)}) collective-permute-start(bf16[48,1536]{1,0:T(8,128)(2,1)S(1)} %get-tuple-element.100), channel_id=1, source_target_pairs={{0,16},{2,18},{4,20},{6,22},{8,24},{10,26},{12,28},{14,30},{16,0},... | collective-permute-start | bytes 442376 | tf_op jit(solution)/shard_map/ppermute | solution.py:51
  387.0 19.8 %collective-permute-start.50 = (bf16[48,1920]{1,0:T(8,128)(2,1)S(1)}, bf16[48,1920]{1,0:T(8,128)(2,1)S(1)}, u32[]{:S(2)}, u32[]{:S(2)}) collective-permute-start(bf16[48,1920]{1,0:T(8,128)(2,1)S(1)} %get-tuple-element.95), channel_id=1, source_target_pairs={{0,8},{2,10},{4,12},{6,14},{8,0},{10,2},{12,4},{14,6},{16,24},{18,... | collective-permute-start | bytes 552968 | tf_op jit(solution)/shard_map/ppermute | solution.py:51
  391.8 15.0 %collective-permute-start.52 = (bf16[48,1920]{1,0:T(8,128)(2,1)S(1)}, bf16[48,1920]{1,0:T(8,128)(2,1)S(1)}, u32[]{:S(2)}, u32[]{:S(2)}) collective-permute-start(bf16[48,1920]{1,0:T(8,128)(2,1)S(1)} %get-tuple-element.96), channel_id=1, source_target_pairs={{0,24},{2,26},{4,28},{6,30},{8,16},{10,18},{12,20},{14,22},{16,8},... | collective-permute-start | bytes 552968 | tf_op jit(solution)/shard_map/ppermute | solution.py:51
  394.8 17.0 %collective-permute-start.51 = (bf16[48,1920]{1,0:T(8,128)(2,1)S(1)}, bf16[48,1920]{1,0:T(8,128)(2,1)S(1)}, u32[]{:S(2)}, u32[]{:S(2)}) collective-permute-start(bf16[48,1920]{1,0:T(8,128)(2,1)S(1)} %get-tuple-element.97), channel_id=1, source_target_pairs={{0,16},{2,18},{4,20},{6,22},{8,24},{10,26},{12,28},{14,30},{16,0},... | collective-permute-start | bytes 552968 | tf_op jit(solution)/shard_map/ppermute | solution.py:51
  (35 other events, 265.6 us)
